TPU v7x, 128 devices: a whole 4x4x4 slice. The times are simulated.
128 devices in a mesh: rows: 64 (over z, x_lo, y, core), cols: 2 (over x_hi).
Axes of the slice: x: 4 (x_hi: 2, x_lo: 2; x = x_hi * 2 + x_lo), y: 4, z: 4, core: 2. Of those that a mesh axis runs over, the one named last changes fastest.
Arguments:
- blocks: bfloat16 [81920, 128, 128], P(('rows', 'cols')), may hold values from -0.1875 to 0.1875
- block_row: int32 [81920], P(('rows', 'cols')), may hold values from 0 to 159
- block_col: int32 [81920], P(('rows', 'cols')), may hold values from 0 to 1023
- right_sides: float32 [10240, 8, 128], P('rows'), as said below
- precond: float32 [2048, 128, 128], P(('cols', 'rows')), as said below
Outputs:
- solution: float32 [2048, 8, 128], P(('cols', 'rows'))
- left_vector: float32 [10240, 8, 128], P('rows')
Inputs may be any that keep to these rules, and one draw needn't show every extreme that they name: `block_row`: each stored block's row position within its row shard. `block_col`: each stored block's column position within its column shard; positions may repeat. `right_sides`: rows of each right-hand side block have positive scales that differ from block to block. `precond`: each block is upper triangular with a positive diagonal.
All inputs are finite; a program needn't handle non-finite values.
Results may differ from a plain program's by a relative error of at most 0.025.
Values may be sent and summed in bfloat16 or wider, within the bound.
No kernel may reach another device: no remote copies, remote signals or barrier semaphores. Data moves between devices by JAX's collectives and lax.ppermute only.
A program may use at most 128 MiB of HBM per device.

v0:
```python
import jax
import jax.numpy as jnp
from jax import lax
from jax.sharding import PartitionSpec as P

ITERS = 3


EPS = 1e-06


def widen(vector):
    return vector[None, :, None]


def squares(field):
    return jnp.sum(field * field, axis=(0, 2))


def shards(blocks, block_row, block_col, right_sides, precond):
    row_count = right_sides.shape[0]
    span = precond.shape[0] * lax.axis_size("rows")

    def backward(left):
        narrow = left.astype(jnp.bfloat16)
        picked = narrow[block_row]
        prod = jnp.einsum("nkc,ncb->nkb", picked, blocks, preferred_element_type=jnp.float32)
        partial_cols = jax.ops.segment_sum(prod, block_col, num_segments=span)
        return lax.psum_scatter(partial_cols, "rows", scatter_dimension=0, tiled=True)

    def apply_pre(field):
        return jnp.einsum("ckb,cbd->ckd", field, precond, precision=lax.Precision.HIGHEST)

    def apply_pre_t(field):
        return jnp.einsum("ckd,cbd->ckb", field, precond, precision=lax.Precision.HIGHEST)

    def row_norm(field):
        return jnp.sqrt(lax.psum(squares(field), "rows") + EPS)

    def column_norm(field):
        return jnp.sqrt(lax.psum(squares(field), ("rows", "cols")) + EPS)

    beta_norm = row_norm(right_sides)
    left_vector = right_sides / widen(beta_norm)
    col_term = apply_pre_t(backward(left_vector))
    phibar = beta_norm
    iterate = jnp.zeros(col_term.shape, jnp.float32)
    search = iterate
    rhobar = beta_norm
    right = iterate
    for sweep in range(ITERS + 1):
        if sweep < ITERS:
            scaled = apply_pre(col_term).astype(jnp.bfloat16)
            alpha_norm = column_norm(col_term)
            fresh = col_term / widen(alpha_norm)
            whole = lax.all_gather(scaled, "rows", axis=0, tiled=True)
            forward_picked = whole[block_col]
            forward_prod = jnp.einsum(
                "nkb,ncb->nkc", forward_picked, blocks, preferred_element_type=jnp.float32
            )
            partial_rows = jax.ops.segment_sum(forward_prod, block_row, num_segments=row_count)
            product = lax.psum(partial_rows.astype(jnp.bfloat16), "cols").astype(jnp.float32)
            row_term = product / widen(alpha_norm) - widen(alpha_norm) * left_vector
            beta_next = row_norm(row_term)
        else:
            alpha_norm = column_norm(col_term)
            fresh = col_term / widen(alpha_norm)
        if sweep == 0:
            search = fresh
            rhobar = alpha_norm
        else:
            rotation = jnp.sqrt(rhobar * rhobar + beta_norm * beta_norm)
            cosine = rhobar / rotation
            sine_part = beta_norm / rotation
            theta_term = sine_part * alpha_norm
            rhobar = -cosine * alpha_norm
            phi_term = cosine * phibar
            phibar = sine_part * phibar
            iterate = iterate + widen(phi_term / rotation) * search
            search = fresh - widen(theta_term / rotation) * search
        right = fresh
        if sweep < ITERS:
            beta_norm = beta_next
            left_vector = row_term / widen(beta_norm)
            col_term = apply_pre_t(backward(left_vector)) - widen(beta_norm) * right
    return (apply_pre(iterate), left_vector)


def solution(mesh):
    return jax.shard_map(
        shards,
        mesh=mesh,
        in_specs=(
            P(("rows", "cols"), None, None),
            P(("rows", "cols")),
            P(("rows", "cols")),
            P("rows", None, None),
            P(("cols", "rows"), None, None),
        ),
        out_specs=(P(("cols", "rows"), None, None), P("rows", None, None)),
        check_vma=False,
    )
```

profile of v0, /device:TPU:1, one launch (start us, length us, event | category | flops | bytes accessed | tf_op | source)
XLA Modules:
  0.0 2404.6 jit_solution(826319010976677686)
XLA Ops:
  8.7 140.9 %psum.70 = f32[8]{0:T(128)S(1)} all-reduce(f32[8]{0:T(128)S(1)} %multiply_reduce_fusion.3), channel_id=1, replica_groups=mesh['rows'=64,'cols'=2] {'rows'}, use_global_device_ids=true, to_apply=%region_1.0 | all-reduce | flops 8 | bytes 64 | tf_op jit(solution)/shard_map/psum | solution.py:38
  153.8 10.9 fusion.28
  166.9 69.1 %scatter_fusion = f32[1024,8,128]{2,1,0:T(8,128)} fusion(f32[1024,8,128]{2,1,0:T(8,128)} %broadcast.30.clone, s32[640]{0:T(1024)S(1)} %copy-done.4, f32[640,8,128]{2,1,0:T(8,128)} %fusion.28), kind=kCustom, calls=%fused_computation.6 | custom fusion | flops 655360 | bytes 7866880 | tf_op jit(solution)/shard_map/scatter-add | solution.py:28
  236.1 285.2 %reduce-scatter.4.cloned.1.call-done = f32[16,8,128]{2,1,0:T(8,128)} async-done(((f32[1024,8,128]{2,1,0:T(8,128)}), f32[16,8,128]{2,1,0:T(8,128)}) %reduce-scatter.4.cloned.1.call-update) | async-done | bytes 65552 | tf_op jit(solution)/shard_map/reduce_scatter | solution.py:29
  525.7 106.5 %all-gather.4.cloned.1.call-done = bf16[1024,8,128]{2,1,0:T(8,128)(2,1)} async-done(((bf16[16,8,128]{2,1,0:T(8,128)(2,1)}), bf16[1024,8,128]{2,1,0:T(8,128)(2,1)}) %all-gather.4.cloned.1.call-update) | async-done | bytes 2097168 | tf_op jit(solution)/shard_map/all_gather | solution.py:56
  635.1 16.1 fusion.29
  651.3 45.5 %scatter_fusion.1 = f32[160,8,128]{2,1,0:T(8,128)S(1)} fusion(f32[160,8,128]{2,1,0:T(8,128)S(1)} %broadcast.34.clone, s32[640]{0:T(1024)S(1)} %copy-done.5, f32[640,8,128]{2,1,0:T(8,128)} %fusion.29), kind=kCustom, calls=%fused_computation.7 | custom fusion | flops 655360 | bytes 7866880 | tf_op jit(solution)/shard_map/scatter-add | solution.py:61
  697.6 64.1 %psum.71 = f32[8]{0:T(128)S(1)} all-reduce(f32[8]{0:T(128)S(1)} %get-tuple-element.21), channel_id=1, replica_groups=mesh['rows'=64,'cols'=2] {'rows','cols'}, use_global_device_ids=true, to_apply=%region_5.0 | all-reduce | flops 8 | bytes 64 | tf_op jit(solution)/shard_map/psum | solution.py:41
  763.1 138.6 %psum.73 = f32[8]{0:T(128)S(1)} all-reduce(f32[8]{0:T(128)S(1)} %get-tuple-element.15), channel_id=1, replica_groups=mesh['rows'=64,'cols'=2] {'rows'}, use_global_device_ids=true, to_apply=%region_9.0 | all-reduce | flops 8 | bytes 64 | tf_op jit(solution)/shard_map/psum | solution.py:38
  904.3 10.9 fusion.30
  917.4 69.1 %scatter_fusion.2 = f32[1024,8,128]{2,1,0:T(8,128)} fusion(f32[1024,8,128]{2,1,0:T(8,128)} %broadcast.30.clone.1, s32[640]{0:T(1024)S(1)} %copy-done.4, f32[640,8,128]{2,1,0:T(8,128)} %fusion.30), kind=kCustom, calls=%fused_computation.8 | custom fusion | flops 655360 | bytes 7866880 | tf_op jit(solution)/shard_map/scatter-add | solution.py:28
  986.6 281.7 %reduce-scatter.6.cloned.1.call-done = f32[16,8,128]{2,1,0:T(8,128)} async-done(((f32[1024,8,128]{2,1,0:T(8,128)}), f32[16,8,128]{2,1,0:T(8,128)}) %reduce-scatter.6.cloned.1.call-update) | async-done | bytes 65552 | tf_op jit(solution)/shard_map/reduce_scatter | solution.py:29
  1272.7 106.5 %all-gather.6.cloned.1.call-done = bf16[1024,8,128]{2,1,0:T(8,128)(2,1)} async-done(((bf16[16,8,128]{2,1,0:T(8,128)(2,1)}), bf16[1024,8,128]{2,1,0:T(8,128)(2,1)}) %all-gather.6.cloned.1.call-update) | async-done | bytes 2097168 | tf_op jit(solution)/shard_map/all_gather | solution.py:56
  1382.1 16.1 fusion.31
  1398.3 45.5 %scatter_fusion.3 = f32[160,8,128]{2,1,0:T(8,128)S(1)} fusion(f32[160,8,128]{2,1,0:T(8,128)S(1)} %broadcast.34.clone.1, s32[640]{0:T(1024)S(1)} %copy-done.5, f32[640,8,128]{2,1,0:T(8,128)} %fusion.31), kind=kCustom, calls=%fused_computation.9 | custom fusion | flops 655360 | bytes 7866880 | tf_op jit(solution)/shard_map/scatter-add | solution.py:61
  1444.6 64.1 %psum.74 = f32[8]{0:T(128)S(1)} all-reduce(f32[8]{0:T(128)S(1)} %get-tuple-element.23), channel_id=1, replica_groups=mesh['rows'=64,'cols'=2] {'rows','cols'}, use_global_device_ids=true, to_apply=%region_13.0 | all-reduce | flops 8 | bytes 64 | tf_op jit(solution)/shard_map/psum | solution.py:41
  1510.1 138.7 %psum.76 = f32[8]{0:T(128)S(1)} all-reduce(f32[8]{0:T(128)S(1)} %get-tuple-element.13), channel_id=1, replica_groups=mesh['rows'=64,'cols'=2] {'rows'}, use_global_device_ids=true, to_apply=%region_17.0 | all-reduce | flops 8 | bytes 64 | tf_op jit(solution)/shard_map/psum | solution.py:38
  1664.3 69.1 %scatter_fusion.4 = f32[1024,8,128]{2,1,0:T(8,128)} fusion(f32[1024,8,128]{2,1,0:T(8,128)} %broadcast.30, s32[640]{0:T(1024)S(1)} %copy-done.4, f32[640,8,128]{2,1,0:T(8,128)} %fusion.32), kind=kCustom, calls=%fused_computation.10 | custom fusion | flops 655360 | bytes 7866880 | tf_op jit(solution)/shard_map/scatter-add | solution.py:28
  1733.6 281.7 %reduce-scatter.8.cloned.1.call-done = f32[16,8,128]{2,1,0:T(8,128)} async-done(((f32[1024,8,128]{2,1,0:T(8,128)}), f32[16,8,128]{2,1,0:T(8,128)}) %reduce-scatter.8.cloned.1.call-update) | async-done | bytes 65552 | tf_op jit(solution)/shard_map/reduce_scatter | solution.py:29
  2019.6 106.5 %all-gather.8.cloned.1.call-done = bf16[1024,8,128]{2,1,0:T(8,128)(2,1)} async-done(((bf16[16,8,128]{2,1,0:T(8,128)(2,1)}), bf16[1024,8,128]{2,1,0:T(8,128)(2,1)}) %all-gather.8.cloned.1.call-update) | async-done | bytes 2097168 | tf_op jit(solution)/shard_map/all_gather | solution.py:56
  2129.1 16.1 fusion.33
  2145.2 45.5 %scatter_fusion.5 = f32[160,8,128]{2,1,0:T(8,128)S(1)} fusion(f32[160,8,128]{2,1,0:T(8,128)S(1)} %broadcast.34, s32[640]{0:T(1024)S(1)} %copy-done.5, f32[640,8,128]{2,1,0:T(8,128)} %fusion.33), kind=kCustom, calls=%fused_computation.11 | custom fusion | flops 655360 | bytes 7866880 | tf_op jit(solution)/shard_map/scatter-add | solution.py:61
  2191.5 64.1 %psum.77 = f32[8]{0:T(128)S(1)} all-reduce(f32[8]{0:T(128)S(1)} %get-tuple-element.25), channel_id=1, replica_groups=mesh['rows'=64,'cols'=2] {'rows','cols'}, use_global_device_ids=true, to_apply=%region_21.0 | all-reduce | flops 8 | bytes 64 | tf_op jit(solution)/shard_map/psum | solution.py:41
  2256.9 138.4 %psum.79 = f32[8]{0:T(128)S(1)} all-reduce(f32[8]{0:T(128)S(1)} %get-tuple-element.11), channel_id=1, replica_groups=mesh['rows'=64,'cols'=2] {'rows'}, use_global_device_ids=true, to_apply=%region_25.0 | all-reduce | flops 8 | bytes 64 | tf_op jit(solution)/shard_map/psum | solution.py:38
  (76 shorter events, 59.5 us)
Async XLA Ops:
  7.2 514.1 %copy-start = (f32[16,128,128]{2,1,0:T(8,128)S(1)}, f32[16,128,128]{2,1,0:T(8,128)}, u32[]{:S(2)}) copy-start(f32[16,128,128]{2,1,0:T(8,128)} %param.9) | copy-start | bytes 3145732
  7.2 514.1 %reduce-scatter.4.cloned.1.call-start = ((), (), s32[]{:S(2)}) async-start(), calls=%async_computation.3 | async-start | bytes 4259840 | tf_op jit(solution)/shard_map/reduce_scatter | solution.py:29
  164.7 2.2 copy-start.4
  236.1 396.1 %all-gather.4.cloned.1.call-start = ((), (), s32[]{:S(2)}) async-start(), calls=%async_computation.4 | async-start | bytes 2129920 | tf_op jit(solution)/shard_map/all_gather | solution.py:56
  525.6 236.1 %all-reduce.4.cloned.1.call-start = ((), (), s32[]{:S(2)}) async-start(), calls=%async_computation.5 | async-start | bytes 655360 | tf_op jit(solution)/shard_map/psum | solution.py:62
  635.1 16.2 copy-start.5
  651.3 110.5 %copy-start.1 = (f32[160,8,128]{2,1,0:T(8,128)S(1)}, f32[160,8,128]{2,1,0:T(8,128)}, u32[]{:S(2)}) copy-start(f32[160,8,128]{2,1,0:T(8,128)} %param.8) | copy-start | bytes 1966084
  697.6 570.7 %reduce-scatter.6.cloned.1.call-start = ((), (), s32[]{:S(2)}) async-start(), calls=%async_computation.6 | async-start | bytes 4259840 | tf_op jit(solution)/shard_map/reduce_scatter | solution.py:29
  763.1 138.7 %copy-start.2 = (f32[160,8,128]{2,1,0:T(8,128)}, f32[160,8,128]{2,1,0:T(8,128)S(1)}, u32[]{:S(2)}) copy-start(f32[160,8,128]{2,1,0:T(8,128)S(1)} %get-tuple-element.16) | copy-start | bytes 1966084
  986.5 392.7 %all-gather.6.cloned.1.call-start = ((), (), s32[]{:S(2)}) async-start(), calls=%async_computation.7 | async-start | bytes 2129920 | tf_op jit(solution)/shard_map/all_gather | solution.py:56
  1272.6 236.1 %all-reduce.6.cloned.1.call-start = ((), (), s32[]{:S(2)}) async-start(), calls=%async_computation.8 | async-start | bytes 655360 | tf_op jit(solution)/shard_map/psum | solution.py:62
  1398.2 110.5 %copy-start.3 = (f32[160,8,128]{2,1,0:T(8,128)S(1)}, f32[160,8,128]{2,1,0:T(8,128)}, u32[]{:S(2)}) copy-start(f32[160,8,128]{2,1,0:T(8,128)} %copy-done.2) | copy-start | bytes 1966084
  1444.5 570.8 %reduce-scatter.8.cloned.1.call-start = ((), (), s32[]{:S(2)}) async-start(), calls=%async_computation.9 | async-start | bytes 4259840 | tf_op jit(solution)/shard_map/reduce_scatter | solution.py:29
  1733.5 392.7 %all-gather.8.cloned.1.call-start = ((), (), s32[]{:S(2)}) async-start(), calls=%async_computation.10 | async-start | bytes 2129920 | tf_op jit(solution)/shard_map/all_gather | solution.py:56
  2019.6 236.0 %all-reduce.8.cloned.1.call-start = ((), (), s32[]{:S(2)}) async-start(), calls=%async_computation.11 | async-start | bytes 655360 | tf_op jit(solution)/shard_map/psum | solution.py:62
Sparse Core Ops, SparseCore 0:
  236.2 285.0 reduce-scatter.3
  525.8 106.4 all-gather.3
  697.7 31.1 all-reduce.3
  986.6 281.6 reduce-scatter.5
  1272.7 106.4 all-gather.5
  1444.6 31.1 all-reduce.5
  1733.6 281.6 reduce-scatter.7
  2019.7 106.4 all-gather.7
  2191.6 31.1 all-reduce.7
where the time goes:
time: 2420 us; the launch traced here: 2400 us
  waiting for transfers between devices  1170 us (48%)
  blocking collectives  749 us (31%)
  other arithmetic  355 us (15%)
  matrix products  95.5 us (4%)
    reduce_scatter x3, waiting for transfers between devices, backward(): lax.psum_scatter(partial_cols, 'rows', scatter_dimension=0, tiled=True)  849 us
    psum x4, blocking collectives, row_norm(): return jnp.sqrt(lax.psum(squares(field), 'rows') + EPS)  557 us
    all_gather x3, waiting for transfers between devices, shards(): whole = lax.all_gather(scaled, 'rows', axis=0, tiled=True)  320 us
    scatter-add x3, other arithmetic, backward(): partial_cols = jax.ops.segment_sum(prod, block_col, num_segments=span)  207 us
    psum x3, blocking collectives, column_norm(): return jnp.sqrt(lax.psum(squares(field), ('rows', 'cols')) + EPS)  192 us
    scatter-add x3, other arithmetic, shards(): jax.ops.segment_sum(forward_prod, block_row, num_segments=row_count)  136 us
  transfers between devices with their start and end apart: 9, of which 6 were waited for; matrix products, arithmetic and copies ran while one was open for 0% of the time, Pallas kernels for 0%

commit v1 on v0

v1 whole, which is shorter than its diff:
```python
import functools

import jax
import jax.numpy as jnp
from jax import lax
from jax.experimental import pallas as pl
from jax.experimental.pallas import tpu as pltpu
from jax.sharding import PartitionSpec as P

ITERS = 3


EPS = 1e-06
HIGHEST = lax.Precision.HIGHEST
F32 = jnp.float32
BF16 = jnp.bfloat16
VM = pl.BlockSpec(memory_space=pltpu.VMEM)
SM = pl.BlockSpec(memory_space=pltpu.SMEM)
LATE = 16


def params():
    return pltpu.CompilerParams(vmem_limit_bytes=32 << 20)


def like(shape, dtype=F32):
    return jax.ShapeDtypeStruct(shape, dtype)


def pack(total, first):
    half = total * 0.5
    top = half.astype(BF16).astype(F32)
    middle = (half - top).astype(BF16).astype(F32)
    low = half - top - middle
    lane = lax.broadcasted_iota(jnp.int32, (total.shape[0], 128), 1) - first
    terms = jnp.where(lane == 0, top, jnp.where(lane == 1, middle, jnp.where(lane == 2, low, 0.0)))
    return terms.astype(BF16)


def unpack(block):
    return jnp.sum(block, axis=-1, keepdims=True) * 2.0


def squares(field):
    return jnp.sum(jnp.sum(field * field, axis=0), axis=-1, keepdims=True)


def accumulate(products, source, target, table, blocks, total):
    count = blocks.shape[0]
    unroll = next(u for u in (128, 64, 32, 16, 8, 4, 2) if count % u == 0)

    def add(base, pending):
        at, term = pending
        spot = target[base + at]
        total[spot] = total[spot] + term

    def step(i, carry):
        base = i * unroll
        pending = []
        for u in range(0, unroll, 2):
            pair = jnp.concatenate([table[source[base + u]], table[source[base + u + 1]]], axis=0)
            pending += list(zip((u, u + 1), products(pair, blocks[pl.ds(base + u, 2)])))
            while len(pending) > LATE:
                add(base, pending.pop(0))
        for item in pending:
            add(base, item)
        return carry

    lax.fori_loop(0, count // unroll, step, 0)


def forward_pair(pair, blocks):
    both = lax.dot_general(
        pair.astype(BF16),
        blocks.reshape(-1, blocks.shape[2]),
        (((1,), (1,)), ((), ())),
        preferred_element_type=F32,
    )
    size = blocks.shape[1]
    half = pair.shape[0] // 2
    return both[:half, :size], both[half:, size:]


def backward_pair(pair, blocks):
    half = pair.shape[0] // 2
    none = jnp.zeros((half, pair.shape[1]), F32)
    spread = jnp.concatenate(
        [jnp.concatenate([pair[:half], none], axis=1), jnp.concatenate([none, pair[half:]], axis=1)], axis=0
    )
    both = jnp.dot(spread.astype(BF16), blocks.reshape(-1, blocks.shape[2]), preferred_element_type=F32)
    return both[:half], both[half:]


def send_sums(here, row_term, row, spot, blocks, kept, sent, total):
    total[...] = jnp.zeros_like(total)
    accumulate(backward_pair, row, spot, row_term, blocks, total)
    half = kept.shape[0] * kept.shape[1]
    kept[...] = total[:half].astype(BF16).reshape(kept.shape)
    sent[...] = total[half:].astype(BF16).reshape(sent.shape)
    norm = pack(squares(row_term[...]), 3 * here[0])
    last = kept.shape[1] - 1
    for chip in range(kept.shape[0]):
        kept[chip, last] = norm
        sent[chip, last] = norm


def first_kernel(here, row, spot, right_sides, blocks, kept, sent, total):
    send_sums(here, right_sides, row, spot, blocks, kept, sent, total)


def new_row_term(mine, other, before, beta, row_term, alpha):
    count = before.shape[0]
    norm = jnp.sqrt(unpack(mine[count].astype(F32)) + unpack(other[count].astype(F32)) + EPS)
    alpha[...] = jnp.broadcast_to(norm, alpha.shape)
    product = mine[:count].astype(F32) + other[:count].astype(F32)
    row_term[...] = product * (1.0 / alpha[...])[None] - before[...] * (alpha[...] / beta[...])[None]


def back_kernel(here, row, spot, mine, other, before, beta, blocks, row_term, alpha, kept, sent, total):
    new_row_term(mine, other, before, beta, row_term, alpha)
    send_sums(here, row_term, row, spot, blocks, kept, sent, total)


def finish_kernel(mine, other, before, beta, row_term, alpha, norms):
    new_row_term(mine, other, before, beta, row_term, alpha)
    norms[...] = jnp.broadcast_to(squares(row_term[...])[None], norms.shape)


def forward_kernel(step, row, spot, mine, other, blocks, product, table, total):
    half = mine.shape[0]
    table[:half] = mine[...].astype(F32)
    table[half:] = other[...].astype(F32)
    total[...] = jnp.zeros_like(total)
    accumulate(forward_pair, spot, row, table, blocks, total)
    count = total.shape[0]
    product[:count] = total[...].astype(BF16)
    norm = jnp.zeros(total.shape[1:], F32)
    for last in range(step - 1, half, step):
        norm = norm + table[last] + table[half + last]
    product[count] = pack(unpack(norm), 0)


def advance(state, alpha, beta):
    col_term, search, iterate, rhobar, phibar = state
    fresh = col_term / alpha
    rotation = jnp.sqrt(rhobar * rhobar + beta * beta)
    cosine = rhobar / rotation
    sine = beta / rotation
    theta = sine * alpha
    phi = cosine * phibar
    iterate = iterate + (phi / rotation) * search
    search = fresh - (theta / rotation) * search
    return fresh, search, iterate, -cosine * alpha, sine * phibar


def column_kernel(sweep, chunks, precond, *refs):
    if sweep == 0:
        col_term, beta, scaled = refs
    elif sweep == 1:
        before, alpha, beta_before, col_term, beta, scaled, search, iterate, rhobar, phibar = refs
        fresh = before[...] / alpha[...][None]
        search[...] = fresh
        iterate[...] = jnp.zeros_like(iterate)
        rhobar[...] = alpha[...]
        phibar[...] = beta_before[...]
    else:
        (before, alpha, beta_before, search_in, iterate_in, rhobar_in, phibar_in) = refs[:7]
        col_term, beta, scaled, search, iterate, rhobar, phibar = refs[7:]
        state = (before[...], search_in[...], iterate_in[...], rhobar_in[...], phibar_in[...])
        fresh, search[...], iterate[...], rhobar[...], phibar[...] = advance(state, alpha[...], beta_before[...])
    own = col_term.shape[0]
    gathered = jnp.sum(chunks[...].astype(F32), axis=0)
    beta[...] = jnp.broadcast_to(jnp.sqrt(unpack(gathered[own]) + EPS), beta.shape)
    gathered = gathered * (1.0 / beta[...])[None]
    norm = jnp.zeros(beta.shape, F32)
    for c in range(own):
        term = lax.dot_general(
            gathered[c], precond[c], (((1,), (1,)), ((), ())), precision=HIGHEST, preferred_element_type=F32
        )
        if sweep > 0:
            term = term - beta[...] * fresh[c]
        col_term[c] = term
        norm = norm + term * term
        whole = jnp.dot(term, precond[c], precision=HIGHEST, preferred_element_type=F32).astype(BF16)
        scaled[:, c] = jnp.broadcast_to(whole[None], (scaled.shape[0],) + whole.shape)
    packed = pack(jnp.sum(norm, axis=-1, keepdims=True), 0)
    scaled[:, own] = jnp.broadcast_to(packed[None], (scaled.shape[0],) + packed.shape)


def last_kernel(norms, row_term, before, alpha, beta_before, search, iterate, rhobar, phibar, precond, out, left):
    beta = jnp.sqrt(jnp.sum(norms[...], axis=0) + EPS)
    left[...] = row_term[...] * (1.0 / beta)[None]
    state = (before[...], search[...], iterate[...], rhobar[...], phibar[...])
    _, direction, solved, rho, phi = advance(state, alpha[...], beta_before[...])
    rotation = jnp.sqrt(rho * rho + beta * beta)
    solved = solved + ((rho / rotation) * phi / rotation) * direction
    for c in range(out.shape[0]):
        out[c] = jnp.dot(solved[c], precond[c], precision=HIGHEST, preferred_element_type=F32)


def call(kernel, out_shape, operands, scalars=0, scratch=(), name=None):
    return pl.pallas_call(
        kernel,
        out_shape=out_shape,
        in_specs=[SM] * scalars + [VM] * (len(operands) - scalars),
        out_specs=jax.tree.map(lambda _: VM, out_shape),
        scratch_shapes=list(scratch),
        compiler_params=params(),
        name=name,
    )(*operands)


def shards(blocks, block_row, block_col, right_sides, precond):
    rows, rhs, size = right_sides.shape
    own = precond.shape[0]
    devices = lax.axis_size("rows")
    chips = devices // 2
    half = chips * (own + 1)
    core = lax.rem(lax.axis_index("rows"), 2)
    here = core[None].astype(jnp.int32)
    owner = block_col // own
    spot = ((owner & 1) ^ core) * half + (owner >> 1) * (own + 1) + block_col % own
    same_core = [[2 * chip + c for chip in range(chips)] for c in range(2)]
    swap = [(d, d ^ 1) for d in range(devices)]

    def exchange(parts):
        return lax.all_to_all(parts, "rows", 0, 0, axis_index_groups=same_core, tiled=True)

    def core_swap(array):
        return lax.ppermute(array, "rows", swap)

    part = like((chips, own + 1, rhs, size), BF16)
    norm = like((rhs, size))
    field = like((own, rhs, size))
    row_field = like((rows, rhs, size))
    total = pltpu.VMEM((2 * half, rhs, size), F32)

    def scatter(kept, sent):
        arrived = core_swap(sent)
        return exchange((kept.astype(F32) + arrived.astype(F32)).astype(BF16))

    kept, sent = call(
        first_kernel, [part, part], (here, block_row, spot, right_sides, blocks), 3, [total], "first_backward"
    )
    row_term = right_sides
    col_term = alpha = beta = None
    state = []
    for sweep in range(ITERS + 1):
        chunks = scatter(kept, sent)
        carried = [] if sweep == 0 else [col_term, alpha, beta] + state
        if sweep == ITERS:
            finished = carried
        new = call(
            functools.partial(column_kernel, sweep),
            [field, norm, part] + ([] if sweep == 0 else [field, field, norm, norm]),
            (chunks, precond, *carried),
            name=f"columns_{sweep}",
        )
        col_term, beta, scaled = new[:3]
        state = list(new[3:])
        if sweep == ITERS:
            break
        mine = exchange(scaled)
        other = core_swap(mine)
        flat = (half, rhs, size)
        product = call(
            functools.partial(forward_kernel, own + 1),
            like((rows + 1, rhs, size), BF16),
            (block_row, spot, mine.reshape(flat), other.reshape(flat), blocks),
            2,
            [pltpu.VMEM((2 * half, rhs, size), F32), pltpu.VMEM((rows, rhs, size), F32)],
            f"forward_{sweep}",
        )
        crossed = lax.ppermute(product, "cols", [(0, 1), (1, 0)])
        if sweep < ITERS - 1:
            row_term, alpha, kept, sent = call(
                back_kernel,
                [row_field, norm, part, part],
                (here, block_row, spot, product, crossed, row_term, beta, blocks),
                3,
                [total],
                f"backward_{sweep}",
            )
        else:
            row_term, alpha, norms = call(
                finish_kernel,
                [row_field, norm, like((devices, rhs, size))],
                (product, crossed, row_term, beta),
                name="finish_rows",
            )
            kept, sent = call(
                first_kernel, [part, part], (here, block_row, spot, row_term, blocks), 3, [total], "last_backward"
            )
    norms = lax.all_to_all(norms, "rows", 0, 0, tiled=True)
    return call(last_kernel, [field, row_field], (norms, row_term, *finished, precond), name="last")


def solution(mesh):
    return jax.shard_map(
        shards,
        mesh=mesh,
        in_specs=(
            P(("rows", "cols"), None, None),
            P(("rows", "cols")),
            P(("rows", "cols")),
            P("rows", None, None),
            P(("cols", "rows"), None, None),
        ),
        out_specs=(P(("cols", "rows"), None, None), P("rows", None, None)),
        check_vma=False,
    )
```

time: 2420 us -> 309 us (0.13)
  waiting for transfers between devices: 1170 us -> 38.4 us
  blocking collectives: 749 us -> 148 us
  other arithmetic: 355 us -> 1.58 us
  Pallas kernels: 0 us -> 98.9 us
  matrix products: 95.5 us -> 0 us
    reduce_scatter x3 -> x0, waiting for transfers between devices: 849 us -> none  [backward(): lax.psum_scatter(partial_cols, 'rows', scatter_dimension=0, tiled=True)]
    psum x7 -> x0, blocking collectives: 749 us -> none  [the longest x4 557 us: row_norm(): return jnp.sqrt(lax.psum(squares(field), 'rows') + EPS)]
    scatter-add x6 -> x0, other arithmetic: 344 us -> none  [the longest x3 207 us: backward(): partial_cols = jax.ops.segment_sum(prod, block_col, num_segments=span)]
    all_gather x3 -> x0, waiting for transfers between devices: 320 us -> none  [shards(): whole = lax.all_gather(scaled, 'rows', axis=0, tiled=True)]
    all_to_all x0 -> x7, blocking collectives: none -> 148 us  [the longest x6 133 us: exchange(): lax.all_to_all(parts, 'rows', 0, 0, axis_index_groups=same_core, tiled=True)]
    pallas_call x0 -> x11, Pallas kernels: none -> 98.9 us  [call(): pl.pallas_call(kernel, out_shape=out_shape, in_specs=[SM] * scalars + [VM...]
    dot_general x13 -> x0, matrix products: 95.5 us -> none  [the longest x3 48.3 us: shards(): jnp.einsum('nkb,ncb->nkc', forward_picked, blocks, preferred_element_type...]
    ppermute x0 -> x9, waiting for transfers between devices: none -> 38.4 us  [the longest x3 24.1 us: shards(): crossed = lax.ppermute(product, 'cols', [(0, 1), (1, 0)])]
  transfers between devices with their start and end apart: 9 -> 9, of which waited for: 6 -> 9; matrix products, arithmetic and copies ran while one was open for 0% -> 0% of each run, Pallas kernels for 0% -> 0%
where the time goes in v1:
time: 309 us; the launch traced here: 308 us
  blocking collectives  148 us (48%)
  Pallas kernels  98.9 us (32%)
  waiting for transfers between devices  38.4 us (12%)
  starting transfers between devices  19 us (6%)
    all_to_all x6, blocking collectives, exchange(): lax.all_to_all(parts, 'rows', 0, 0, axis_index_groups=same_core, tiled=True)  133 us
    pallas_call x11, Pallas kernels, call(): pl.pallas_call(kernel, out_shape=out_shape, in_specs=[SM] * scalars + [VM...  98.9 us
    ppermute x3, waiting for transfers between devices, shards(): crossed = lax.ppermute(product, 'cols', [(0, 1), (1, 0)])  24.1 us
    all_to_all x1, blocking collectives, shards(): norms = lax.all_to_all(norms, 'rows', 0, 0, tiled=True)  14.9 us
    ppermute x6, waiting for transfers between devices, core_swap(): return lax.ppermute(array, 'rows', swap)  14.3 us
    ppermute x6, starting transfers between devices, core_swap(): return lax.ppermute(array, 'rows', swap)  11.6 us
    ppermute x3, starting transfers between devices, shards(): crossed = lax.ppermute(product, 'cols', [(0, 1), (1, 0)])  7.47 us
  transfers between devices with their start and end apart: 9, of which 9 were waited for; matrix products, arithmetic and copies ran while one was open for 0% of the time, Pallas kernels for 0%

profile of v1, /device:TPU:1, one launch (start us, length us, event | category | flops | bytes accessed | tf_op | source)
XLA Modules:
  0.0 308.4 jit_solution(5554370680096429885)
XLA Ops:
  3.1 11.6 %first_backward.1 = (bf16[32,17,8,128]{3,2,1,0:T(8,128)(2,1)S(1)}, bf16[32,17,8,128]{3,2,1,0:T(8,128)(2,1)S(1)}) custom-call(s32[1]{0:T(128)} %bitcast.here, s32[640]{0:T(1024)S(1)} %copy-done.3, s32[640]{0:T(1024)S(1)} %fusion.spot, f32[160,8,128]{2,1,0:T(8,128)S(1)} %copy-done.1, bf16[640,128,128]{2,1,0:T(8,128)(2,1)} %blocks.11), custom_call_target="tpu_custom_call" | custom-call | tf_op jit(solution)/shard_map/first_backward/pallas_call | solution.py:202
  18.9 26.7 %all_to_all.36.chunks = bf16[32,17,8,128]{3,2,1,0:T(8,128)(2,1)S(1)} all-to-all(bf16[32,17,8,128]{3,2,1,0:T(8,128)(2,1)S(1)} %add_convert_fusion.2), channel_id=1, replica_groups={{0,4,8,12,16,20,24,28,32,36,40,44,48,52,56,60,64,68,72,76,80,84,88,92,9..., dimensions={0} | all-to-all | bytes 2228224 | tf_op jit(solution)/shard_map/all_to_all | solution.py:227
  45.6 6.7 %columns_0.1 = (f32[16,8,128]{2,1,0:T(8,128)S(1)}, f32[8,128]{1,0:T(8,128)S(1)}, bf16[32,17,8,128]{3,2,1,0:T(8,128)(2,1)S(1)}) custom-call(bf16[32,17,8,128]{3,2,1,0:T(8,128)(2,1)S(1)} %all_to_all.36.chunks, f32[16,128,128]{2,1,0:T(8,128)S(1)} %copy-done), custom_call_target="tpu_custom_call" | custom-call | tf_op jit(solution)/shard_map/columns_0/pallas_call | solution.py:202
  52.3 21.5 %all_to_all.37 = bf16[32,17,8,128]{3,2,1,0:T(8,128)(2,1)S(1)} all-to-all(bf16[32,17,8,128]{3,2,1,0:T(8,128)(2,1)S(1)} %get-tuple-element.34), channel_id=1, replica_groups={{0,4,8,12,16,20,24,28,32,36,40,44,48,52,56,60,64,68,72,76,80,84,88,92,9..., dimensions={0} | all-to-all | bytes 2228224 | tf_op jit(solution)/shard_map/all_to_all | solution.py:227
  73.8 2.5 collective-permute-start.1
  78.7 13.7 %forward_0.1.mine = bf16[161,8,128]{2,1,0:T(8,128)(2,1)S(1)} custom-call(s32[640]{0:T(1024)S(1)} %copy-done.4, s32[640]{0:T(1024)S(1)} %fusion.spot, bf16[544,8,128]{2,1,0:T(8,128)(2,1)S(1)} %bitcast.8, bf16[544,8,128]{2,1,0:T(8,128)(2,1)S(1)} %bitcast.11, bf16[640,128,128]{2,1,0:T(8,128)(2,1)} %blocks.11), custom_call_target="tpu_custom_call" | custom-call | tf_op jit(solution)/shard_map/forward_0/pallas_call | solution.py:202
  92.3 2.5 collective-permute-start.2
  94.8 8.0 %collective-permute-done.2.other = bf16[161,8,128]{2,1,0:T(8,128)(2,1)S(1)} collective-permute-done((bf16[161,8,128]{2,1,0:T(8,128)(2,1)S(1)}, bf16[161,8,128]{2,1,0:T(8,128)(2,1)S(1)}, u32[]{:S(2)}, u32[]{:S(2)}) %collective-permute-start.2) | collective-permute-done | bytes 329760 | tf_op jit(solution)/shard_map/ppermute | solution.py:274
  102.9 11.9 %backward_0.1 = (f32[160,8,128]{2,1,0:T(8,128)S(1)}, f32[8,128]{1,0:T(8,128)S(1)}, bf16[32,17,8,128]{3,2,1,0:T(8,128)(2,1)S(1)}, bf16[32,17,8,128]{3,2,1,0:T(8,128)(2,1)S(1)}) custom-call(s32[1]{0:T(128)} %bitcast.here, s32[640]{0:T(1024)S(1)} %copy-done.4, s32[640]{0:T(1024)S(1)} %fusion.spot, bf16[161,8,128]{2,1,0:T(8,128)(2,1)S(1)} %forward_0.1.mine, ...), custom_call_target="tpu_custom_call" | custom-call | tf_op jit(solution)/shard_map/backward_0/pallas_call | solution.py:202
  118.7 21.1 %all_to_all.38.chunks = bf16[32,17,8,128]{3,2,1,0:T(8,128)(2,1)S(1)} all-to-all(bf16[32,17,8,128]{3,2,1,0:T(8,128)(2,1)S(1)} %add_convert_fusion.1), channel_id=1, replica_groups={{0,4,8,12,16,20,24,28,32,36,40,44,48,52,56,60,64,68,72,76,80,84,88,92,9..., dimensions={0} | all-to-all | bytes 2228224 | tf_op jit(solution)/shard_map/all_to_all | solution.py:227
  139.8 6.8 %columns_1.1 = (f32[16,8,128]{2,1,0:T(8,128)S(1)}, f32[8,128]{1,0:T(8,128)S(1)}, bf16[32,17,8,128]{3,2,1,0:T(8,128)(2,1)S(1)}, f32[16,8,128]{2,1,0:T(8,128)S(1)}...) custom-call(bf16[32,17,8,128]{3,2,1,0:T(8,128)(2,1)S(1)} %all_to_all.38.chunks, ...), custom_call_target="tpu_custom_call" | custom-call | tf_op jit(solution)/shard_map/columns_1/pallas_call | solution.py:202
  146.6 21.5 %all_to_all.39 = bf16[32,17,8,128]{3,2,1,0:T(8,128)(2,1)S(1)} all-to-all(bf16[32,17,8,128]{3,2,1,0:T(8,128)(2,1)S(1)} %get-tuple-element.40), channel_id=1, replica_groups={{0,4,8,12,16,20,24,28,32,36,40,44,48,52,56,60,64,68,72,76,80,84,88,92,9..., dimensions={0} | all-to-all | bytes 2228224 | tf_op jit(solution)/shard_map/all_to_all | solution.py:227
  168.0 2.5 collective-permute-start.4
  172.9 13.6 %forward_1.1.mine = bf16[161,8,128]{2,1,0:T(8,128)(2,1)S(1)} custom-call(s32[640]{0:T(1024)S(1)} %copy-done.4, s32[640]{0:T(1024)S(1)} %fusion.spot, bf16[544,8,128]{2,1,0:T(8,128)(2,1)S(1)} %bitcast.9, bf16[544,8,128]{2,1,0:T(8,128)(2,1)S(1)} %bitcast.12, bf16[640,128,128]{2,1,0:T(8,128)(2,1)} %blocks.11), custom_call_target="tpu_custom_call" | custom-call | tf_op jit(solution)/shard_map/forward_1/pallas_call | solution.py:202
  186.5 2.5 collective-permute-start.5
  189.0 8.0 %collective-permute-done.5.other = bf16[161,8,128]{2,1,0:T(8,128)(2,1)S(1)} collective-permute-done((bf16[161,8,128]{2,1,0:T(8,128)(2,1)S(1)}, bf16[161,8,128]{2,1,0:T(8,128)(2,1)S(1)}, u32[]{:S(2)}, u32[]{:S(2)}) %collective-permute-start.5) | collective-permute-done | bytes 329760 | tf_op jit(solution)/shard_map/ppermute | solution.py:274
  197.1 11.9 %backward_1.1 = (f32[160,8,128]{2,1,0:T(8,128)S(1)}, f32[8,128]{1,0:T(8,128)S(1)}, bf16[32,17,8,128]{3,2,1,0:T(8,128)(2,1)S(1)}, bf16[32,17,8,128]{3,2,1,0:T(8,128)(2,1)S(1)}) custom-call(s32[1]{0:T(128)} %bitcast.here, s32[640]{0:T(1024)S(1)} %copy-done.4, s32[640]{0:T(1024)S(1)} %fusion.spot, bf16[161,8,128]{2,1,0:T(8,128)(2,1)S(1)} %forward_1.1.mine, ...), custom_call_target="tpu_custom_call" | custom-call | tf_op jit(solution)/shard_map/backward_1/pallas_call | solution.py:202
  212.9 21.1 %all_to_all.40.chunks = bf16[32,17,8,128]{3,2,1,0:T(8,128)(2,1)S(1)} all-to-all(bf16[32,17,8,128]{3,2,1,0:T(8,128)(2,1)S(1)} %add_convert_fusion), channel_id=1, replica_groups={{0,4,8,12,16,20,24,28,32,36,40,44,48,52,56,60,64,68,72,76,80,84,88,92,9..., dimensions={0} | all-to-all | bytes 2228224 | tf_op jit(solution)/shard_map/all_to_all | solution.py:227
  234.0 6.8 %columns_2.1 = (f32[16,8,128]{2,1,0:T(8,128)S(1)}, f32[8,128]{1,0:T(8,128)S(1)}, bf16[32,17,8,128]{3,2,1,0:T(8,128)(2,1)S(1)}, f32[16,8,128]{2,1,0:T(8,128)S(1)}...) custom-call(bf16[32,17,8,128]{3,2,1,0:T(8,128)(2,1)S(1)} %all_to_all.40.chunks, ...), custom_call_target="tpu_custom_call" | custom-call | tf_op jit(solution)/shard_map/columns_2/pallas_call | solution.py:202
  240.7 21.5 %all_to_all.41 = bf16[32,17,8,128]{3,2,1,0:T(8,128)(2,1)S(1)} all-to-all(bf16[32,17,8,128]{3,2,1,0:T(8,128)(2,1)S(1)} %get-tuple-element.51), channel_id=1, replica_groups={{0,4,8,12,16,20,24,28,32,36,40,44,48,52,56,60,64,68,72,76,80,84,88,92,9..., dimensions={0} | all-to-all | bytes 2228224 | tf_op jit(solution)/shard_map/all_to_all | solution.py:227
  262.2 2.5 collective-permute-start.7
  267.1 13.6 %forward_2.1.mine = bf16[161,8,128]{2,1,0:T(8,128)(2,1)S(1)} custom-call(s32[640]{0:T(1024)S(1)} %copy-done.4, s32[640]{0:T(1024)S(1)} %fusion.spot, bf16[544,8,128]{2,1,0:T(8,128)(2,1)S(1)} %bitcast.7, bf16[544,8,128]{2,1,0:T(8,128)(2,1)S(1)} %bitcast.10, bf16[640,128,128]{2,1,0:T(8,128)(2,1)} %blocks.11), custom_call_target="tpu_custom_call" | custom-call | tf_op jit(solution)/shard_map/forward_2/pallas_call | solution.py:202
  283.1 8.1 %collective-permute-done.8.other = bf16[161,8,128]{2,1,0:T(8,128)(2,1)S(1)} collective-permute-done((bf16[161,8,128]{2,1,0:T(8,128)(2,1)S(1)}, bf16[161,8,128]{2,1,0:T(8,128)(2,1)S(1)}, u32[]{:S(2)}, u32[]{:S(2)}) %collective-permute-start.8) | collective-permute-done | bytes 329760 | tf_op jit(solution)/shard_map/ppermute | solution.py:274
  291.8 14.9 %all_to_all.42.norms = f32[64,8,128]{2,1,0:T(8,128)S(1)} all-to-all(f32[64,8,128]{2,1,0:T(8,128)S(1)} %get-tuple-element.54), channel_id=1, replica_groups=mesh['rows'=64,'cols'=2] {'rows'}, dimensions={0} | all-to-all | bytes 524288 | tf_op jit(solution)/shard_map/all_to_all | solution.py:294
  (26 shorter events, 26.5 us)
Async XLA Ops:
  1.3 1.1 copy-start.1
  2.4 0.7 copy-start.3
  14.7 3.9 %collective-permute-start = (bf16[32,17,8,128]{3,2,1,0:T(8,128)(2,1)S(1)}, bf16[32,17,8,128]{3,2,1,0:T(8,128)(2,1)S(1)}, u32[]{:S(2)}, u32[]{:S(2)}) collective-permute-start(bf16[32,17,8,128]{3,2,1,0:T(8,128)(2,1)S(1)} %get-tuple-element.33), channel_id=1, source_target_pairs={{0,2},{2,0},{4,6},{6,4},{8,10},{10,8},{12,14},{14,12},{16,18},{18,... | collective-permute-start | bytes 3342344 | tf_op jit(solution)/shard_map/ppermute | solution.py:230
  18.9 26.7 %copy-start = (f32[16,128,128]{2,1,0:T(8,128)S(1)}, f32[16,128,128]{2,1,0:T(8,128)}, u32[]{:S(2)}) copy-start(f32[16,128,128]{2,1,0:T(8,128)} %precond.7) | copy-start | bytes 3145732
  52.3 26.4 %copy-start.4 = (s32[640]{0:T(1024)S(1)}, s32[640]{0:T(1024)}, u32[]{:S(2)}) copy-start(s32[640]{0:T(1024)} %row.11) | copy-start | bytes 7684
  73.8 4.9 %collective-permute-start.1 = (bf16[32,17,8,128]{3,2,1,0:T(8,128)(2,1)S(1)}, bf16[32,17,8,128]{3,2,1,0:T(8,128)(2,1)S(1)}, u32[]{:S(2)}, u32[]{:S(2)}) collective-permute-start(bf16[32,17,8,128]{3,2,1,0:T(8,128)(2,1)S(1)} %all_to_all.37), channel_id=1, source_target_pairs={{0,2},{2,0},{4,6},{6,4},{8,10},{10,8},{12,14},{14,12},{16,18},{18,... | collective-permute-start | bytes 3342344 | tf_op jit(solution)/shard_map/ppermute | solution.py:230
  78.7 24.2 %copy-start.2 = (f32[160,8,128]{2,1,0:T(8,128)S(1)}, f32[160,8,128]{2,1,0:T(8,128)}, u32[]{:S(2)}) copy-start(f32[160,8,128]{2,1,0:T(8,128)} %before.1) | copy-start | bytes 1966084
  92.3 10.5 %collective-permute-start.2 = (bf16[161,8,128]{2,1,0:T(8,128)(2,1)S(1)}, bf16[161,8,128]{2,1,0:T(8,128)(2,1)S(1)}, u32[]{:S(2)}, u32[]{:S(2)}) collective-permute-start(bf16[161,8,128]{2,1,0:T(8,128)(2,1)S(1)} %forward_0.1.mine), channel_id=1, source_target_pairs={{0,1},{1,0},{2,3},{3,2},{4,5},{5,4},{6,7},{7,6},{8,9},{9,8},{10,11... | collective-permute-start | bytes 989192 | tf_op jit(solution)/shard_map/ppermute | solution.py:274
  114.8 3.7 %collective-permute-start.3 = (bf16[32,17,8,128]{3,2,1,0:T(8,128)(2,1)S(1)}, bf16[32,17,8,128]{3,2,1,0:T(8,128)(2,1)S(1)}, u32[]{:S(2)}, u32[]{:S(2)}) collective-permute-start(bf16[32,17,8,128]{3,2,1,0:T(8,128)(2,1)S(1)} %get-tuple-element.37), channel_id=1, source_target_pairs={{0,2},{2,0},{4,6},{6,4},{8,10},{10,8},{12,14},{14,12},{16,18},{18,... | collective-permute-start | bytes 3342344 | tf_op jit(solution)/shard_map/ppermute | solution.py:230
  168.0 4.9 %collective-permute-start.4 = (bf16[32,17,8,128]{3,2,1,0:T(8,128)(2,1)S(1)}, bf16[32,17,8,128]{3,2,1,0:T(8,128)(2,1)S(1)}, u32[]{:S(2)}, u32[]{:S(2)}) collective-permute-start(bf16[32,17,8,128]{3,2,1,0:T(8,128)(2,1)S(1)} %all_to_all.39), channel_id=1, source_target_pairs={{0,2},{2,0},{4,6},{6,4},{8,10},{10,8},{12,14},{14,12},{16,18},{18,... | collective-permute-start | bytes 3342344 | tf_op jit(solution)/shard_map/ppermute | solution.py:230
  186.5 10.5 %collective-permute-start.5 = (bf16[161,8,128]{2,1,0:T(8,128)(2,1)S(1)}, bf16[161,8,128]{2,1,0:T(8,128)(2,1)S(1)}, u32[]{:S(2)}, u32[]{:S(2)}) collective-permute-start(bf16[161,8,128]{2,1,0:T(8,128)(2,1)S(1)} %forward_1.1.mine), channel_id=1, source_target_pairs={{0,1},{1,0},{2,3},{3,2},{4,5},{5,4},{6,7},{7,6},{8,9},{9,8},{10,11... | collective-permute-start | bytes 989192 | tf_op jit(solution)/shard_map/ppermute | solution.py:274
  209.0 3.7 %collective-permute-start.6 = (bf16[32,17,8,128]{3,2,1,0:T(8,128)(2,1)S(1)}, bf16[32,17,8,128]{3,2,1,0:T(8,128)(2,1)S(1)}, u32[]{:S(2)}, u32[]{:S(2)}) collective-permute-start(bf16[32,17,8,128]{3,2,1,0:T(8,128)(2,1)S(1)} %get-tuple-element.44), channel_id=1, source_target_pairs={{0,2},{2,0},{4,6},{6,4},{8,10},{10,8},{12,14},{14,12},{16,18},{18,... | collective-permute-start | bytes 3342344 | tf_op jit(solution)/shard_map/ppermute | solution.py:230
  262.2 4.9 %collective-permute-start.7 = (bf16[32,17,8,128]{3,2,1,0:T(8,128)(2,1)S(1)}, bf16[32,17,8,128]{3,2,1,0:T(8,128)(2,1)S(1)}, u32[]{:S(2)}, u32[]{:S(2)}) collective-permute-start(bf16[32,17,8,128]{3,2,1,0:T(8,128)(2,1)S(1)} %all_to_all.41), channel_id=1, source_target_pairs={{0,2},{2,0},{4,6},{6,4},{8,10},{10,8},{12,14},{14,12},{16,18},{18,... | collective-permute-start | bytes 3342344 | tf_op jit(solution)/shard_map/ppermute | solution.py:230
  280.7 10.5 %collective-permute-start.8 = (bf16[161,8,128]{2,1,0:T(8,128)(2,1)S(1)}, bf16[161,8,128]{2,1,0:T(8,128)(2,1)S(1)}, u32[]{:S(2)}, u32[]{:S(2)}) collective-permute-start(bf16[161,8,128]{2,1,0:T(8,128)(2,1)S(1)} %forward_2.1.mine), channel_id=1, source_target_pairs={{0,1},{1,0},{2,3},{3,2},{4,5},{5,4},{6,7},{7,6},{8,9},{9,8},{10,11... | collective-permute-start | bytes 989192 | tf_op jit(solution)/shard_map/ppermute | solution.py:274

commit v2 on v1

--- a/solution.py
+++ b/solution.py
@@ -11,7 +11,6 @@
 
 
 EPS = 1e-06
-HIGHEST = lax.Precision.HIGHEST
 F32 = jnp.float32
 BF16 = jnp.bfloat16
 VM = pl.BlockSpec(memory_space=pltpu.VMEM)
@@ -20,7 +19,7 @@
 
 
 def params():
-    return pltpu.CompilerParams(vmem_limit_bytes=32 << 20)
+    return pltpu.CompilerParams(vmem_limit_bytes=16 << 20)
 
 
 def like(shape, dtype=F32):
@@ -45,9 +44,13 @@
     return jnp.sum(jnp.sum(field * field, axis=0), axis=-1, keepdims=True)
 
 
-def accumulate(products, source, target, table, blocks, total):
+def unroll_of(count):
+    return next(u for u in (128, 64, 32, 16, 8, 4, 2) if count % u == 0)
+
+
+def accumulate(products, source, target, table, blocks, total, arrive=None):
     count = blocks.shape[0]
-    unroll = next(u for u in (128, 64, 32, 16, 8, 4, 2) if count % u == 0)
+    unroll = unroll_of(count)
 
     def add(base, pending):
         at, term = pending
@@ -56,6 +59,8 @@
 
     def step(i, carry):
         base = i * unroll
+        if arrive is not None:
+            arrive(i)
         pending = []
         for u in range(0, unroll, 2):
             pair = jnp.concatenate([table[source[base + u]], table[source[base + u + 1]]], axis=0)
@@ -91,9 +96,9 @@
     return both[:half], both[half:]
 
 
-def send_sums(here, row_term, row, spot, blocks, kept, sent, total):
+def send_sums(here, row_term, row, spot, blocks, kept, sent, total, arrive=None):
     total[...] = jnp.zeros_like(total)
-    accumulate(backward_pair, row, spot, row_term, blocks, total)
+    accumulate(backward_pair, row, spot, row_term, blocks, total, arrive)
     half = kept.shape[0] * kept.shape[1]
     kept[...] = total[:half].astype(BF16).reshape(kept.shape)
     sent[...] = total[half:].astype(BF16).reshape(sent.shape)
@@ -104,8 +109,24 @@
         sent[chip, last] = norm
 
 
-def first_kernel(here, row, spot, right_sides, blocks, kept, sent, total):
-    send_sums(here, right_sides, row, spot, blocks, kept, sent, total)
+def first_kernel(here, row, spot, right_sides, blocks, kept, sent, held, total, table, done):
+    count = unroll_of(blocks.shape[0])
+    parts = blocks.shape[0] // count
+
+    def load(i):
+        span = pl.ds(i * count, count)
+        return pltpu.make_async_copy(blocks.at[span], held.at[span], done.at[i])
+
+    right = pltpu.make_async_copy(right_sides, table, done.at[parts])
+    right.start()
+    for i in range(parts):
+        load(i).start()
+    right.wait()
+    send_sums(here, table, row, spot, held, kept, sent, total, lambda i: load(i).wait())
+
+
+def dead_kernel(here, row, spot, row_term, blocks, kept, sent, total):
+    send_sums(here, row_term, row, spot, blocks, kept, sent, total)
 
 
 def new_row_term(mine, other, before, beta, row_term, alpha):
@@ -121,9 +142,16 @@
     send_sums(here, row_term, row, spot, blocks, kept, sent, total)
 
 
+def diagonal(count):
+    lanes = (count, 128)
+    return lax.broadcasted_iota(jnp.int32, lanes, 0) == lax.broadcasted_iota(jnp.int32, lanes, 1)
+
+
 def finish_kernel(mine, other, before, beta, row_term, alpha, norms):
     new_row_term(mine, other, before, beta, row_term, alpha)
-    norms[...] = jnp.broadcast_to(squares(row_term[...])[None], norms.shape)
+    total = squares(row_term[...])
+    flat = jnp.sum(jnp.where(diagonal(total.shape[0]), total, 0.0), axis=0, keepdims=True)
+    norms[...] = jnp.broadcast_to(flat[None], norms.shape)
 
 
 def forward_kernel(step, row, spot, mine, other, blocks, product, table, total):
@@ -153,56 +181,67 @@
     return fresh, search, iterate, -cosine * alpha, sine * phibar
 
 
-def column_kernel(sweep, chunks, precond, *refs):
+def times(field, high, low, side):
+    top = field.astype(BF16)
+    rest = (field - top.astype(F32)).astype(BF16)
+    dims = (((1,), (side,)), ((), ()))
+    both = lax.dot_general(jnp.concatenate([top, rest], axis=0), high, dims, preferred_element_type=F32)
+    half = field.shape[0]
+    return both[:half] + both[half:] + lax.dot_general(top, low, dims, preferred_element_type=F32)
+
+
+def column_kernel(sweep, chunks, *refs):
     if sweep == 0:
-        col_term, beta, scaled = refs
+        precond, col_term, beta, scaled, high, low = refs
+        top = precond[...].astype(BF16)
+        high[...] = top
+        low[...] = (precond[...] - top.astype(F32)).astype(BF16)
     elif sweep == 1:
-        before, alpha, beta_before, col_term, beta, scaled, search, iterate, rhobar, phibar = refs
+        high, low, before, alpha, beta_before, col_term, beta, scaled, search, iterate, rhobar, phibar = refs
         fresh = before[...] / alpha[...][None]
         search[...] = fresh
         iterate[...] = jnp.zeros_like(iterate)
         rhobar[...] = alpha[...]
         phibar[...] = beta_before[...]
     else:
-        (before, alpha, beta_before, search_in, iterate_in, rhobar_in, phibar_in) = refs[:7]
-        col_term, beta, scaled, search, iterate, rhobar, phibar = refs[7:]
+        (high, low, before, alpha, beta_before, search_in, iterate_in, rhobar_in, phibar_in) = refs[:9]
+        col_term, beta, scaled, search, iterate, rhobar, phibar = refs[9:]
         state = (before[...], search_in[...], iterate_in[...], rhobar_in[...], phibar_in[...])
         fresh, search[...], iterate[...], rhobar[...], phibar[...] = advance(state, alpha[...], beta_before[...])
     own = col_term.shape[0]
     gathered = jnp.sum(chunks[...].astype(F32), axis=0)
     beta[...] = jnp.broadcast_to(jnp.sqrt(unpack(gathered[own]) + EPS), beta.shape)
     gathered = gathered * (1.0 / beta[...])[None]
-    norm = jnp.zeros(beta.shape, F32)
+    terms = [times(gathered[c], high[c], low[c], 1) for c in range(own)]
+    if sweep > 0:
+        terms = [terms[c] - beta[...] * fresh[c] for c in range(own)]
+    norm = sum(term * term for term in terms)
+    wholes = [times(terms[c], high[c], low[c], 0).astype(BF16) for c in range(own)]
     for c in range(own):
-        term = lax.dot_general(
-            gathered[c], precond[c], (((1,), (1,)), ((), ())), precision=HIGHEST, preferred_element_type=F32
-        )
-        if sweep > 0:
-            term = term - beta[...] * fresh[c]
-        col_term[c] = term
-        norm = norm + term * term
-        whole = jnp.dot(term, precond[c], precision=HIGHEST, preferred_element_type=F32).astype(BF16)
-        scaled[:, c] = jnp.broadcast_to(whole[None], (scaled.shape[0],) + whole.shape)
+        col_term[c] = terms[c]
+        scaled[:, c] = jnp.broadcast_to(wholes[c][None], (scaled.shape[0],) + wholes[c].shape)
     packed = pack(jnp.sum(norm, axis=-1, keepdims=True), 0)
     scaled[:, own] = jnp.broadcast_to(packed[None], (scaled.shape[0],) + packed.shape)
 
 
-def last_kernel(norms, row_term, before, alpha, beta_before, search, iterate, rhobar, phibar, precond, out, left):
-    beta = jnp.sqrt(jnp.sum(norms[...], axis=0) + EPS)
+def last_kernel(norms, row_term, high, low, before, alpha, beta_before, search, iterate, rhobar, phibar, out, left):
+    flat = jnp.sum(norms[...], axis=0)
+    total = jnp.sum(jnp.where(diagonal(alpha.shape[0]), flat, 0.0), axis=-1, keepdims=True)
+    beta = jnp.broadcast_to(jnp.sqrt(total + EPS), alpha.shape)
     left[...] = row_term[...] * (1.0 / beta)[None]
     state = (before[...], search[...], iterate[...], rhobar[...], phibar[...])
     _, direction, solved, rho, phi = advance(state, alpha[...], beta_before[...])
     rotation = jnp.sqrt(rho * rho + beta * beta)
     solved = solved + ((rho / rotation) * phi / rotation) * direction
     for c in range(out.shape[0]):
-        out[c] = jnp.dot(solved[c], precond[c], precision=HIGHEST, preferred_element_type=F32)
-
-
-def call(kernel, out_shape, operands, scalars=0, scratch=(), name=None):
+        out[c] = times(solved[c], high[c], low[c], 0)
+
+
+def call(kernel, out_shape, operands, scalars=0, scratch=(), name=None, space=pltpu.VMEM):
     return pl.pallas_call(
         kernel,
         out_shape=out_shape,
-        in_specs=[SM] * scalars + [VM] * (len(operands) - scalars),
+        in_specs=[SM] * scalars + [pl.BlockSpec(memory_space=space)] * (len(operands) - scalars),
         out_specs=jax.tree.map(lambda _: VM, out_shape),
         scratch_shapes=list(scratch),
         compiler_params=params(),
@@ -239,27 +278,39 @@
         arrived = core_swap(sent)
         return exchange((kept.astype(F32) + arrived.astype(F32)).astype(BF16))
 
-    kept, sent = call(
-        first_kernel, [part, part], (here, block_row, spot, right_sides, blocks), 3, [total], "first_backward"
+    kept, sent, held = call(
+        first_kernel,
+        [part, part, pltpu.VMEM(blocks.shape, BF16)],
+        (here, block_row, spot, pltpu.with_memory_space_constraint(right_sides, pltpu.HBM), blocks),
+        3,
+        [
+            total,
+            pltpu.VMEM((rows, rhs, size), F32),
+            pltpu.SemaphoreType.DMA((blocks.shape[0] // unroll_of(blocks.shape[0]) + 1,)),
+        ],
+        "first_backward",
+        pl.ANY,
     )
+    blocks = pltpu.with_memory_space_constraint(held, pltpu.VMEM)
     row_term = right_sides
     col_term = alpha = beta = None
     state = []
     for sweep in range(ITERS + 1):
         chunks = scatter(kept, sent)
-        carried = [] if sweep == 0 else [col_term, alpha, beta] + state
-        if sweep == ITERS:
-            finished = carried
+        carried = [precond] if sweep == 0 else [high, low, col_term, alpha, beta] + state
         new = call(
             functools.partial(column_kernel, sweep),
-            [field, norm, part] + ([] if sweep == 0 else [field, field, norm, norm]),
-            (chunks, precond, *carried),
+            [field, norm, part] + ([like(precond.shape, BF16)] * 2 if sweep == 0 else [field, field, norm, norm]),
+            (chunks, *carried),
             name=f"columns_{sweep}",
         )
         col_term, beta, scaled = new[:3]
-        state = list(new[3:])
         if sweep == ITERS:
             break
+        if sweep == 0:
+            high, low = new[3:]
+        else:
+            state = list(new[3:])
         mine = exchange(scaled)
         other = core_swap(mine)
         flat = (half, rhs, size)
@@ -284,15 +335,15 @@
         else:
             row_term, alpha, norms = call(
                 finish_kernel,
-                [row_field, norm, like((devices, rhs, size))],
+                [row_field, norm, like((devices, 1, size))],
                 (product, crossed, row_term, beta),
                 name="finish_rows",
             )
             kept, sent = call(
-                first_kernel, [part, part], (here, block_row, spot, row_term, blocks), 3, [total], "last_backward"
+                dead_kernel, [part, part], (here, block_row, spot, row_term, blocks), 3, [total], "last_backward"
             )
     norms = lax.all_to_all(norms, "rows", 0, 0, tiled=True)
-    return call(last_kernel, [field, row_field], (norms, row_term, *finished, precond), name="last")
+    return call(last_kernel, [field, row_field], (norms, row_term, *carried), name="last")
 
 
 def solution(mesh):

time: 309 us -> 254 us (0.82)
  Pallas kernels: 98.9 us -> 46.9 us
    pallas_call x11, Pallas kernels: 98.9 us -> 46.9 us  [call(): pl.pallas_call(kernel, out_shape=out_shape, in_specs=[SM] * scalars + [pl...]
where the time goes in v2:
time: 254 us
  blocking collectives  146 us (57%)
  Pallas kernels  46.9 us (18%)
  waiting for transfers between devices  38.3 us (15%)
  starting transfers between devices  19.3 us (8%)
    all_to_all x6, blocking collectives, exchange(): lax.all_to_all(parts, 'rows', 0, 0, axis_index_groups=same_core, tiled=True)  133 us
    pallas_call x11, Pallas kernels, call(): pl.pallas_call(kernel, out_shape=out_shape, in_specs=[SM] * scalars + [pl...  46.9 us
    ppermute x3, waiting for transfers between devices, shards(): crossed = lax.ppermute(product, 'cols', [(0, 1), (1, 0)])  24.1 us
    ppermute x6, waiting for transfers between devices, core_swap(): return lax.ppermute(array, 'rows', swap)  14.3 us
    all_to_all x1, blocking collectives, shards(): norms = lax.all_to_all(norms, 'rows', 0, 0, tiled=True)  12.8 us
    ppermute x6, starting transfers between devices, core_swap(): return lax.ppermute(array, 'rows', swap)  11.6 us
    ppermute x3, starting transfers between devices, shards(): crossed = lax.ppermute(product, 'cols', [(0, 1), (1, 0)])  7.67 us
  transfers between devices with their start and end apart: 9, of which 9 were waited for; matrix products, arithmetic and copies ran while one was open for 0% of the time, Pallas kernels for 0%

profile of v2, /device:TPU:1, one launch (start us, length us, event | category | flops | bytes accessed | tf_op | source)
XLA Modules:
  0.0 253.5 jit_solution(3334080096619795104)
XLA Ops:
  2.0 9.2 %first_backward.1 = (bf16[32,17,8,128]{3,2,1,0:T(8,128)(2,1)S(1)}, bf16[32,17,8,128]{3,2,1,0:T(8,128)(2,1)S(1)}, bf16[640,128,128]{2,1,0:T(8,128)(2,1)S(1)}) custom-call(s32[1]{0:T(128)} %bitcast.here, s32[640]{0:T(1024)S(1)} %copy-done.2, s32[640]{0:T(1024)S(1)} %fusion.spot, f32[160,8,128]{2,1,0:T(8,128)} %before.1, bf16[640,128,128]{2,1,0:T(8,128)(2,1)} %blocks.1), custom_call_target="tpu_custom_call" | custom-call | tf_op jit(solution)/shard_map/first_backward/pallas_call | solution.py:241
  12.7 2.4 collective-permute-done
  15.4 26.6 %all_to_all.36.chunks = bf16[32,17,8,128]{3,2,1,0:T(8,128)(2,1)S(1)} all-to-all(bf16[32,17,8,128]{3,2,1,0:T(8,128)(2,1)S(1)} %add_convert_fusion.2), channel_id=1, replica_groups={{0,4,8,12,16,20,24,28,32,36,40,44,48,52,56,60,64,68,72,76,80,84,88,92,9..., dimensions={0} | all-to-all | bytes 2228224 | tf_op jit(solution)/shard_map/all_to_all | solution.py:266
  43.2 21.5 %all_to_all.37 = bf16[32,17,8,128]{3,2,1,0:T(8,128)(2,1)S(1)} all-to-all(bf16[32,17,8,128]{3,2,1,0:T(8,128)(2,1)S(1)} %get-tuple-element.37), channel_id=1, replica_groups={{0,4,8,12,16,20,24,28,32,36,40,44,48,52,56,60,64,68,72,76,80,84,88,92,9..., dimensions={0} | all-to-all | bytes 2228224 | tf_op jit(solution)/shard_map/all_to_all | solution.py:266
  64.6 2.5 collective-permute-start.1
  69.5 7.2 %forward_0.1.mine = bf16[161,8,128]{2,1,0:T(8,128)(2,1)S(1)} custom-call(s32[640]{0:T(1024)S(1)} %copy-done.3, s32[640]{0:T(1024)S(1)} %fusion.spot, bf16[544,8,128]{2,1,0:T(8,128)(2,1)S(1)} %bitcast.8, bf16[544,8,128]{2,1,0:T(8,128)(2,1)S(1)} %bitcast.11, bf16[640,128,128]{2,1,0:T(8,128)(2,1)S(1)} %get-tuple-element.38.blocks), custom_call_target="tpu_custom_call" | custom-call | tf_op jit(solution)/shard_map/forward_0/pallas_call | solution.py:241
  76.7 2.5 collective-permute-start.2
  79.2 8.0 %collective-permute-done.2.other = bf16[161,8,128]{2,1,0:T(8,128)(2,1)S(1)} collective-permute-done((bf16[161,8,128]{2,1,0:T(8,128)(2,1)S(1)}, bf16[161,8,128]{2,1,0:T(8,128)(2,1)S(1)}, u32[]{:S(2)}, u32[]{:S(2)}) %collective-permute-start.2) | collective-permute-done | bytes 329760 | tf_op jit(solution)/shard_map/ppermute | solution.py:325
  87.3 5.5 %backward_0.1 = (f32[160,8,128]{2,1,0:T(8,128)S(1)}, f32[8,128]{1,0:T(8,128)S(1)}, bf16[32,17,8,128]{3,2,1,0:T(8,128)(2,1)S(1)}, bf16[32,17,8,128]{3,2,1,0:T(8,128)(2,1)S(1)}) custom-call(s32[1]{0:T(128)} %bitcast.here, s32[640]{0:T(1024)S(1)} %copy-done.3, s32[640]{0:T(1024)S(1)} %fusion.spot, bf16[161,8,128]{2,1,0:T(8,128)(2,1)S(1)} %forward_0.1.mine, ...), custom_call_target="tpu_custom_call" | custom-call | tf_op jit(solution)/shard_map/backward_0/pallas_call | solution.py:241
  96.8 21.1 %all_to_all.38.chunks = bf16[32,17,8,128]{3,2,1,0:T(8,128)(2,1)S(1)} all-to-all(bf16[32,17,8,128]{3,2,1,0:T(8,128)(2,1)S(1)} %add_convert_fusion.1), channel_id=1, replica_groups={{0,4,8,12,16,20,24,28,32,36,40,44,48,52,56,60,64,68,72,76,80,84,88,92,9..., dimensions={0} | all-to-all | bytes 2228224 | tf_op jit(solution)/shard_map/all_to_all | solution.py:266
  118.9 21.5 %all_to_all.39 = bf16[32,17,8,128]{3,2,1,0:T(8,128)(2,1)S(1)} all-to-all(bf16[32,17,8,128]{3,2,1,0:T(8,128)(2,1)S(1)} %get-tuple-element.46), channel_id=1, replica_groups={{0,4,8,12,16,20,24,28,32,36,40,44,48,52,56,60,64,68,72,76,80,84,88,92,9..., dimensions={0} | all-to-all | bytes 2228224 | tf_op jit(solution)/shard_map/all_to_all | solution.py:266
  140.3 2.5 collective-permute-start.4
  142.8 2.4 collective-permute-done.4
  145.2 7.2 %forward_1.1.mine = bf16[161,8,128]{2,1,0:T(8,128)(2,1)S(1)} custom-call(s32[640]{0:T(1024)S(1)} %copy-done.3, s32[640]{0:T(1024)S(1)} %fusion.spot, bf16[544,8,128]{2,1,0:T(8,128)(2,1)S(1)} %bitcast.9, bf16[544,8,128]{2,1,0:T(8,128)(2,1)S(1)} %bitcast.12, bf16[640,128,128]{2,1,0:T(8,128)(2,1)S(1)} %get-tuple-element.38.blocks), custom_call_target="tpu_custom_call" | custom-call | tf_op jit(solution)/shard_map/forward_1/pallas_call | solution.py:241
  152.4 2.7 %collective-permute-start.5 = (bf16[161,8,128]{2,1,0:T(8,128)(2,1)S(1)}, bf16[161,8,128]{2,1,0:T(8,128)(2,1)S(1)}, u32[]{:S(2)}, u32[]{:S(2)}) collective-permute-start(bf16[161,8,128]{2,1,0:T(8,128)(2,1)S(1)} %forward_1.1.mine), channel_id=1, source_target_pairs={{0,1},{1,0},{2,3},{3,2},{4,5},{5,4},{6,7},{7,6},{8,9},{9,8},{10,11... | collective-permute-start | bytes 989192 | tf_op jit(solution)/shard_map/ppermute | solution.py:325
  155.1 8.0 %collective-permute-done.5.other = bf16[161,8,128]{2,1,0:T(8,128)(2,1)S(1)} collective-permute-done((bf16[161,8,128]{2,1,0:T(8,128)(2,1)S(1)}, bf16[161,8,128]{2,1,0:T(8,128)(2,1)S(1)}, u32[]{:S(2)}, u32[]{:S(2)}) %collective-permute-start.5) | collective-permute-done | bytes 329760 | tf_op jit(solution)/shard_map/ppermute | solution.py:325
  163.1 5.5 %backward_1.1 = (f32[160,8,128]{2,1,0:T(8,128)S(1)}, f32[8,128]{1,0:T(8,128)S(1)}, bf16[32,17,8,128]{3,2,1,0:T(8,128)(2,1)S(1)}, bf16[32,17,8,128]{3,2,1,0:T(8,128)(2,1)S(1)}) custom-call(s32[1]{0:T(128)} %bitcast.here, s32[640]{0:T(1024)S(1)} %copy-done.3, s32[640]{0:T(1024)S(1)} %fusion.spot, bf16[161,8,128]{2,1,0:T(8,128)(2,1)S(1)} %forward_1.1.mine, ...), custom_call_target="tpu_custom_call" | custom-call | tf_op jit(solution)/shard_map/backward_1/pallas_call | solution.py:241
  172.6 21.1 %all_to_all.40.chunks = bf16[32,17,8,128]{3,2,1,0:T(8,128)(2,1)S(1)} all-to-all(bf16[32,17,8,128]{3,2,1,0:T(8,128)(2,1)S(1)} %add_convert_fusion), channel_id=1, replica_groups={{0,4,8,12,16,20,24,28,32,36,40,44,48,52,56,60,64,68,72,76,80,84,88,92,9..., dimensions={0} | all-to-all | bytes 2228224 | tf_op jit(solution)/shard_map/all_to_all | solution.py:266
  194.8 21.5 %all_to_all.41 = bf16[32,17,8,128]{3,2,1,0:T(8,128)(2,1)S(1)} all-to-all(bf16[32,17,8,128]{3,2,1,0:T(8,128)(2,1)S(1)} %get-tuple-element.57), channel_id=1, replica_groups={{0,4,8,12,16,20,24,28,32,36,40,44,48,52,56,60,64,68,72,76,80,84,88,92,9..., dimensions={0} | all-to-all | bytes 2228224 | tf_op jit(solution)/shard_map/all_to_all | solution.py:266
  216.2 2.5 collective-permute-start.7
  221.1 7.2 %forward_2.1.mine = bf16[161,8,128]{2,1,0:T(8,128)(2,1)S(1)} custom-call(s32[640]{0:T(1024)S(1)} %copy-done.3, s32[640]{0:T(1024)S(1)} %fusion.spot, bf16[544,8,128]{2,1,0:T(8,128)(2,1)S(1)} %bitcast.7, bf16[544,8,128]{2,1,0:T(8,128)(2,1)S(1)} %bitcast.10, bf16[640,128,128]{2,1,0:T(8,128)(2,1)S(1)} %get-tuple-element.38.blocks), custom_call_target="tpu_custom_call" | custom-call | tf_op jit(solution)/shard_map/forward_2/pallas_call | solution.py:241
  228.3 2.5 collective-permute-start.8
  230.8 8.0 %collective-permute-done.8.other = bf16[161,8,128]{2,1,0:T(8,128)(2,1)S(1)} collective-permute-done((bf16[161,8,128]{2,1,0:T(8,128)(2,1)S(1)}, bf16[161,8,128]{2,1,0:T(8,128)(2,1)S(1)}, u32[]{:S(2)}, u32[]{:S(2)}) %collective-permute-start.8) | collective-permute-done | bytes 329760 | tf_op jit(solution)/shard_map/ppermute | solution.py:325
  239.4 12.8 %all_to_all.42.norms = f32[64,1,128]{2,1,0:T(1,128)S(1)} all-to-all(f32[64,1,128]{2,1,0:T(1,128)S(1)} %get-tuple-element.60), channel_id=1, replica_groups=mesh['rows'=64,'cols'=2] {'rows'}, dimensions={0} | all-to-all | bytes 65536 | tf_op jit(solution)/shard_map/all_to_all | solution.py:345
  (24 shorter events, 20.9 us)
Async XLA Ops:
  1.3 0.7 copy-start.2
  11.2 3.9 %collective-permute-start = (bf16[32,17,8,128]{3,2,1,0:T(8,128)(2,1)S(1)}, bf16[32,17,8,128]{3,2,1,0:T(8,128)(2,1)S(1)}, u32[]{:S(2)}, u32[]{:S(2)}) collective-permute-start(bf16[32,17,8,128]{3,2,1,0:T(8,128)(2,1)S(1)} %get-tuple-element.36), channel_id=1, source_target_pairs={{0,2},{2,0},{4,6},{6,4},{8,10},{10,8},{12,14},{14,12},{16,18},{18,... | collective-permute-start | bytes 3342344 | tf_op jit(solution)/shard_map/ppermute | solution.py:269
  15.4 26.7 %copy-start.1 = (f32[16,128,128]{2,1,0:T(8,128)S(1)}, f32[16,128,128]{2,1,0:T(8,128)}, u32[]{:S(2)}) copy-start(f32[16,128,128]{2,1,0:T(8,128)} %refs_0_.1) | copy-start | bytes 3145732
  43.2 26.4 %copy-start.3 = (s32[640]{0:T(1024)S(1)}, s32[640]{0:T(1024)}, u32[]{:S(2)}) copy-start(s32[640]{0:T(1024)} %row.11) | copy-start | bytes 7684
  64.6 4.9 %collective-permute-start.1 = (bf16[32,17,8,128]{3,2,1,0:T(8,128)(2,1)S(1)}, bf16[32,17,8,128]{3,2,1,0:T(8,128)(2,1)S(1)}, u32[]{:S(2)}, u32[]{:S(2)}) collective-permute-start(bf16[32,17,8,128]{3,2,1,0:T(8,128)(2,1)S(1)} %all_to_all.37), channel_id=1, source_target_pairs={{0,2},{2,0},{4,6},{6,4},{8,10},{10,8},{12,14},{14,12},{16,18},{18,... | collective-permute-start | bytes 3342344 | tf_op jit(solution)/shard_map/ppermute | solution.py:269
  69.5 17.7 %copy-start = (f32[160,8,128]{2,1,0:T(8,128)S(1)}, f32[160,8,128]{2,1,0:T(8,128)}, u32[]{:S(2)}) copy-start(f32[160,8,128]{2,1,0:T(8,128)} %before.1) | copy-start | bytes 1966084
  76.7 10.5 %collective-permute-start.2 = (bf16[161,8,128]{2,1,0:T(8,128)(2,1)S(1)}, bf16[161,8,128]{2,1,0:T(8,128)(2,1)S(1)}, u32[]{:S(2)}, u32[]{:S(2)}) collective-permute-start(bf16[161,8,128]{2,1,0:T(8,128)(2,1)S(1)} %forward_0.1.mine), channel_id=1, source_target_pairs={{0,1},{1,0},{2,3},{3,2},{4,5},{5,4},{6,7},{7,6},{8,9},{9,8},{10,11... | collective-permute-start | bytes 989192 | tf_op jit(solution)/shard_map/ppermute | solution.py:325
  92.8 3.7 %collective-permute-start.3 = (bf16[32,17,8,128]{3,2,1,0:T(8,128)(2,1)S(1)}, bf16[32,17,8,128]{3,2,1,0:T(8,128)(2,1)S(1)}, u32[]{:S(2)}, u32[]{:S(2)}) collective-permute-start(bf16[32,17,8,128]{3,2,1,0:T(8,128)(2,1)S(1)} %get-tuple-element.41), channel_id=1, source_target_pairs={{0,2},{2,0},{4,6},{6,4},{8,10},{10,8},{12,14},{14,12},{16,18},{18,... | collective-permute-start | bytes 3342344 | tf_op jit(solution)/shard_map/ppermute | solution.py:269
  140.3 4.9 %collective-permute-start.4 = (bf16[32,17,8,128]{3,2,1,0:T(8,128)(2,1)S(1)}, bf16[32,17,8,128]{3,2,1,0:T(8,128)(2,1)S(1)}, u32[]{:S(2)}, u32[]{:S(2)}) collective-permute-start(bf16[32,17,8,128]{3,2,1,0:T(8,128)(2,1)S(1)} %all_to_all.39), channel_id=1, source_target_pairs={{0,2},{2,0},{4,6},{6,4},{8,10},{10,8},{12,14},{14,12},{16,18},{18,... | collective-permute-start | bytes 3342344 | tf_op jit(solution)/shard_map/ppermute | solution.py:269
  152.4 10.7 %collective-permute-start.5 = (bf16[161,8,128]{2,1,0:T(8,128)(2,1)S(1)}, bf16[161,8,128]{2,1,0:T(8,128)(2,1)S(1)}, u32[]{:S(2)}, u32[]{:S(2)}) collective-permute-start(bf16[161,8,128]{2,1,0:T(8,128)(2,1)S(1)} %forward_1.1.mine), channel_id=1, source_target_pairs={{0,1},{1,0},{2,3},{3,2},{4,5},{5,4},{6,7},{7,6},{8,9},{9,8},{10,11... | collective-permute-start | bytes 989192 | tf_op jit(solution)/shard_map/ppermute | solution.py:325
  168.7 3.7 %collective-permute-start.6 = (bf16[32,17,8,128]{3,2,1,0:T(8,128)(2,1)S(1)}, bf16[32,17,8,128]{3,2,1,0:T(8,128)(2,1)S(1)}, u32[]{:S(2)}, u32[]{:S(2)}) collective-permute-start(bf16[32,17,8,128]{3,2,1,0:T(8,128)(2,1)S(1)} %get-tuple-element.50), channel_id=1, source_target_pairs={{0,2},{2,0},{4,6},{6,4},{8,10},{10,8},{12,14},{14,12},{16,18},{18,... | collective-permute-start | bytes 3342344 | tf_op jit(solution)/shard_map/ppermute | solution.py:269
  216.2 4.9 %collective-permute-start.7 = (bf16[32,17,8,128]{3,2,1,0:T(8,128)(2,1)S(1)}, bf16[32,17,8,128]{3,2,1,0:T(8,128)(2,1)S(1)}, u32[]{:S(2)}, u32[]{:S(2)}) collective-permute-start(bf16[32,17,8,128]{3,2,1,0:T(8,128)(2,1)S(1)} %all_to_all.41), channel_id=1, source_target_pairs={{0,2},{2,0},{4,6},{6,4},{8,10},{10,8},{12,14},{14,12},{16,18},{18,... | collective-permute-start | bytes 3342344 | tf_op jit(solution)/shard_map/ppermute | solution.py:269
  228.3 10.5 %collective-permute-start.8 = (bf16[161,8,128]{2,1,0:T(8,128)(2,1)S(1)}, bf16[161,8,128]{2,1,0:T(8,128)(2,1)S(1)}, u32[]{:S(2)}, u32[]{:S(2)}) collective-permute-start(bf16[161,8,128]{2,1,0:T(8,128)(2,1)S(1)} %forward_2.1.mine), channel_id=1, source_target_pairs={{0,1},{1,0},{2,3},{3,2},{4,5},{5,4},{6,7},{7,6},{8,9},{9,8},{10,11... | collective-permute-start | bytes 989192 | tf_op jit(solution)/shard_map/ppermute | solution.py:325

commit v3 on v2

--- a/solution.py
+++ b/solution.py
@@ -16,10 +16,8 @@
 VM = pl.BlockSpec(memory_space=pltpu.VMEM)
 SM = pl.BlockSpec(memory_space=pltpu.SMEM)
 LATE = 16
-
-
-def params():
-    return pltpu.CompilerParams(vmem_limit_bytes=16 << 20)
+AHEAD = 3
+PLAIN = (1, 5)
 
 
 def like(shape, dtype=F32):
@@ -44,27 +42,35 @@
     return jnp.sum(jnp.sum(field * field, axis=0), axis=-1, keepdims=True)
 
 
-def unroll_of(count):
-    return next(u for u in (128, 64, 32, 16, 8, 4, 2) if count % u == 0)
-
-
-def accumulate(products, source, target, table, blocks, total, arrive=None):
-    count = blocks.shape[0]
-    unroll = unroll_of(count)
+def part_of(whole, plain):
+    return next(u for u in (64, 32, 16, 8, 4, 2) if whole % u == 0 and plain % u == 0)
+
+
+def unroll_of(count, most):
+    return next(u for u in (320, 160, 128, 64, 32, 16, 8, 4, 2) if u <= most and count % u == 0)
+
+
+def accumulate(products, source, target, table, get, total, first, count, most=320, arrive=None, also=None):
+    if count == 0:
+        return
+    unroll = unroll_of(count, most)
 
     def add(base, pending):
         at, term = pending
-        spot = target[base + at]
+        spot = target(base + at)
         total[spot] = total[spot] + term
 
     def step(i, carry):
-        base = i * unroll
+        base = first + i * unroll
         if arrive is not None:
-            arrive(i)
+            arrive(first // unroll + i)
         pending = []
         for u in range(0, unroll, 2):
-            pair = jnp.concatenate([table[source[base + u]], table[source[base + u + 1]]], axis=0)
-            pending += list(zip((u, u + 1), products(pair, blocks[pl.ds(base + u, 2)])))
+            pair = jnp.concatenate([table[source(base + u)], table[source(base + u + 1)]], axis=0)
+            if also is not None:
+                also(base + u)
+                also(base + u + 1)
+            pending += list(zip((u, u + 1), products(pair, get(base + u))))
             while len(pending) > LATE:
                 add(base, pending.pop(0))
         for item in pending:
@@ -74,7 +80,7 @@
     lax.fori_loop(0, count // unroll, step, 0)
 
 
-def forward_pair(pair, blocks):
+def turned_pair(pair, blocks):
     both = lax.dot_general(
         pair.astype(BF16),
         blocks.reshape(-1, blocks.shape[2]),
@@ -86,7 +92,7 @@
     return both[:half, :size], both[half:, size:]
 
 
-def backward_pair(pair, blocks):
+def block_pair(pair, blocks):
     half = pair.shape[0] // 2
     none = jnp.zeros((half, pair.shape[1]), F32)
     spread = jnp.concatenate(
@@ -96,9 +102,7 @@
     return both[:half], both[half:]
 
 
-def send_sums(here, row_term, row, spot, blocks, kept, sent, total, arrive=None):
-    total[...] = jnp.zeros_like(total)
-    accumulate(backward_pair, row, spot, row_term, blocks, total, arrive)
+def finish_sums(here, row_term, kept, sent, total):
     half = kept.shape[0] * kept.shape[1]
     kept[...] = total[:half].astype(BF16).reshape(kept.shape)
     sent[...] = total[half:].astype(BF16).reshape(sent.shape)
@@ -109,24 +113,90 @@
         sent[chip, last] = norm
 
 
-def first_kernel(here, row, spot, right_sides, blocks, kept, sent, held, total, table, done):
-    count = unroll_of(blocks.shape[0])
-    parts = blocks.shape[0] // count
-
-    def load(i):
-        span = pl.ds(i * count, count)
-        return pltpu.make_async_copy(blocks.at[span], held.at[span], done.at[i])
-
-    right = pltpu.make_async_copy(right_sides, table, done.at[parts])
-    right.start()
-    for i in range(parts):
-        load(i).start()
-    right.wait()
-    send_sums(here, table, row, spot, held, kept, sent, total, lambda i: load(i).wait())
-
-
-def dead_kernel(here, row, spot, row_term, blocks, kept, sent, total):
-    send_sums(here, row_term, row, spot, blocks, kept, sent, total)
+def send_sums(here, row, spot, row_term, stored, kept, sent, total):
+    count = row.shape[0]
+    plain = stored.shape[0] - count
+    total[...] = jnp.zeros_like(total)
+    rows, spots = lambda n: row[n], lambda n: spot[n]
+    accumulate(block_pair, rows, spots, row_term, lambda n: stored[pl.ds(count + n, 2)], total, 0, plain)
+    accumulate(turned_pair, rows, spots, row_term, lambda n: stored[pl.ds(n, 2)], total, plain, count - plain)
+    finish_sums(here, row_term, kept, sent, total)
+
+
+def place(column, core, own, half):
+    owner = column // own
+    return ((owner & 1) ^ core) * half + (owner >> 1) * (own + 1) + column % own
+
+
+def first_kernel(own, here, row_in, column_in, right_sides, blocks, kept, sent, stored, total, rest, table, row, column, done):
+    whole = blocks.shape[0]
+    plain = stored.shape[0] - whole
+    count = part_of(whole, plain)
+    half = kept.shape[0] * kept.shape[1]
+    core = here[0]
+    shift = own.bit_length() - 1
+
+    def load(i, early):
+        to = stored.at[pl.ds(whole + i * count, count)] if early else rest.at[pl.ds(i * count - plain, count)]
+        return pltpu.make_async_copy(blocks.at[pl.ds(i * count, count)], to, done.at[i])
+
+    def start(i):
+        @pl.when(i < plain // count)
+        def _():
+            load(i, True).start()
+
+        @pl.when((i >= plain // count) & (i < whole // count))
+        def _():
+            load(i, False).start()
+
+    small = [
+        pltpu.make_async_copy(a, b, done.at[whole // count + i])
+        for i, (a, b) in enumerate(((row_in, row), (column_in, column), (right_sides, table)))
+    ]
+    for copy in small:
+        copy.start()
+    for i in range(AHEAD):
+        start(i)
+
+    def spot(n):
+        if own != 1 << shift:
+            return place(column[n], core, own, half)
+        owner = lax.shift_right_logical(column[n], shift)
+        chip = lax.shift_right_logical(owner, 1)
+        return ((owner & 1) ^ core) * half + chip * (own + 1) + (column[n] & (own - 1))
+
+    for copy in small:
+        copy.wait()
+    total[...] = jnp.zeros_like(total)
+    for early, first, until in ((True, 0, plain), (False, plain, whole)):
+        ref, shifted = (stored, whole) if early else (rest, -plain)
+
+        def arrive(i, early=early):
+            load(i, early).wait()
+            start(i + AHEAD)
+
+        def turn(n, ref=ref, shifted=shifted):
+            stored[n] = ref[shifted + n].T
+
+        def get(n, ref=ref, shifted=shifted):
+            return ref[pl.ds(shifted + n, 2)]
+
+        accumulate(
+            block_pair, lambda n: row[n], spot, table, get, total, first, until - first, count, arrive, turn
+        )
+    finish_sums(here, table, kept, sent, total)
+
+
+def place_kernel(own, half, here, column, spot):
+    spot[...] = place(column[...], here[0], own, half)
+
+
+def add_kernel(kept, arrived, both):
+    both[...] = (kept[...].astype(F32) + arrived[...].astype(F32)).astype(BF16)
+
+
+def dead_kernel(here, row, spot, row_term, stored, kept, sent, total):
+    send_sums(here, row, spot, row_term, stored, kept, sent, total)
 
 
 def new_row_term(mine, other, before, beta, row_term, alpha):
@@ -137,9 +207,9 @@
     row_term[...] = product * (1.0 / alpha[...])[None] - before[...] * (alpha[...] / beta[...])[None]
 
 
-def back_kernel(here, row, spot, mine, other, before, beta, blocks, row_term, alpha, kept, sent, total):
+def back_kernel(here, row, spot, mine, other, before, beta, stored, row_term, alpha, kept, sent, total):
     new_row_term(mine, other, before, beta, row_term, alpha)
-    send_sums(here, row_term, row, spot, blocks, kept, sent, total)
+    send_sums(here, row, spot, row_term, stored, kept, sent, total)
 
 
 def diagonal(count):
@@ -154,12 +224,13 @@
     norms[...] = jnp.broadcast_to(flat[None], norms.shape)
 
 
-def forward_kernel(step, row, spot, mine, other, blocks, product, table, total):
+def forward_kernel(step, row, spot, mine, other, stored, product, table, total):
     half = mine.shape[0]
     table[:half] = mine[...].astype(F32)
     table[half:] = other[...].astype(F32)
     total[...] = jnp.zeros_like(total)
-    accumulate(forward_pair, spot, row, table, blocks, total)
+    rows, spots = lambda n: row[n], lambda n: spot[n]
+    accumulate(block_pair, spots, rows, table, lambda n: stored[pl.ds(n, 2)], total, 0, row.shape[0])
     count = total.shape[0]
     product[:count] = total[...].astype(BF16)
     norm = jnp.zeros(total.shape[1:], F32)
@@ -237,14 +308,14 @@
         out[c] = times(solved[c], high[c], low[c], 0)
 
 
-def call(kernel, out_shape, operands, scalars=0, scratch=(), name=None, space=pltpu.VMEM):
+def call(kernel, out_shape, operands, scalars=0, scratch=(), name=None, space=pltpu.VMEM, room=8):
     return pl.pallas_call(
         kernel,
         out_shape=out_shape,
         in_specs=[SM] * scalars + [pl.BlockSpec(memory_space=space)] * (len(operands) - scalars),
         out_specs=jax.tree.map(lambda _: VM, out_shape),
         scratch_shapes=list(scratch),
-        compiler_params=params(),
+        compiler_params=pltpu.CompilerParams(vmem_limit_bytes=room << 20),
         name=name,
     )(*operands)
 
@@ -257,8 +328,9 @@
     half = chips * (own + 1)
     core = lax.rem(lax.axis_index("rows"), 2)
     here = core[None].astype(jnp.int32)
-    owner = block_col // own
-    spot = ((owner & 1) ^ core) * half + (owner >> 1) * (own + 1) + block_col % own
+    spot = call(
+        functools.partial(place_kernel, own, half), like(block_col.shape, jnp.int32), (here, block_col), 1, name="place"
+    )
     same_core = [[2 * chip + c for chip in range(chips)] for c in range(2)]
     swap = [(d, d ^ 1) for d in range(devices)]
 
@@ -275,23 +347,29 @@
     total = pltpu.VMEM((2 * half, rhs, size), F32)
 
     def scatter(kept, sent):
-        arrived = core_swap(sent)
-        return exchange((kept.astype(F32) + arrived.astype(F32)).astype(BF16))
-
-    kept, sent, held = call(
-        first_kernel,
-        [part, part, pltpu.VMEM(blocks.shape, BF16)],
-        (here, block_row, spot, pltpu.with_memory_space_constraint(right_sides, pltpu.HBM), blocks),
-        3,
+        return exchange(call(add_kernel, part, (kept, core_swap(sent)), name="add_cores"))
+
+    in_hbm = [pltpu.with_memory_space_constraint(a, pltpu.HBM) for a in (block_row, block_col, right_sides, blocks)]
+    count = blocks.shape[0]
+    plain = count * PLAIN[0] // PLAIN[1] // 2 * 2
+    kept, sent, stored = call(
+        functools.partial(first_kernel, own),
+        [part, part, pltpu.VMEM((count + plain,) + blocks.shape[1:], BF16)],
+        (here, *in_hbm),
+        1,
         [
             total,
+            pltpu.VMEM((count - plain,) + blocks.shape[1:], BF16),
             pltpu.VMEM((rows, rhs, size), F32),
-            pltpu.SemaphoreType.DMA((blocks.shape[0] // unroll_of(blocks.shape[0]) + 1,)),
+            pltpu.SMEM(block_row.shape, jnp.int32),
+            pltpu.SMEM(block_col.shape, jnp.int32),
+            pltpu.SemaphoreType.DMA((count // part_of(count, plain) + 3,)),
         ],
         "first_backward",
         pl.ANY,
+        7 + (2 * (count - plain) * size * size >> 20),
     )
-    blocks = pltpu.with_memory_space_constraint(held, pltpu.VMEM)
+    stored = pltpu.with_memory_space_constraint(stored, pltpu.VMEM)
     row_term = right_sides
     col_term = alpha = beta = None
     state = []
@@ -317,7 +395,7 @@
         product = call(
             functools.partial(forward_kernel, own + 1),
             like((rows + 1, rhs, size), BF16),
-            (block_row, spot, mine.reshape(flat), other.reshape(flat), blocks),
+            (block_row, spot, mine.reshape(flat), other.reshape(flat), stored),
             2,
             [pltpu.VMEM((2 * half, rhs, size), F32), pltpu.VMEM((rows, rhs, size), F32)],
             f"forward_{sweep}",
@@ -327,7 +405,7 @@
             row_term, alpha, kept, sent = call(
                 back_kernel,
                 [row_field, norm, part, part],
-                (here, block_row, spot, product, crossed, row_term, beta, blocks),
+                (here, block_row, spot, product, crossed, row_term, beta, stored),
                 3,
                 [total],
                 f"backward_{sweep}",
@@ -340,7 +418,7 @@
                 name="finish_rows",
             )
             kept, sent = call(
-                dead_kernel, [part, part], (here, block_row, spot, row_term, blocks), 3, [total], "last_backward"
+                dead_kernel, [part, part], (here, block_row, spot, row_term, stored), 3, [total], "last_backward"
             )
     norms = lax.all_to_all(norms, "rows", 0, 0, tiled=True)
     return call(last_kernel, [field, row_field], (norms, row_term, *carried), name="last")

time: 254 us -> 248 us (0.976)
  Pallas kernels: 46.9 us -> 43.8 us
    pallas_call x11 -> x15, Pallas kernels: 46.9 us -> 43.8 us  [call(): pl.pallas_call(kernel, out_shape=out_shape, in_specs=[SM] * scalars + [pl...]
where the time goes in v3:
time: 248 us
  blocking collectives  146 us (59%)
  Pallas kernels  43.8 us (18%)
  waiting for transfers between devices  38.4 us (15%)
  starting transfers between devices  19 us (8%)
    all_to_all x6, blocking collectives, exchange(): lax.all_to_all(parts, 'rows', 0, 0, axis_index_groups=same_core, tiled=True)  133 us
    pallas_call x15, Pallas kernels, call(): pl.pallas_call(kernel, out_shape=out_shape, in_specs=[SM] * scalars + [pl...  43.8 us
    ppermute x3, waiting for transfers between devices, shards(): crossed = lax.ppermute(product, 'cols', [(0, 1), (1, 0)])  24.1 us
    ppermute x6, waiting for transfers between devices, core_swap(): return lax.ppermute(array, 'rows', swap)  14.3 us
    all_to_all x1, blocking collectives, shards(): norms = lax.all_to_all(norms, 'rows', 0, 0, tiled=True)  12.8 us
    ppermute x6, starting transfers between devices, core_swap(): return lax.ppermute(array, 'rows', swap)  11.6 us
    ppermute x3, starting transfers between devices, shards(): crossed = lax.ppermute(product, 'cols', [(0, 1), (1, 0)])  7.44 us
  transfers between devices with their start and end apart: 9, of which 9 were waited for; matrix products, arithmetic and copies ran while one was open for 0% of the time, Pallas kernels for 0%

profile of v3, /device:TPU:1, one launch (start us, length us, event | category | flops | bytes accessed | tf_op | source)
XLA Modules:
  0.0 247.9 jit_solution(4387724175638254344)
XLA Ops:
  0.6 9.1 %first_backward.1 = (bf16[32,17,8,128]{3,2,1,0:T(8,128)(2,1)S(1)}, bf16[32,17,8,128]{3,2,1,0:T(8,128)(2,1)S(1)}, bf16[768,128,128]{2,1,0:T(8,128)(2,1)S(1)}) custom-call(s32[1]{0:T(128)} %bitcast.here, s32[640]{0:T(1024)} %row.9, s32[640]{0:T(1024)} %column_in.1, f32[160,8,128]{2,1,0:T(8,128)} %before.1, bf16[640,128,128]{2,1,0:T(8,128)(2,1)} %blocks.1), custom_call_target="tpu_custom_call" | custom-call | tf_op jit(solution)/shard_map/first_backward/pallas_call | solution.py:312
  11.3 2.4 collective-permute-done.arrived
  13.9 26.7 %all_to_all.36.chunks = bf16[32,17,8,128]{3,2,1,0:T(8,128)(2,1)S(1)} all-to-all(bf16[32,17,8,128]{3,2,1,0:T(8,128)(2,1)S(1)} %add_cores.3), channel_id=1, replica_groups={{0,4,8,12,16,20,24,28,32,36,40,44,48,52,56,60,64,68,72,76,80,84,88,92,9..., dimensions={0} | all-to-all | bytes 2228224 | tf_op jit(solution)/shard_map/all_to_all | solution.py:338
  41.7 21.5 %all_to_all.37 = bf16[32,17,8,128]{3,2,1,0:T(8,128)(2,1)S(1)} all-to-all(bf16[32,17,8,128]{3,2,1,0:T(8,128)(2,1)S(1)} %get-tuple-element.37), channel_id=1, replica_groups={{0,4,8,12,16,20,24,28,32,36,40,44,48,52,56,60,64,68,72,76,80,84,88,92,9..., dimensions={0} | all-to-all | bytes 2228224 | tf_op jit(solution)/shard_map/all_to_all | solution.py:338
  63.1 2.5 %collective-permute-start.1 = (bf16[32,17,8,128]{3,2,1,0:T(8,128)(2,1)S(1)}, bf16[32,17,8,128]{3,2,1,0:T(8,128)(2,1)S(1)}, u32[]{:S(2)}, u32[]{:S(2)}) collective-permute-start(bf16[32,17,8,128]{3,2,1,0:T(8,128)(2,1)S(1)} %all_to_all.37), channel_id=1, source_target_pairs={{0,2},{2,0},{4,6},{6,4},{8,10},{10,8},{12,14},{14,12},{16,18},{18,... | collective-permute-start | bytes 3342344 | tf_op jit(solution)/shard_map/ppermute | solution.py:341
  68.0 4.8 %forward_0.1.mine = bf16[161,8,128]{2,1,0:T(8,128)(2,1)S(1)} custom-call(s32[640]{0:T(1024)S(1)} %copy-done.2, s32[640]{0:T(1024)S(1)} %place.1.spot, bf16[544,8,128]{2,1,0:T(8,128)(2,1)S(1)} %bitcast.7, bf16[544,8,128]{2,1,0:T(8,128)(2,1)S(1)} %bitcast.10, bf16[768,128,128]{2,1,0:T(8,128)(2,1)S(1)} %get-tuple-element.38.stored), custom_call_target="tpu_custom_call" | custom-call | tf_op jit(solution)/shard_map/forward_0/pallas_call | solution.py:312
  72.8 2.5 %collective-permute-start.2 = (bf16[161,8,128]{2,1,0:T(8,128)(2,1)S(1)}, bf16[161,8,128]{2,1,0:T(8,128)(2,1)S(1)}, u32[]{:S(2)}, u32[]{:S(2)}) collective-permute-start(bf16[161,8,128]{2,1,0:T(8,128)(2,1)S(1)} %forward_0.1.mine), channel_id=1, source_target_pairs={{0,1},{1,0},{2,3},{3,2},{4,5},{5,4},{6,7},{7,6},{8,9},{9,8},{10,11... | collective-permute-start | bytes 989192 | tf_op jit(solution)/shard_map/ppermute | solution.py:403
  75.3 8.0 %collective-permute-done.2.other = bf16[161,8,128]{2,1,0:T(8,128)(2,1)S(1)} collective-permute-done((bf16[161,8,128]{2,1,0:T(8,128)(2,1)S(1)}, bf16[161,8,128]{2,1,0:T(8,128)(2,1)S(1)}, u32[]{:S(2)}, u32[]{:S(2)}) %collective-permute-start.2) | collective-permute-done | bytes 329760 | tf_op jit(solution)/shard_map/ppermute | solution.py:403
  83.3 7.3 %backward_0.1 = (f32[160,8,128]{2,1,0:T(8,128)S(1)}, f32[8,128]{1,0:T(8,128)S(1)}, bf16[32,17,8,128]{3,2,1,0:T(8,128)(2,1)S(1)}, bf16[32,17,8,128]{3,2,1,0:T(8,128)(2,1)S(1)}) custom-call(s32[1]{0:T(128)} %bitcast.here, s32[640]{0:T(1024)S(1)} %copy-done.2, s32[640]{0:T(1024)S(1)} %place.1.spot, bf16[161,8,128]{2,1,0:T(8,128)(2,1)S(1)} %forward_0.1.mine, ...), custom_call_target="tpu_custom_call" | custom-call | tf_op jit(solution)/shard_map/backward_0/pallas_call | solution.py:312
  91.9 2.4 collective-permute-done.3.arrived
  94.5 21.1 %all_to_all.38.chunks = bf16[32,17,8,128]{3,2,1,0:T(8,128)(2,1)S(1)} all-to-all(bf16[32,17,8,128]{3,2,1,0:T(8,128)(2,1)S(1)} %add_cores.4), channel_id=1, replica_groups={{0,4,8,12,16,20,24,28,32,36,40,44,48,52,56,60,64,68,72,76,80,84,88,92,9..., dimensions={0} | all-to-all | bytes 2228224 | tf_op jit(solution)/shard_map/all_to_all | solution.py:338
  116.6 21.5 %all_to_all.39 = bf16[32,17,8,128]{3,2,1,0:T(8,128)(2,1)S(1)} all-to-all(bf16[32,17,8,128]{3,2,1,0:T(8,128)(2,1)S(1)} %get-tuple-element.46), channel_id=1, replica_groups={{0,4,8,12,16,20,24,28,32,36,40,44,48,52,56,60,64,68,72,76,80,84,88,92,9..., dimensions={0} | all-to-all | bytes 2228224 | tf_op jit(solution)/shard_map/all_to_all | solution.py:338
  138.1 2.5 %collective-permute-start.4 = (bf16[32,17,8,128]{3,2,1,0:T(8,128)(2,1)S(1)}, bf16[32,17,8,128]{3,2,1,0:T(8,128)(2,1)S(1)}, u32[]{:S(2)}, u32[]{:S(2)}) collective-permute-start(bf16[32,17,8,128]{3,2,1,0:T(8,128)(2,1)S(1)} %all_to_all.39), channel_id=1, source_target_pairs={{0,2},{2,0},{4,6},{6,4},{8,10},{10,8},{12,14},{14,12},{16,18},{18,... | collective-permute-start | bytes 3342344 | tf_op jit(solution)/shard_map/ppermute | solution.py:341
  143.0 4.8 %forward_1.1.mine = bf16[161,8,128]{2,1,0:T(8,128)(2,1)S(1)} custom-call(s32[640]{0:T(1024)S(1)} %copy-done.2, s32[640]{0:T(1024)S(1)} %place.1.spot, bf16[544,8,128]{2,1,0:T(8,128)(2,1)S(1)} %bitcast.9, bf16[544,8,128]{2,1,0:T(8,128)(2,1)S(1)} %bitcast.12, bf16[768,128,128]{2,1,0:T(8,128)(2,1)S(1)} %get-tuple-element.38.stored), custom_call_target="tpu_custom_call" | custom-call | tf_op jit(solution)/shard_map/forward_1/pallas_call | solution.py:312
  147.7 2.5 %collective-permute-start.5 = (bf16[161,8,128]{2,1,0:T(8,128)(2,1)S(1)}, bf16[161,8,128]{2,1,0:T(8,128)(2,1)S(1)}, u32[]{:S(2)}, u32[]{:S(2)}) collective-permute-start(bf16[161,8,128]{2,1,0:T(8,128)(2,1)S(1)} %forward_1.1.mine), channel_id=1, source_target_pairs={{0,1},{1,0},{2,3},{3,2},{4,5},{5,4},{6,7},{7,6},{8,9},{9,8},{10,11... | collective-permute-start | bytes 989192 | tf_op jit(solution)/shard_map/ppermute | solution.py:403
  150.2 8.0 %collective-permute-done.5.other = bf16[161,8,128]{2,1,0:T(8,128)(2,1)S(1)} collective-permute-done((bf16[161,8,128]{2,1,0:T(8,128)(2,1)S(1)}, bf16[161,8,128]{2,1,0:T(8,128)(2,1)S(1)}, u32[]{:S(2)}, u32[]{:S(2)}) %collective-permute-start.5) | collective-permute-done | bytes 329760 | tf_op jit(solution)/shard_map/ppermute | solution.py:403
  158.3 7.3 %backward_1.1 = (f32[160,8,128]{2,1,0:T(8,128)S(1)}, f32[8,128]{1,0:T(8,128)S(1)}, bf16[32,17,8,128]{3,2,1,0:T(8,128)(2,1)S(1)}, bf16[32,17,8,128]{3,2,1,0:T(8,128)(2,1)S(1)}) custom-call(s32[1]{0:T(128)} %bitcast.here, s32[640]{0:T(1024)S(1)} %copy-done.2, s32[640]{0:T(1024)S(1)} %place.1.spot, bf16[161,8,128]{2,1,0:T(8,128)(2,1)S(1)} %forward_1.1.mine, ...), custom_call_target="tpu_custom_call" | custom-call | tf_op jit(solution)/shard_map/backward_1/pallas_call | solution.py:312
  169.5 21.1 %all_to_all.40.chunks = bf16[32,17,8,128]{3,2,1,0:T(8,128)(2,1)S(1)} all-to-all(bf16[32,17,8,128]{3,2,1,0:T(8,128)(2,1)S(1)} %add_cores.5), channel_id=1, replica_groups={{0,4,8,12,16,20,24,28,32,36,40,44,48,52,56,60,64,68,72,76,80,84,88,92,9..., dimensions={0} | all-to-all | bytes 2228224 | tf_op jit(solution)/shard_map/all_to_all | solution.py:338
  191.6 21.5 %all_to_all.41 = bf16[32,17,8,128]{3,2,1,0:T(8,128)(2,1)S(1)} all-to-all(bf16[32,17,8,128]{3,2,1,0:T(8,128)(2,1)S(1)} %get-tuple-element.57), channel_id=1, replica_groups={{0,4,8,12,16,20,24,28,32,36,40,44,48,52,56,60,64,68,72,76,80,84,88,92,9..., dimensions={0} | all-to-all | bytes 2228224 | tf_op jit(solution)/shard_map/all_to_all | solution.py:338
  213.1 2.5 %collective-permute-start.7 = (bf16[32,17,8,128]{3,2,1,0:T(8,128)(2,1)S(1)}, bf16[32,17,8,128]{3,2,1,0:T(8,128)(2,1)S(1)}, u32[]{:S(2)}, u32[]{:S(2)}) collective-permute-start(bf16[32,17,8,128]{3,2,1,0:T(8,128)(2,1)S(1)} %all_to_all.41), channel_id=1, source_target_pairs={{0,2},{2,0},{4,6},{6,4},{8,10},{10,8},{12,14},{14,12},{16,18},{18,... | collective-permute-start | bytes 3342344 | tf_op jit(solution)/shard_map/ppermute | solution.py:341
  217.9 4.8 %forward_2.1.mine = bf16[161,8,128]{2,1,0:T(8,128)(2,1)S(1)} custom-call(s32[640]{0:T(1024)S(1)} %copy-done.2, s32[640]{0:T(1024)S(1)} %place.1.spot, bf16[544,8,128]{2,1,0:T(8,128)(2,1)S(1)} %bitcast.8, bf16[544,8,128]{2,1,0:T(8,128)(2,1)S(1)} %bitcast.11, bf16[768,128,128]{2,1,0:T(8,128)(2,1)S(1)} %get-tuple-element.38.stored), custom_call_target="tpu_custom_call" | custom-call | tf_op jit(solution)/shard_map/forward_2/pallas_call | solution.py:312
  222.7 2.5 %collective-permute-start.8 = (bf16[161,8,128]{2,1,0:T(8,128)(2,1)S(1)}, bf16[161,8,128]{2,1,0:T(8,128)(2,1)S(1)}, u32[]{:S(2)}, u32[]{:S(2)}) collective-permute-start(bf16[161,8,128]{2,1,0:T(8,128)(2,1)S(1)} %forward_2.1.mine), channel_id=1, source_target_pairs={{0,1},{1,0},{2,3},{3,2},{4,5},{5,4},{6,7},{7,6},{8,9},{9,8},{10,11... | collective-permute-start | bytes 989192 | tf_op jit(solution)/shard_map/ppermute | solution.py:403
  225.2 8.0 %collective-permute-done.8.other = bf16[161,8,128]{2,1,0:T(8,128)(2,1)S(1)} collective-permute-done((bf16[161,8,128]{2,1,0:T(8,128)(2,1)S(1)}, bf16[161,8,128]{2,1,0:T(8,128)(2,1)S(1)}, u32[]{:S(2)}, u32[]{:S(2)}) %collective-permute-start.8) | collective-permute-done | bytes 329760 | tf_op jit(solution)/shard_map/ppermute | solution.py:403
  233.8 12.8 %all_to_all.42.norms = f32[64,1,128]{2,1,0:T(1,128)S(1)} all-to-all(f32[64,1,128]{2,1,0:T(1,128)S(1)} %get-tuple-element.60), channel_id=1, replica_groups=mesh['rows'=64,'cols'=2] {'rows'}, dimensions={0} | all-to-all | bytes 65536 | tf_op jit(solution)/shard_map/all_to_all | solution.py:423
  (24 shorter events, 19.4 us)
Async XLA Ops:
  9.8 3.9 %collective-permute-start = (bf16[32,17,8,128]{3,2,1,0:T(8,128)(2,1)S(1)}, bf16[32,17,8,128]{3,2,1,0:T(8,128)(2,1)S(1)}, u32[]{:S(2)}, u32[]{:S(2)}) collective-permute-start(bf16[32,17,8,128]{3,2,1,0:T(8,128)(2,1)S(1)} %get-tuple-element.36), channel_id=1, source_target_pairs={{0,2},{2,0},{4,6},{6,4},{8,10},{10,8},{12,14},{14,12},{16,18},{18,... | collective-permute-start | bytes 3342344 | tf_op jit(solution)/shard_map/ppermute | solution.py:341
  13.9 26.7 %copy-start.1 = (f32[16,128,128]{2,1,0:T(8,128)S(1)}, f32[16,128,128]{2,1,0:T(8,128)}, u32[]{:S(2)}) copy-start(f32[16,128,128]{2,1,0:T(8,128)} %refs_0_.1) | copy-start | bytes 3145732
  41.7 24.0 %copy-start.3 = (s32[640]{0:T(1024)S(1)}, s32[640]{0:T(1024)}, u32[]{:S(2)}) copy-start(s32[640]{0:T(1024)} %column_in.1) | copy-start | bytes 7684
  41.7 26.4 %copy-start.2 = (s32[640]{0:T(1024)S(1)}, s32[640]{0:T(1024)}, u32[]{:S(2)}) copy-start(s32[640]{0:T(1024)} %row.9) | copy-start | bytes 7684
  63.1 4.9 %collective-permute-start.1 = (bf16[32,17,8,128]{3,2,1,0:T(8,128)(2,1)S(1)}, bf16[32,17,8,128]{3,2,1,0:T(8,128)(2,1)S(1)}, u32[]{:S(2)}, u32[]{:S(2)}) collective-permute-start(bf16[32,17,8,128]{3,2,1,0:T(8,128)(2,1)S(1)} %all_to_all.37), channel_id=1, source_target_pairs={{0,2},{2,0},{4,6},{6,4},{8,10},{10,8},{12,14},{14,12},{16,18},{18,... | collective-permute-start | bytes 3342344 | tf_op jit(solution)/shard_map/ppermute | solution.py:341
  68.0 15.3 %copy-start = (f32[160,8,128]{2,1,0:T(8,128)S(1)}, f32[160,8,128]{2,1,0:T(8,128)}, u32[]{:S(2)}) copy-start(f32[160,8,128]{2,1,0:T(8,128)} %before.1) | copy-start | bytes 1966084
  72.8 10.5 %collective-permute-start.2 = (bf16[161,8,128]{2,1,0:T(8,128)(2,1)S(1)}, bf16[161,8,128]{2,1,0:T(8,128)(2,1)S(1)}, u32[]{:S(2)}, u32[]{:S(2)}) collective-permute-start(bf16[161,8,128]{2,1,0:T(8,128)(2,1)S(1)} %forward_0.1.mine), channel_id=1, source_target_pairs={{0,1},{1,0},{2,3},{3,2},{4,5},{5,4},{6,7},{7,6},{8,9},{9,8},{10,11... | collective-permute-start | bytes 989192 | tf_op jit(solution)/shard_map/ppermute | solution.py:403
  90.6 3.6 %collective-permute-start.3 = (bf16[32,17,8,128]{3,2,1,0:T(8,128)(2,1)S(1)}, bf16[32,17,8,128]{3,2,1,0:T(8,128)(2,1)S(1)}, u32[]{:S(2)}, u32[]{:S(2)}) collective-permute-start(bf16[32,17,8,128]{3,2,1,0:T(8,128)(2,1)S(1)} %get-tuple-element.41), channel_id=1, source_target_pairs={{0,2},{2,0},{4,6},{6,4},{8,10},{10,8},{12,14},{14,12},{16,18},{18,... | collective-permute-start | bytes 3342344 | tf_op jit(solution)/shard_map/ppermute | solution.py:341
  138.1 4.9 %collective-permute-start.4 = (bf16[32,17,8,128]{3,2,1,0:T(8,128)(2,1)S(1)}, bf16[32,17,8,128]{3,2,1,0:T(8,128)(2,1)S(1)}, u32[]{:S(2)}, u32[]{:S(2)}) collective-permute-start(bf16[32,17,8,128]{3,2,1,0:T(8,128)(2,1)S(1)} %all_to_all.39), channel_id=1, source_target_pairs={{0,2},{2,0},{4,6},{6,4},{8,10},{10,8},{12,14},{14,12},{16,18},{18,... | collective-permute-start | bytes 3342344 | tf_op jit(solution)/shard_map/ppermute | solution.py:341
  147.7 10.5 %collective-permute-start.5 = (bf16[161,8,128]{2,1,0:T(8,128)(2,1)S(1)}, bf16[161,8,128]{2,1,0:T(8,128)(2,1)S(1)}, u32[]{:S(2)}, u32[]{:S(2)}) collective-permute-start(bf16[161,8,128]{2,1,0:T(8,128)(2,1)S(1)} %forward_1.1.mine), channel_id=1, source_target_pairs={{0,1},{1,0},{2,3},{3,2},{4,5},{5,4},{6,7},{7,6},{8,9},{9,8},{10,11... | collective-permute-start | bytes 989192 | tf_op jit(solution)/shard_map/ppermute | solution.py:403
  165.6 3.6 %collective-permute-start.6 = (bf16[32,17,8,128]{3,2,1,0:T(8,128)(2,1)S(1)}, bf16[32,17,8,128]{3,2,1,0:T(8,128)(2,1)S(1)}, u32[]{:S(2)}, u32[]{:S(2)}) collective-permute-start(bf16[32,17,8,128]{3,2,1,0:T(8,128)(2,1)S(1)} %get-tuple-element.50), channel_id=1, source_target_pairs={{0,2},{2,0},{4,6},{6,4},{8,10},{10,8},{12,14},{14,12},{16,18},{18,... | collective-permute-start | bytes 3342344 | tf_op jit(solution)/shard_map/ppermute | solution.py:341
  213.1 4.9 %collective-permute-start.7 = (bf16[32,17,8,128]{3,2,1,0:T(8,128)(2,1)S(1)}, bf16[32,17,8,128]{3,2,1,0:T(8,128)(2,1)S(1)}, u32[]{:S(2)}, u32[]{:S(2)}) collective-permute-start(bf16[32,17,8,128]{3,2,1,0:T(8,128)(2,1)S(1)} %all_to_all.41), channel_id=1, source_target_pairs={{0,2},{2,0},{4,6},{6,4},{8,10},{10,8},{12,14},{14,12},{16,18},{18,... | collective-permute-start | bytes 3342344 | tf_op jit(solution)/shard_map/ppermute | solution.py:341
  222.7 10.5 %collective-permute-start.8 = (bf16[161,8,128]{2,1,0:T(8,128)(2,1)S(1)}, bf16[161,8,128]{2,1,0:T(8,128)(2,1)S(1)}, u32[]{:S(2)}, u32[]{:S(2)}) collective-permute-start(bf16[161,8,128]{2,1,0:T(8,128)(2,1)S(1)} %forward_2.1.mine), channel_id=1, source_target_pairs={{0,1},{1,0},{2,3},{3,2},{4,5},{5,4},{6,7},{7,6},{8,9},{9,8},{10,11... | collective-permute-start | bytes 989192 | tf_op jit(solution)/shard_map/ppermute | solution.py:403

commit v4 on v3

--- a/solution.py
+++ b/solution.py
@@ -17,7 +17,7 @@
 SM = pl.BlockSpec(memory_space=pltpu.SMEM)
 LATE = 16
 AHEAD = 3
-PLAIN = (1, 5)
+PLAIN = (0, 1)
 
 
 def like(shape, dtype=F32):
@@ -47,10 +47,10 @@
 
 
 def unroll_of(count, most):
-    return next(u for u in (320, 160, 128, 64, 32, 16, 8, 4, 2) if u <= most and count % u == 0)
-
-
-def accumulate(products, source, target, table, get, total, first, count, most=320, arrive=None, also=None):
+    return next(u for u in (640, 320, 160, 128, 64, 32, 16, 8, 4, 2) if u <= most and count % u == 0)
+
+
+def accumulate(products, source, target, table, get, total, first, count, most=640, arrive=None, also=None):
     if count == 0:
         return
     unroll = unroll_of(count, most)
@@ -80,18 +80,6 @@
     lax.fori_loop(0, count // unroll, step, 0)
 
 
-def turned_pair(pair, blocks):
-    both = lax.dot_general(
-        pair.astype(BF16),
-        blocks.reshape(-1, blocks.shape[2]),
-        (((1,), (1,)), ((), ())),
-        preferred_element_type=F32,
-    )
-    size = blocks.shape[1]
-    half = pair.shape[0] // 2
-    return both[:half, :size], both[half:, size:]
-
-
 def block_pair(pair, blocks):
     half = pair.shape[0] // 2
     none = jnp.zeros((half, pair.shape[1]), F32)
@@ -113,14 +101,24 @@
         sent[chip, last] = norm
 
 
-def send_sums(here, row, spot, row_term, stored, kept, sent, total):
-    count = row.shape[0]
-    plain = stored.shape[0] - count
+def send_sums(here, row, spot, row_term, blocks, kept, sent, total):
     total[...] = jnp.zeros_like(total)
-    rows, spots = lambda n: row[n], lambda n: spot[n]
-    accumulate(block_pair, rows, spots, row_term, lambda n: stored[pl.ds(count + n, 2)], total, 0, plain)
-    accumulate(turned_pair, rows, spots, row_term, lambda n: stored[pl.ds(n, 2)], total, plain, count - plain)
+    get = lambda n: blocks[pl.ds(n, 2)]
+    accumulate(block_pair, lambda n: row[n], lambda n: spot[n], row_term, get, total, 0, row.shape[0])
     finish_sums(here, row_term, kept, sent, total)
+
+
+def load_kernel(blocks, after, loaded, done):
+    parts = done.shape[0]
+    count = blocks.shape[0] // parts
+    copies = [
+        pltpu.make_async_copy(blocks.at[pl.ds(i * count, count)], loaded.at[pl.ds(i * count, count)], done.at[i])
+        for i in range(parts)
+    ]
+    for copy in copies:
+        copy.start()
+    for copy in copies:
+        copy.wait()
 
 
 def place(column, core, own, half):
@@ -195,8 +193,8 @@
     both[...] = (kept[...].astype(F32) + arrived[...].astype(F32)).astype(BF16)
 
 
-def dead_kernel(here, row, spot, row_term, stored, kept, sent, total):
-    send_sums(here, row, spot, row_term, stored, kept, sent, total)
+def dead_kernel(here, row, spot, row_term, blocks, kept, sent, total):
+    send_sums(here, row, spot, row_term, blocks, kept, sent, total)
 
 
 def new_row_term(mine, other, before, beta, row_term, alpha):
@@ -207,9 +205,9 @@
     row_term[...] = product * (1.0 / alpha[...])[None] - before[...] * (alpha[...] / beta[...])[None]
 
 
-def back_kernel(here, row, spot, mine, other, before, beta, stored, row_term, alpha, kept, sent, total):
+def back_kernel(here, row, spot, mine, other, before, beta, blocks, row_term, alpha, kept, sent, total):
     new_row_term(mine, other, before, beta, row_term, alpha)
-    send_sums(here, row, spot, row_term, stored, kept, sent, total)
+    send_sums(here, row, spot, row_term, blocks, kept, sent, total)
 
 
 def diagonal(count):
@@ -217,7 +215,7 @@
     return lax.broadcasted_iota(jnp.int32, lanes, 0) == lax.broadcasted_iota(jnp.int32, lanes, 1)
 
 
-def finish_kernel(mine, other, before, beta, row_term, alpha, norms):
+def finish_kernel(mine, other, before, beta, after, row_term, alpha, norms):
     new_row_term(mine, other, before, beta, row_term, alpha)
     total = squares(row_term[...])
     flat = jnp.sum(jnp.where(diagonal(total.shape[0]), total, 0.0), axis=0, keepdims=True)
@@ -295,7 +293,14 @@
     scaled[:, own] = jnp.broadcast_to(packed[None], (scaled.shape[0],) + packed.shape)
 
 
-def last_kernel(norms, row_term, high, low, before, alpha, beta_before, search, iterate, rhobar, phibar, out, left):
+def prepare_kernel(after, high, low, *refs):
+    half = len(refs) // 2
+    for field, out in zip(refs[:half], refs[half:]):
+        for c in range(field.shape[0]):
+            out[c] = times(field[c], high[c], low[c], 0)
+
+
+def last_kernel(norms, row_term, before, search, iterate, alpha, beta_before, rhobar, phibar, out, left):
     flat = jnp.sum(norms[...], axis=0)
     total = jnp.sum(jnp.where(diagonal(alpha.shape[0]), flat, 0.0), axis=-1, keepdims=True)
     beta = jnp.broadcast_to(jnp.sqrt(total + EPS), alpha.shape)
@@ -303,12 +308,10 @@
     state = (before[...], search[...], iterate[...], rhobar[...], phibar[...])
     _, direction, solved, rho, phi = advance(state, alpha[...], beta_before[...])
     rotation = jnp.sqrt(rho * rho + beta * beta)
-    solved = solved + ((rho / rotation) * phi / rotation) * direction
-    for c in range(out.shape[0]):
-        out[c] = times(solved[c], high[c], low[c], 0)
-
-
-def call(kernel, out_shape, operands, scalars=0, scratch=(), name=None, space=pltpu.VMEM, room=8):
+    out[...] = solved + ((rho / rotation) * phi / rotation) * direction
+
+
+def call(kernel, out_shape, operands, scalars=0, scratch=(), name=None, space=pltpu.VMEM, room=8, cost=None):
     return pl.pallas_call(
         kernel,
         out_shape=out_shape,
@@ -316,6 +319,7 @@
         out_specs=jax.tree.map(lambda _: VM, out_shape),
         scratch_shapes=list(scratch),
         compiler_params=pltpu.CompilerParams(vmem_limit_bytes=room << 20),
+        cost_estimate=cost,
         name=name,
     )(*operands)
 
@@ -401,27 +405,43 @@
             f"forward_{sweep}",
         )
         crossed = lax.ppermute(product, "cols", [(0, 1), (1, 0)])
+        loaded = call(
+            load_kernel,
+            pltpu.VMEM(blocks.shape, BF16),
+            (in_hbm[3], product),
+            0,
+            [pltpu.SemaphoreType.DMA((unroll_of(count, 8),))],
+            f"load_{sweep}",
+            pl.ANY,
+            1,
+            pl.CostEstimate(flops=0, bytes_accessed=4 * count * size * size, transcendentals=0),
+        )
+        loaded = pltpu.with_memory_space_constraint(loaded, pltpu.VMEM)
         if sweep < ITERS - 1:
             row_term, alpha, kept, sent = call(
                 back_kernel,
                 [row_field, norm, part, part],
-                (here, block_row, spot, product, crossed, row_term, beta, stored),
+                (here, block_row, spot, product, crossed, row_term, beta, loaded),
                 3,
                 [total],
                 f"backward_{sweep}",
             )
         else:
+            search, iterate, rhobar, phibar = state
+            fields = (col_term, search, iterate)
+            ready = call(prepare_kernel, [field] * 3, (product, high, low, *fields), name="prepare")
             row_term, alpha, norms = call(
                 finish_kernel,
                 [row_field, norm, like((devices, 1, size))],
-                (product, crossed, row_term, beta),
+                (product, crossed, row_term, beta, ready[0]),
                 name="finish_rows",
             )
+            factors = (alpha, beta, rhobar, phibar)
             kept, sent = call(
-                dead_kernel, [part, part], (here, block_row, spot, row_term, stored), 3, [total], "last_backward"
+                dead_kernel, [part, part], (here, block_row, spot, row_term, loaded), 3, [total], "last_backward"
             )
     norms = lax.all_to_all(norms, "rows", 0, 0, tiled=True)
-    return call(last_kernel, [field, row_field], (norms, row_term, *carried), name="last")
+    return call(last_kernel, [field, row_field], (norms, row_term, *ready, *factors), name="last")
 
 
 def solution(mesh):

time: 248 us -> 243 us (0.980)
  waiting for transfers between devices: 38.4 us -> 23.2 us
  Pallas kernels: 43.8 us -> 52.8 us
    ppermute x3, waiting for transfers between devices: 24.1 us -> 8.91 us  [shards(): crossed = lax.ppermute(product, 'cols', [(0, 1), (1, 0)])]
    pallas_call x15 -> x18, Pallas kernels: 43.8 us -> 52.8 us  [call(): pl.pallas_call(kernel, out_shape=out_shape, in_specs=[SM] * scalars + [pl...]
  transfers between devices with their start and end apart: 9 -> 9, of which waited for: 9 -> 9; matrix products, arithmetic and copies ran while one was open for 0% -> 0% of each run, Pallas kernels for 0% -> 6%
where the time goes in v4:
time: 243 us; the launch traced here: 242 us
  blocking collectives  146 us (60%)
  Pallas kernels  52.8 us (22%)
  waiting for transfers between devices  23.2 us (10%)
  starting transfers between devices  19.6 us (8%)
    all_to_all x6, blocking collectives, exchange(): lax.all_to_all(parts, 'rows', 0, 0, axis_index_groups=same_core, tiled=True)  133 us
    pallas_call x18, Pallas kernels, call(): pl.pallas_call(kernel, out_shape=out_shape, in_specs=[SM] * scalars + [pl...  52.8 us
    ppermute x6, waiting for transfers between devices, core_swap(): return lax.ppermute(array, 'rows', swap)  14.3 us
    all_to_all x1, blocking collectives, shards(): norms = lax.all_to_all(norms, 'rows', 0, 0, tiled=True)  12.8 us
    ppermute x6, starting transfers between devices, core_swap(): return lax.ppermute(array, 'rows', swap)  11.6 us
    ppermute x3, waiting for transfers between devices, shards(): crossed = lax.ppermute(product, 'cols', [(0, 1), (1, 0)])  8.91 us
    ppermute x3, starting transfers between devices, shards(): crossed = lax.ppermute(product, 'cols', [(0, 1), (1, 0)])  7.97 us
  transfers between devices with their start and end apart: 9, of which 9 were waited for; matrix products, arithmetic and copies ran while one was open for 0% of the time, Pallas kernels for 6%

profile of v4, /device:TPU:1, one launch (start us, length us, event | category | flops | bytes accessed | tf_op | source)
XLA Modules:
  0.0 242.3 jit_solution(2981726224644843319)
XLA Ops:
  0.6 8.9 %first_backward.1 = (bf16[32,17,8,128]{3,2,1,0:T(8,128)(2,1)S(1)}, bf16[32,17,8,128]{3,2,1,0:T(8,128)(2,1)S(1)}, bf16[640,128,128]{2,1,0:T(8,128)(2,1)S(1)}) custom-call(s32[1]{0:T(128)} %bitcast.here, s32[640]{0:T(1024)} %row.9, s32[640]{0:T(1024)} %column_in.1, f32[160,8,128]{2,1,0:T(8,128)} %before.1, bf16[640,128,128]{2,1,0:T(8,128)(2,1)} %blocks.5), custom_call_target="tpu_custom_call" | custom-call | tf_op jit(solution)/shard_map/first_backward/pallas_call | solution.py:315
  11.1 2.4 collective-permute-done.arrived
  13.7 26.6 %all_to_all.36.chunks = bf16[32,17,8,128]{3,2,1,0:T(8,128)(2,1)S(1)} all-to-all(bf16[32,17,8,128]{3,2,1,0:T(8,128)(2,1)S(1)} %add_cores.3), channel_id=1, replica_groups={{0,4,8,12,16,20,24,28,32,36,40,44,48,52,56,60,64,68,72,76,80,84,88,92,9..., dimensions={0} | all-to-all | bytes 2228224 | tf_op jit(solution)/shard_map/all_to_all | solution.py:342
  41.5 21.5 %all_to_all.37 = bf16[32,17,8,128]{3,2,1,0:T(8,128)(2,1)S(1)} all-to-all(bf16[32,17,8,128]{3,2,1,0:T(8,128)(2,1)S(1)} %get-tuple-element.40), channel_id=1, replica_groups={{0,4,8,12,16,20,24,28,32,36,40,44,48,52,56,60,64,68,72,76,80,84,88,92,9..., dimensions={0} | all-to-all | bytes 2228224 | tf_op jit(solution)/shard_map/all_to_all | solution.py:342
  62.9 2.5 %collective-permute-start.1 = (bf16[32,17,8,128]{3,2,1,0:T(8,128)(2,1)S(1)}, bf16[32,17,8,128]{3,2,1,0:T(8,128)(2,1)S(1)}, u32[]{:S(2)}, u32[]{:S(2)}) collective-permute-start(bf16[32,17,8,128]{3,2,1,0:T(8,128)(2,1)S(1)} %all_to_all.37), channel_id=1, source_target_pairs={{0,2},{2,0},{4,6},{6,4},{8,10},{10,8},{12,14},{14,12},{16,18},{18,... | collective-permute-start | bytes 3342344 | tf_op jit(solution)/shard_map/ppermute | solution.py:345
  67.8 4.4 %forward_0.1.after.mine = bf16[161,8,128]{2,1,0:T(8,128)(2,1)S(1)} custom-call(s32[640]{0:T(1024)S(1)} %copy-done.2, s32[640]{0:T(1024)S(1)} %place.1.spot, bf16[544,8,128]{2,1,0:T(8,128)(2,1)S(1)} %bitcast.7, bf16[544,8,128]{2,1,0:T(8,128)(2,1)S(1)} %bitcast.10, bf16[640,128,128]{2,1,0:T(8,128)(2,1)S(1)} %get-tuple-element.41.stored), custom_call_target="tpu_custom_call" | custom-call | tf_op jit(solution)/shard_map/forward_0/pallas_call | solution.py:315
  72.3 2.7 %collective-permute-start.2 = (bf16[161,8,128]{2,1,0:T(8,128)(2,1)S(1)}, bf16[161,8,128]{2,1,0:T(8,128)(2,1)S(1)}, u32[]{:S(2)}, u32[]{:S(2)}) collective-permute-start(bf16[161,8,128]{2,1,0:T(8,128)(2,1)S(1)} %forward_0.1.after.mine), channel_id=1, source_target_pairs={{0,1},{1,0},{2,3},{3,2},{4,5},{5,4},{6,7},{7,6},{8,9},{9,8},{10,11... | collective-permute-start | bytes 989192 | tf_op jit(solution)/shard_map/ppermute | solution.py:407
  75.0 7.1 %load_0.1.blocks = bf16[640,128,128]{2,1,0:T(8,128)(2,1)S(1)} custom-call(bf16[640,128,128]{2,1,0:T(8,128)(2,1)} %blocks.5, bf16[161,8,128]{2,1,0:T(8,128)(2,1)S(1)} %forward_0.1.after.mine), custom_call_target="tpu_custom_call" | custom-call | bytes 41943040 | tf_op jit(solution)/shard_map/load_0/pallas_call | solution.py:315
  83.0 4.9 %backward_0.1 = (f32[160,8,128]{2,1,0:T(8,128)S(1)}, f32[8,128]{1,0:T(8,128)S(1)}, bf16[32,17,8,128]{3,2,1,0:T(8,128)(2,1)S(1)}, bf16[32,17,8,128]{3,2,1,0:T(8,128)(2,1)S(1)}) custom-call(s32[1]{0:T(128)} %bitcast.here, s32[640]{0:T(1024)S(1)} %copy-done.2, s32[640]{0:T(1024)S(1)} %place.1.spot, bf16[161,8,128]{2,1,0:T(8,128)(2,1)S(1)} %forward_0.1.after.mine, ...), custom_call_target="tpu_custom_call" | custom-call | tf_op jit(solution)/shard_map/backward_0/pallas_call | solution.py:315
  89.2 2.4 collective-permute-done.3.arrived
  91.9 21.1 %all_to_all.38.chunks = bf16[32,17,8,128]{3,2,1,0:T(8,128)(2,1)S(1)} all-to-all(bf16[32,17,8,128]{3,2,1,0:T(8,128)(2,1)S(1)} %add_cores.4), channel_id=1, replica_groups={{0,4,8,12,16,20,24,28,32,36,40,44,48,52,56,60,64,68,72,76,80,84,88,92,9..., dimensions={0} | all-to-all | bytes 2228224 | tf_op jit(solution)/shard_map/all_to_all | solution.py:342
  114.0 21.5 %all_to_all.39 = bf16[32,17,8,128]{3,2,1,0:T(8,128)(2,1)S(1)} all-to-all(bf16[32,17,8,128]{3,2,1,0:T(8,128)(2,1)S(1)} %get-tuple-element.49), channel_id=1, replica_groups={{0,4,8,12,16,20,24,28,32,36,40,44,48,52,56,60,64,68,72,76,80,84,88,92,9..., dimensions={0} | all-to-all | bytes 2228224 | tf_op jit(solution)/shard_map/all_to_all | solution.py:342
  135.4 2.5 %collective-permute-start.4 = (bf16[32,17,8,128]{3,2,1,0:T(8,128)(2,1)S(1)}, bf16[32,17,8,128]{3,2,1,0:T(8,128)(2,1)S(1)}, u32[]{:S(2)}, u32[]{:S(2)}) collective-permute-start(bf16[32,17,8,128]{3,2,1,0:T(8,128)(2,1)S(1)} %all_to_all.39), channel_id=1, source_target_pairs={{0,2},{2,0},{4,6},{6,4},{8,10},{10,8},{12,14},{14,12},{16,18},{18,... | collective-permute-start | bytes 3342344 | tf_op jit(solution)/shard_map/ppermute | solution.py:345
  140.3 4.4 %forward_1.1.after.mine = bf16[161,8,128]{2,1,0:T(8,128)(2,1)S(1)} custom-call(s32[640]{0:T(1024)S(1)} %copy-done.2, s32[640]{0:T(1024)S(1)} %place.1.spot, bf16[544,8,128]{2,1,0:T(8,128)(2,1)S(1)} %bitcast.9, bf16[544,8,128]{2,1,0:T(8,128)(2,1)S(1)} %bitcast.12, bf16[640,128,128]{2,1,0:T(8,128)(2,1)S(1)} %get-tuple-element.41.stored), custom_call_target="tpu_custom_call" | custom-call | tf_op jit(solution)/shard_map/forward_1/pallas_call | solution.py:315
  144.8 2.7 %collective-permute-start.5 = (bf16[161,8,128]{2,1,0:T(8,128)(2,1)S(1)}, bf16[161,8,128]{2,1,0:T(8,128)(2,1)S(1)}, u32[]{:S(2)}, u32[]{:S(2)}) collective-permute-start(bf16[161,8,128]{2,1,0:T(8,128)(2,1)S(1)} %forward_1.1.after.mine), channel_id=1, source_target_pairs={{0,1},{1,0},{2,3},{3,2},{4,5},{5,4},{6,7},{7,6},{8,9},{9,8},{10,11... | collective-permute-start | bytes 989192 | tf_op jit(solution)/shard_map/ppermute | solution.py:407
  147.5 7.1 %load_1.1.blocks = bf16[640,128,128]{2,1,0:T(8,128)(2,1)S(1)} custom-call(bf16[640,128,128]{2,1,0:T(8,128)(2,1)} %blocks.5, bf16[161,8,128]{2,1,0:T(8,128)(2,1)S(1)} %forward_1.1.after.mine), custom_call_target="tpu_custom_call" | custom-call | bytes 41943040 | tf_op jit(solution)/shard_map/load_1/pallas_call | solution.py:315
  155.6 4.9 %backward_1.1 = (f32[160,8,128]{2,1,0:T(8,128)S(1)}, f32[8,128]{1,0:T(8,128)S(1)}, bf16[32,17,8,128]{3,2,1,0:T(8,128)(2,1)S(1)}, bf16[32,17,8,128]{3,2,1,0:T(8,128)(2,1)S(1)}) custom-call(s32[1]{0:T(128)} %bitcast.here, s32[640]{0:T(1024)S(1)} %copy-done.2, s32[640]{0:T(1024)S(1)} %place.1.spot, bf16[161,8,128]{2,1,0:T(8,128)(2,1)S(1)} %forward_1.1.after.mine, ...), custom_call_target="tpu_custom_call" | custom-call | tf_op jit(solution)/shard_map/backward_1/pallas_call | solution.py:315
  164.4 21.1 %all_to_all.40.chunks = bf16[32,17,8,128]{3,2,1,0:T(8,128)(2,1)S(1)} all-to-all(bf16[32,17,8,128]{3,2,1,0:T(8,128)(2,1)S(1)} %add_cores.5), channel_id=1, replica_groups={{0,4,8,12,16,20,24,28,32,36,40,44,48,52,56,60,64,68,72,76,80,84,88,92,9..., dimensions={0} | all-to-all | bytes 2228224 | tf_op jit(solution)/shard_map/all_to_all | solution.py:342
  186.5 21.5 %all_to_all.41 = bf16[32,17,8,128]{3,2,1,0:T(8,128)(2,1)S(1)} all-to-all(bf16[32,17,8,128]{3,2,1,0:T(8,128)(2,1)S(1)} %get-tuple-element.60), channel_id=1, replica_groups={{0,4,8,12,16,20,24,28,32,36,40,44,48,52,56,60,64,68,72,76,80,84,88,92,9..., dimensions={0} | all-to-all | bytes 2228224 | tf_op jit(solution)/shard_map/all_to_all | solution.py:342
  208.0 2.5 %collective-permute-start.7 = (bf16[32,17,8,128]{3,2,1,0:T(8,128)(2,1)S(1)}, bf16[32,17,8,128]{3,2,1,0:T(8,128)(2,1)S(1)}, u32[]{:S(2)}, u32[]{:S(2)}) collective-permute-start(bf16[32,17,8,128]{3,2,1,0:T(8,128)(2,1)S(1)} %all_to_all.41), channel_id=1, source_target_pairs={{0,2},{2,0},{4,6},{6,4},{8,10},{10,8},{12,14},{14,12},{16,18},{18,... | collective-permute-start | bytes 3342344 | tf_op jit(solution)/shard_map/ppermute | solution.py:345
  212.9 4.4 %forward_2.1.after.mine = bf16[161,8,128]{2,1,0:T(8,128)(2,1)S(1)} custom-call(s32[640]{0:T(1024)S(1)} %copy-done.2, s32[640]{0:T(1024)S(1)} %place.1.spot, bf16[544,8,128]{2,1,0:T(8,128)(2,1)S(1)} %bitcast.8, bf16[544,8,128]{2,1,0:T(8,128)(2,1)S(1)} %bitcast.11, bf16[640,128,128]{2,1,0:T(8,128)(2,1)S(1)} %get-tuple-element.41.stored), custom_call_target="tpu_custom_call" | custom-call | tf_op jit(solution)/shard_map/forward_2/pallas_call | solution.py:315
  217.3 2.5 %collective-permute-start.8 = (bf16[161,8,128]{2,1,0:T(8,128)(2,1)S(1)}, bf16[161,8,128]{2,1,0:T(8,128)(2,1)S(1)}, u32[]{:S(2)}, u32[]{:S(2)}) collective-permute-start(bf16[161,8,128]{2,1,0:T(8,128)(2,1)S(1)} %forward_2.1.after.mine), channel_id=1, source_target_pairs={{0,1},{1,0},{2,3},{3,2},{4,5},{5,4},{6,7},{7,6},{8,9},{9,8},{10,11... | collective-permute-start | bytes 989192 | tf_op jit(solution)/shard_map/ppermute | solution.py:407
  220.8 7.1 %collective-permute-done.8.other = bf16[161,8,128]{2,1,0:T(8,128)(2,1)S(1)} collective-permute-done((bf16[161,8,128]{2,1,0:T(8,128)(2,1)S(1)}, bf16[161,8,128]{2,1,0:T(8,128)(2,1)S(1)}, u32[]{:S(2)}, u32[]{:S(2)}) %collective-permute-start.8) | collective-permute-done | bytes 329760 | tf_op jit(solution)/shard_map/ppermute | solution.py:407
  228.4 12.8 %all_to_all.42.norms = f32[64,1,128]{2,1,0:T(1,128)S(1)} all-to-all(f32[64,1,128]{2,1,0:T(1,128)S(1)} %get-tuple-element.67), channel_id=1, replica_groups=mesh['rows'=64,'cols'=2] {'rows'}, dimensions={0} | all-to-all | bytes 65536 | tf_op jit(solution)/shard_map/all_to_all | solution.py:443
  (27 shorter events, 21.9 us)
Async XLA Ops:
  9.6 3.9 %collective-permute-start = (bf16[32,17,8,128]{3,2,1,0:T(8,128)(2,1)S(1)}, bf16[32,17,8,128]{3,2,1,0:T(8,128)(2,1)S(1)}, u32[]{:S(2)}, u32[]{:S(2)}) collective-permute-start(bf16[32,17,8,128]{3,2,1,0:T(8,128)(2,1)S(1)} %get-tuple-element.39), channel_id=1, source_target_pairs={{0,2},{2,0},{4,6},{6,4},{8,10},{10,8},{12,14},{14,12},{16,18},{18,... | collective-permute-start | bytes 3342344 | tf_op jit(solution)/shard_map/ppermute | solution.py:345
  13.7 26.7 %copy-start.1 = (f32[16,128,128]{2,1,0:T(8,128)S(1)}, f32[16,128,128]{2,1,0:T(8,128)}, u32[]{:S(2)}) copy-start(f32[16,128,128]{2,1,0:T(8,128)} %refs_0_.1) | copy-start | bytes 3145732
  41.4 24.0 %copy-start.3 = (s32[640]{0:T(1024)S(1)}, s32[640]{0:T(1024)}, u32[]{:S(2)}) copy-start(s32[640]{0:T(1024)} %column_in.1) | copy-start | bytes 7684
  41.5 26.4 %copy-start.2 = (s32[640]{0:T(1024)S(1)}, s32[640]{0:T(1024)}, u32[]{:S(2)}) copy-start(s32[640]{0:T(1024)} %row.9) | copy-start | bytes 7684
  62.9 4.9 %collective-permute-start.1 = (bf16[32,17,8,128]{3,2,1,0:T(8,128)(2,1)S(1)}, bf16[32,17,8,128]{3,2,1,0:T(8,128)(2,1)S(1)}, u32[]{:S(2)}, u32[]{:S(2)}) collective-permute-start(bf16[32,17,8,128]{3,2,1,0:T(8,128)(2,1)S(1)} %all_to_all.37), channel_id=1, source_target_pairs={{0,2},{2,0},{4,6},{6,4},{8,10},{10,8},{12,14},{14,12},{16,18},{18,... | collective-permute-start | bytes 3342344 | tf_op jit(solution)/shard_map/ppermute | solution.py:345
  72.3 10.7 %copy-start = (f32[160,8,128]{2,1,0:T(8,128)S(1)}, f32[160,8,128]{2,1,0:T(8,128)}, u32[]{:S(2)}) copy-start(f32[160,8,128]{2,1,0:T(8,128)} %before.1) | copy-start | bytes 1966084
  72.3 10.7 %collective-permute-start.2 = (bf16[161,8,128]{2,1,0:T(8,128)(2,1)S(1)}, bf16[161,8,128]{2,1,0:T(8,128)(2,1)S(1)}, u32[]{:S(2)}, u32[]{:S(2)}) collective-permute-start(bf16[161,8,128]{2,1,0:T(8,128)(2,1)S(1)} %forward_0.1.after.mine), channel_id=1, source_target_pairs={{0,1},{1,0},{2,3},{3,2},{4,5},{5,4},{6,7},{7,6},{8,9},{9,8},{10,11... | collective-permute-start | bytes 989192 | tf_op jit(solution)/shard_map/ppermute | solution.py:407
  87.9 3.7 %collective-permute-start.3 = (bf16[32,17,8,128]{3,2,1,0:T(8,128)(2,1)S(1)}, bf16[32,17,8,128]{3,2,1,0:T(8,128)(2,1)S(1)}, u32[]{:S(2)}, u32[]{:S(2)}) collective-permute-start(bf16[32,17,8,128]{3,2,1,0:T(8,128)(2,1)S(1)} %get-tuple-element.44), channel_id=1, source_target_pairs={{0,2},{2,0},{4,6},{6,4},{8,10},{10,8},{12,14},{14,12},{16,18},{18,... | collective-permute-start | bytes 3342344 | tf_op jit(solution)/shard_map/ppermute | solution.py:345
  135.4 4.9 %collective-permute-start.4 = (bf16[32,17,8,128]{3,2,1,0:T(8,128)(2,1)S(1)}, bf16[32,17,8,128]{3,2,1,0:T(8,128)(2,1)S(1)}, u32[]{:S(2)}, u32[]{:S(2)}) collective-permute-start(bf16[32,17,8,128]{3,2,1,0:T(8,128)(2,1)S(1)} %all_to_all.39), channel_id=1, source_target_pairs={{0,2},{2,0},{4,6},{6,4},{8,10},{10,8},{12,14},{14,12},{16,18},{18,... | collective-permute-start | bytes 3342344 | tf_op jit(solution)/shard_map/ppermute | solution.py:345
  144.8 10.8 %collective-permute-start.5 = (bf16[161,8,128]{2,1,0:T(8,128)(2,1)S(1)}, bf16[161,8,128]{2,1,0:T(8,128)(2,1)S(1)}, u32[]{:S(2)}, u32[]{:S(2)}) collective-permute-start(bf16[161,8,128]{2,1,0:T(8,128)(2,1)S(1)} %forward_1.1.after.mine), channel_id=1, source_target_pairs={{0,1},{1,0},{2,3},{3,2},{4,5},{5,4},{6,7},{7,6},{8,9},{9,8},{10,11... | collective-permute-start | bytes 989192 | tf_op jit(solution)/shard_map/ppermute | solution.py:407
  160.5 3.7 %collective-permute-start.6 = (bf16[32,17,8,128]{3,2,1,0:T(8,128)(2,1)S(1)}, bf16[32,17,8,128]{3,2,1,0:T(8,128)(2,1)S(1)}, u32[]{:S(2)}, u32[]{:S(2)}) collective-permute-start(bf16[32,17,8,128]{3,2,1,0:T(8,128)(2,1)S(1)} %get-tuple-element.53), channel_id=1, source_target_pairs={{0,2},{2,0},{4,6},{6,4},{8,10},{10,8},{12,14},{14,12},{16,18},{18,... | collective-permute-start | bytes 3342344 | tf_op jit(solution)/shard_map/ppermute | solution.py:345
  208.0 4.9 %collective-permute-start.7 = (bf16[32,17,8,128]{3,2,1,0:T(8,128)(2,1)S(1)}, bf16[32,17,8,128]{3,2,1,0:T(8,128)(2,1)S(1)}, u32[]{:S(2)}, u32[]{:S(2)}) collective-permute-start(bf16[32,17,8,128]{3,2,1,0:T(8,128)(2,1)S(1)} %all_to_all.41), channel_id=1, source_target_pairs={{0,2},{2,0},{4,6},{6,4},{8,10},{10,8},{12,14},{14,12},{16,18},{18,... | collective-permute-start | bytes 3342344 | tf_op jit(solution)/shard_map/ppermute | solution.py:345
  217.3 10.5 %collective-permute-start.8 = (bf16[161,8,128]{2,1,0:T(8,128)(2,1)S(1)}, bf16[161,8,128]{2,1,0:T(8,128)(2,1)S(1)}, u32[]{:S(2)}, u32[]{:S(2)}) collective-permute-start(bf16[161,8,128]{2,1,0:T(8,128)(2,1)S(1)} %forward_2.1.after.mine), channel_id=1, source_target_pairs={{0,1},{1,0},{2,3},{3,2},{4,5},{5,4},{6,7},{7,6},{8,9},{9,8},{10,11... | collective-permute-start | bytes 989192 | tf_op jit(solution)/shard_map/ppermute | solution.py:407

commit v5 on v4

--- a/solution.py
+++ b/solution.py
@@ -50,7 +50,7 @@
     return next(u for u in (640, 320, 160, 128, 64, 32, 16, 8, 4, 2) if u <= most and count % u == 0)
 
 
-def accumulate(products, source, target, table, get, total, first, count, most=640, arrive=None, also=None):
+def accumulate(products, pick, target, get, total, first, count, most=640, arrive=None, also=None):
     if count == 0:
         return
     unroll = unroll_of(count, most)
@@ -66,7 +66,7 @@
             arrive(first // unroll + i)
         pending = []
         for u in range(0, unroll, 2):
-            pair = jnp.concatenate([table[source(base + u)], table[source(base + u + 1)]], axis=0)
+            pair = jnp.concatenate([pick(base + u), pick(base + u + 1)], axis=0)
             if also is not None:
                 also(base + u)
                 also(base + u + 1)
@@ -90,22 +90,21 @@
     return both[:half], both[half:]
 
 
-def finish_sums(here, row_term, kept, sent, total):
-    half = kept.shape[0] * kept.shape[1]
-    kept[...] = total[:half].astype(BF16).reshape(kept.shape)
+def finish_sums(here, row_term, sent, total):
+    half = sent.shape[0] * sent.shape[1]
     sent[...] = total[half:].astype(BF16).reshape(sent.shape)
     norm = pack(squares(row_term[...]), 3 * here[0])
-    last = kept.shape[1] - 1
-    for chip in range(kept.shape[0]):
-        kept[chip, last] = norm
-        sent[chip, last] = norm
-
-
-def send_sums(here, row, spot, row_term, blocks, kept, sent, total):
+    step = sent.shape[1]
+    for chip in range(sent.shape[0]):
+        total[chip * step + step - 1] = norm.astype(F32)
+        sent[chip, step - 1] = norm
+
+
+def send_sums(here, row, spot, row_term, blocks, total, sent):
     total[...] = jnp.zeros_like(total)
     get = lambda n: blocks[pl.ds(n, 2)]
-    accumulate(block_pair, lambda n: row[n], lambda n: spot[n], row_term, get, total, 0, row.shape[0])
-    finish_sums(here, row_term, kept, sent, total)
+    accumulate(block_pair, lambda n: row_term[row[n]], lambda n: spot[n], get, total, 0, row.shape[0])
+    finish_sums(here, row_term, sent, total)
 
 
 def load_kernel(blocks, after, loaded, done):
@@ -126,11 +125,11 @@
     return ((owner & 1) ^ core) * half + (owner >> 1) * (own + 1) + column % own
 
 
-def first_kernel(own, here, row_in, column_in, right_sides, blocks, kept, sent, stored, total, rest, table, row, column, done):
+def first_kernel(own, here, row_in, column_in, right_sides, blocks, total, sent, stored, rest, table, row, column, done):
     whole = blocks.shape[0]
     plain = stored.shape[0] - whole
     count = part_of(whole, plain)
-    half = kept.shape[0] * kept.shape[1]
+    half = sent.shape[0] * sent.shape[1]
     core = here[0]
     shift = own.bit_length() - 1
 
@@ -180,21 +179,22 @@
             return ref[pl.ds(shifted + n, 2)]
 
         accumulate(
-            block_pair, lambda n: row[n], spot, table, get, total, first, until - first, count, arrive, turn
+            block_pair, lambda n: table[row[n]], spot, get, total, first, until - first, count, arrive, turn
         )
-    finish_sums(here, table, kept, sent, total)
+    finish_sums(here, table, sent, total)
 
 
 def place_kernel(own, half, here, column, spot):
     spot[...] = place(column[...], here[0], own, half)
 
 
-def add_kernel(kept, arrived, both):
-    both[...] = (kept[...].astype(F32) + arrived[...].astype(F32)).astype(BF16)
-
-
-def dead_kernel(here, row, spot, row_term, blocks, kept, sent, total):
-    send_sums(here, row, spot, row_term, blocks, kept, sent, total)
+def add_kernel(total, arrived, both):
+    half = both.shape[0] * both.shape[1]
+    both[...] = (total[:half].reshape(both.shape) + arrived[...].astype(F32)).astype(BF16)
+
+
+def dead_kernel(here, row, spot, row_term, blocks, total, sent):
+    send_sums(here, row, spot, row_term, blocks, total, sent)
 
 
 def new_row_term(mine, other, before, beta, row_term, alpha):
@@ -205,9 +205,9 @@
     row_term[...] = product * (1.0 / alpha[...])[None] - before[...] * (alpha[...] / beta[...])[None]
 
 
-def back_kernel(here, row, spot, mine, other, before, beta, blocks, row_term, alpha, kept, sent, total):
+def back_kernel(here, row, spot, mine, other, before, beta, blocks, row_term, alpha, total, sent):
     new_row_term(mine, other, before, beta, row_term, alpha)
-    send_sums(here, row, spot, row_term, blocks, kept, sent, total)
+    send_sums(here, row, spot, row_term, blocks, total, sent)
 
 
 def diagonal(count):
@@ -222,18 +222,22 @@
     norms[...] = jnp.broadcast_to(flat[None], norms.shape)
 
 
-def forward_kernel(step, row, spot, mine, other, stored, product, table, total):
+def forward_kernel(step, row, spot, mine, other, stored, product, total):
     half = mine.shape[0]
-    table[:half] = mine[...].astype(F32)
-    table[half:] = other[...].astype(F32)
     total[...] = jnp.zeros_like(total)
-    rows, spots = lambda n: row[n], lambda n: spot[n]
-    accumulate(block_pair, spots, rows, table, lambda n: stored[pl.ds(n, 2)], total, 0, row.shape[0])
+
+    def pick(n):
+        at = spot[n]
+        near = mine[jnp.minimum(at, half - 1)].astype(F32)
+        far = other[jnp.maximum(at - half, 0)].astype(F32)
+        return jnp.where(at < half, near, far)
+
+    accumulate(block_pair, pick, lambda n: row[n], lambda n: stored[pl.ds(n, 2)], total, 0, row.shape[0])
     count = total.shape[0]
     product[:count] = total[...].astype(BF16)
     norm = jnp.zeros(total.shape[1:], F32)
     for last in range(step - 1, half, step):
-        norm = norm + table[last] + table[half + last]
+        norm = norm + mine[last].astype(F32) + other[last].astype(F32)
     product[count] = pack(unpack(norm), 0)
 
 
@@ -348,21 +352,20 @@
     norm = like((rhs, size))
     field = like((own, rhs, size))
     row_field = like((rows, rhs, size))
-    total = pltpu.VMEM((2 * half, rhs, size), F32)
-
-    def scatter(kept, sent):
-        return exchange(call(add_kernel, part, (kept, core_swap(sent)), name="add_cores"))
+    sums = like((2 * half, rhs, size))
+
+    def scatter(total, sent):
+        return exchange(call(add_kernel, part, (total, core_swap(sent)), name="add_cores"))
 
     in_hbm = [pltpu.with_memory_space_constraint(a, pltpu.HBM) for a in (block_row, block_col, right_sides, blocks)]
     count = blocks.shape[0]
     plain = count * PLAIN[0] // PLAIN[1] // 2 * 2
-    kept, sent, stored = call(
+    total, sent, stored = call(
         functools.partial(first_kernel, own),
-        [part, part, pltpu.VMEM((count + plain,) + blocks.shape[1:], BF16)],
+        [sums, part, pltpu.VMEM((count + plain,) + blocks.shape[1:], BF16)],
         (here, *in_hbm),
         1,
         [
-            total,
             pltpu.VMEM((count - plain,) + blocks.shape[1:], BF16),
             pltpu.VMEM((rows, rhs, size), F32),
             pltpu.SMEM(block_row.shape, jnp.int32),
@@ -378,7 +381,7 @@
     col_term = alpha = beta = None
     state = []
     for sweep in range(ITERS + 1):
-        chunks = scatter(kept, sent)
+        chunks = scatter(total, sent)
         carried = [precond] if sweep == 0 else [high, low, col_term, alpha, beta] + state
         new = call(
             functools.partial(column_kernel, sweep),
@@ -401,7 +404,7 @@
             like((rows + 1, rhs, size), BF16),
             (block_row, spot, mine.reshape(flat), other.reshape(flat), stored),
             2,
-            [pltpu.VMEM((2 * half, rhs, size), F32), pltpu.VMEM((rows, rhs, size), F32)],
+            [pltpu.VMEM((rows, rhs, size), F32)],
             f"forward_{sweep}",
         )
         crossed = lax.ppermute(product, "cols", [(0, 1), (1, 0)])
@@ -418,12 +421,12 @@
         )
         loaded = pltpu.with_memory_space_constraint(loaded, pltpu.VMEM)
         if sweep < ITERS - 1:
-            row_term, alpha, kept, sent = call(
+            row_term, alpha, total, sent = call(
                 back_kernel,
-                [row_field, norm, part, part],
+                [row_field, norm, sums, part],
                 (here, block_row, spot, product, crossed, row_term, beta, loaded),
                 3,
-                [total],
+                (),
                 f"backward_{sweep}",
             )
         else:
@@ -437,8 +440,8 @@
                 name="finish_rows",
             )
             factors = (alpha, beta, rhobar, phibar)
-            kept, sent = call(
-                dead_kernel, [part, part], (here, block_row, spot, row_term, loaded), 3, [total], "last_backward"
+            total, sent = call(
+                dead_kernel, [sums, part], (here, block_row, spot, row_term, loaded), 3, (), "last_backward"
             )
     norms = lax.all_to_all(norms, "rows", 0, 0, tiled=True)
     return call(last_kernel, [field, row_field], (norms, row_term, *ready, *factors), name="last")

time: 243 us -> 242 us (level)
  no operation moved by 1% of the time
where the time goes in v5:
time: 242 us
  blocking collectives  146 us (60%)
  Pallas kernels  52.2 us (22%)
  waiting for transfers between devices  23.2 us (10%)
  starting transfers between devices  19.6 us (8%)
    all_to_all x6, blocking collectives, exchange(): lax.all_to_all(parts, 'rows', 0, 0, axis_index_groups=same_core, tiled=True)  133 us
    pallas_call x18, Pallas kernels, call(): pl.pallas_call(kernel, out_shape=out_shape, in_specs=[SM] * scalars + [pl...  52.2 us
    ppermute x6, waiting for transfers between devices, core_swap(): return lax.ppermute(array, 'rows', swap)  14.3 us
    all_to_all x1, blocking collectives, shards(): norms = lax.all_to_all(norms, 'rows', 0, 0, tiled=True)  12.8 us
    ppermute x6, starting transfers between devices, core_swap(): return lax.ppermute(array, 'rows', swap)  11.6 us
    ppermute x3, waiting for transfers between devices, shards(): crossed = lax.ppermute(product, 'cols', [(0, 1), (1, 0)])  8.94 us
    ppermute x3, starting transfers between devices, shards(): crossed = lax.ppermute(product, 'cols', [(0, 1), (1, 0)])  8 us
  transfers between devices with their start and end apart: 9, of which 9 were waited for; matrix products, arithmetic and copies ran while one was open for 0% of the time, Pallas kernels for 6%

profile of v5, /device:TPU:1, one launch (start us, length us, event | category | flops | bytes accessed | tf_op | source)
XLA Modules:
  0.0 241.7 jit_solution(10530094464592000222)
XLA Ops:
  0.6 8.9 %first_backward.1 = (f32[1088,8,128]{2,1,0:T(8,128)S(1)}, bf16[32,17,8,128]{3,2,1,0:T(8,128)(2,1)S(1)}, bf16[640,128,128]{2,1,0:T(8,128)(2,1)S(1)}) custom-call(s32[1]{0:T(128)} %bitcast.here, s32[640]{0:T(1024)} %row.9, s32[640]{0:T(1024)} %column_in.1, f32[160,8,128]{2,1,0:T(8,128)} %before.1, bf16[640,128,128]{2,1,0:T(8,128)(2,1)} %blocks.5), custom_call_target="tpu_custom_call" | custom-call | tf_op jit(solution)/shard_map/first_backward/pallas_call | solution.py:319
  11.0 2.4 collective-permute-done.arrived
  13.6 26.6 %all_to_all.36.chunks = bf16[32,17,8,128]{3,2,1,0:T(8,128)(2,1)S(1)} all-to-all(bf16[32,17,8,128]{3,2,1,0:T(8,128)(2,1)S(1)} %add_cores.3), channel_id=1, replica_groups={{0,4,8,12,16,20,24,28,32,36,40,44,48,52,56,60,64,68,72,76,80,84,88,92,9..., dimensions={0} | all-to-all | bytes 2228224 | tf_op jit(solution)/shard_map/all_to_all | solution.py:346
  41.3 21.5 %all_to_all.37 = bf16[32,17,8,128]{3,2,1,0:T(8,128)(2,1)S(1)} all-to-all(bf16[32,17,8,128]{3,2,1,0:T(8,128)(2,1)S(1)} %get-tuple-element.40), channel_id=1, replica_groups={{0,4,8,12,16,20,24,28,32,36,40,44,48,52,56,60,64,68,72,76,80,84,88,92,9..., dimensions={0} | all-to-all | bytes 2228224 | tf_op jit(solution)/shard_map/all_to_all | solution.py:346
  62.8 2.5 %collective-permute-start.1 = (bf16[32,17,8,128]{3,2,1,0:T(8,128)(2,1)S(1)}, bf16[32,17,8,128]{3,2,1,0:T(8,128)(2,1)S(1)}, u32[]{:S(2)}, u32[]{:S(2)}) collective-permute-start(bf16[32,17,8,128]{3,2,1,0:T(8,128)(2,1)S(1)} %all_to_all.37), channel_id=1, source_target_pairs={{0,2},{2,0},{4,6},{6,4},{8,10},{10,8},{12,14},{14,12},{16,18},{18,... | collective-permute-start | bytes 3342344 | tf_op jit(solution)/shard_map/ppermute | solution.py:349
  67.7 4.4 %forward_0.1.after.mine = bf16[161,8,128]{2,1,0:T(8,128)(2,1)S(1)} custom-call(s32[640]{0:T(1024)S(1)} %copy-done.2, s32[640]{0:T(1024)S(1)} %place.1.spot, bf16[544,8,128]{2,1,0:T(8,128)(2,1)S(1)} %bitcast.7, bf16[544,8,128]{2,1,0:T(8,128)(2,1)S(1)} %bitcast.10, bf16[640,128,128]{2,1,0:T(8,128)(2,1)S(1)} %get-tuple-element.41.stored), custom_call_target="tpu_custom_call" | custom-call | tf_op jit(solution)/shard_map/forward_0/pallas_call | solution.py:319
  72.1 2.7 %collective-permute-start.2 = (bf16[161,8,128]{2,1,0:T(8,128)(2,1)S(1)}, bf16[161,8,128]{2,1,0:T(8,128)(2,1)S(1)}, u32[]{:S(2)}, u32[]{:S(2)}) collective-permute-start(bf16[161,8,128]{2,1,0:T(8,128)(2,1)S(1)} %forward_0.1.after.mine), channel_id=1, source_target_pairs={{0,1},{1,0},{2,3},{3,2},{4,5},{5,4},{6,7},{7,6},{8,9},{9,8},{10,11... | collective-permute-start | bytes 989192 | tf_op jit(solution)/shard_map/ppermute | solution.py:410
  74.8 7.1 %load_0.1.blocks = bf16[640,128,128]{2,1,0:T(8,128)(2,1)S(1)} custom-call(bf16[640,128,128]{2,1,0:T(8,128)(2,1)} %blocks.5, bf16[161,8,128]{2,1,0:T(8,128)(2,1)S(1)} %forward_0.1.after.mine), custom_call_target="tpu_custom_call" | custom-call | bytes 41943040 | tf_op jit(solution)/shard_map/load_0/pallas_call | solution.py:319
  82.9 4.8 %backward_0.1 = (f32[160,8,128]{2,1,0:T(8,128)S(1)}, f32[8,128]{1,0:T(8,128)S(1)}, f32[1088,8,128]{2,1,0:T(8,128)S(1)}, bf16[32,17,8,128]{3,2,1,0:T(8,128)(2,1)S(1)}) custom-call(s32[1]{0:T(128)} %bitcast.here, s32[640]{0:T(1024)S(1)} %copy-done.2, s32[640]{0:T(1024)S(1)} %place.1.spot, bf16[161,8,128]{2,1,0:T(8,128)(2,1)S(1)} %forward_0.1.after.mine, ...), custom_call_target="tpu_custom_call" | custom-call | tf_op jit(solution)/shard_map/backward_0/pallas_call | solution.py:319
  91.5 21.1 %all_to_all.38.chunks = bf16[32,17,8,128]{3,2,1,0:T(8,128)(2,1)S(1)} all-to-all(bf16[32,17,8,128]{3,2,1,0:T(8,128)(2,1)S(1)} %add_cores.4), channel_id=1, replica_groups={{0,4,8,12,16,20,24,28,32,36,40,44,48,52,56,60,64,68,72,76,80,84,88,92,9..., dimensions={0} | all-to-all | bytes 2228224 | tf_op jit(solution)/shard_map/all_to_all | solution.py:346
  113.6 21.5 %all_to_all.39 = bf16[32,17,8,128]{3,2,1,0:T(8,128)(2,1)S(1)} all-to-all(bf16[32,17,8,128]{3,2,1,0:T(8,128)(2,1)S(1)} %get-tuple-element.49), channel_id=1, replica_groups={{0,4,8,12,16,20,24,28,32,36,40,44,48,52,56,60,64,68,72,76,80,84,88,92,9..., dimensions={0} | all-to-all | bytes 2228224 | tf_op jit(solution)/shard_map/all_to_all | solution.py:346
  135.1 2.5 %collective-permute-start.4 = (bf16[32,17,8,128]{3,2,1,0:T(8,128)(2,1)S(1)}, bf16[32,17,8,128]{3,2,1,0:T(8,128)(2,1)S(1)}, u32[]{:S(2)}, u32[]{:S(2)}) collective-permute-start(bf16[32,17,8,128]{3,2,1,0:T(8,128)(2,1)S(1)} %all_to_all.39), channel_id=1, source_target_pairs={{0,2},{2,0},{4,6},{6,4},{8,10},{10,8},{12,14},{14,12},{16,18},{18,... | collective-permute-start | bytes 3342344 | tf_op jit(solution)/shard_map/ppermute | solution.py:349
  137.6 2.4 collective-permute-done.4
  140.0 4.4 %forward_1.1.after.mine = bf16[161,8,128]{2,1,0:T(8,128)(2,1)S(1)} custom-call(s32[640]{0:T(1024)S(1)} %copy-done.2, s32[640]{0:T(1024)S(1)} %place.1.spot, bf16[544,8,128]{2,1,0:T(8,128)(2,1)S(1)} %bitcast.9, bf16[544,8,128]{2,1,0:T(8,128)(2,1)S(1)} %bitcast.12, bf16[640,128,128]{2,1,0:T(8,128)(2,1)S(1)} %get-tuple-element.41.stored), custom_call_target="tpu_custom_call" | custom-call | tf_op jit(solution)/shard_map/forward_1/pallas_call | solution.py:319
  144.4 2.8 %collective-permute-start.5 = (bf16[161,8,128]{2,1,0:T(8,128)(2,1)S(1)}, bf16[161,8,128]{2,1,0:T(8,128)(2,1)S(1)}, u32[]{:S(2)}, u32[]{:S(2)}) collective-permute-start(bf16[161,8,128]{2,1,0:T(8,128)(2,1)S(1)} %forward_1.1.after.mine), channel_id=1, source_target_pairs={{0,1},{1,0},{2,3},{3,2},{4,5},{5,4},{6,7},{7,6},{8,9},{9,8},{10,11... | collective-permute-start | bytes 989192 | tf_op jit(solution)/shard_map/ppermute | solution.py:410
  147.1 7.1 %load_1.1.blocks = bf16[640,128,128]{2,1,0:T(8,128)(2,1)S(1)} custom-call(bf16[640,128,128]{2,1,0:T(8,128)(2,1)} %blocks.5, bf16[161,8,128]{2,1,0:T(8,128)(2,1)S(1)} %forward_1.1.after.mine), custom_call_target="tpu_custom_call" | custom-call | bytes 41943040 | tf_op jit(solution)/shard_map/load_1/pallas_call | solution.py:319
  155.2 4.8 %backward_1.1 = (f32[160,8,128]{2,1,0:T(8,128)S(1)}, f32[8,128]{1,0:T(8,128)S(1)}, f32[1088,8,128]{2,1,0:T(8,128)S(1)}, bf16[32,17,8,128]{3,2,1,0:T(8,128)(2,1)S(1)}) custom-call(s32[1]{0:T(128)} %bitcast.here, s32[640]{0:T(1024)S(1)} %copy-done.2, s32[640]{0:T(1024)S(1)} %place.1.spot, bf16[161,8,128]{2,1,0:T(8,128)(2,1)S(1)} %forward_1.1.after.mine, ...), custom_call_target="tpu_custom_call" | custom-call | tf_op jit(solution)/shard_map/backward_1/pallas_call | solution.py:319
  163.8 21.1 %all_to_all.40.chunks = bf16[32,17,8,128]{3,2,1,0:T(8,128)(2,1)S(1)} all-to-all(bf16[32,17,8,128]{3,2,1,0:T(8,128)(2,1)S(1)} %add_cores.5), channel_id=1, replica_groups={{0,4,8,12,16,20,24,28,32,36,40,44,48,52,56,60,64,68,72,76,80,84,88,92,9..., dimensions={0} | all-to-all | bytes 2228224 | tf_op jit(solution)/shard_map/all_to_all | solution.py:346
  185.9 21.5 %all_to_all.41 = bf16[32,17,8,128]{3,2,1,0:T(8,128)(2,1)S(1)} all-to-all(bf16[32,17,8,128]{3,2,1,0:T(8,128)(2,1)S(1)} %get-tuple-element.60), channel_id=1, replica_groups={{0,4,8,12,16,20,24,28,32,36,40,44,48,52,56,60,64,68,72,76,80,84,88,92,9..., dimensions={0} | all-to-all | bytes 2228224 | tf_op jit(solution)/shard_map/all_to_all | solution.py:346
  207.4 2.5 %collective-permute-start.7 = (bf16[32,17,8,128]{3,2,1,0:T(8,128)(2,1)S(1)}, bf16[32,17,8,128]{3,2,1,0:T(8,128)(2,1)S(1)}, u32[]{:S(2)}, u32[]{:S(2)}) collective-permute-start(bf16[32,17,8,128]{3,2,1,0:T(8,128)(2,1)S(1)} %all_to_all.41), channel_id=1, source_target_pairs={{0,2},{2,0},{4,6},{6,4},{8,10},{10,8},{12,14},{14,12},{16,18},{18,... | collective-permute-start | bytes 3342344 | tf_op jit(solution)/shard_map/ppermute | solution.py:349
  212.3 4.4 %forward_2.1.after.mine = bf16[161,8,128]{2,1,0:T(8,128)(2,1)S(1)} custom-call(s32[640]{0:T(1024)S(1)} %copy-done.2, s32[640]{0:T(1024)S(1)} %place.1.spot, bf16[544,8,128]{2,1,0:T(8,128)(2,1)S(1)} %bitcast.8, bf16[544,8,128]{2,1,0:T(8,128)(2,1)S(1)} %bitcast.11, bf16[640,128,128]{2,1,0:T(8,128)(2,1)S(1)} %get-tuple-element.41.stored), custom_call_target="tpu_custom_call" | custom-call | tf_op jit(solution)/shard_map/forward_2/pallas_call | solution.py:319
  216.7 2.5 %collective-permute-start.8 = (bf16[161,8,128]{2,1,0:T(8,128)(2,1)S(1)}, bf16[161,8,128]{2,1,0:T(8,128)(2,1)S(1)}, u32[]{:S(2)}, u32[]{:S(2)}) collective-permute-start(bf16[161,8,128]{2,1,0:T(8,128)(2,1)S(1)} %forward_2.1.after.mine), channel_id=1, source_target_pairs={{0,1},{1,0},{2,3},{3,2},{4,5},{5,4},{6,7},{7,6},{8,9},{9,8},{10,11... | collective-permute-start | bytes 989192 | tf_op jit(solution)/shard_map/ppermute | solution.py:410
  220.1 7.1 %collective-permute-done.8.other = bf16[161,8,128]{2,1,0:T(8,128)(2,1)S(1)} collective-permute-done((bf16[161,8,128]{2,1,0:T(8,128)(2,1)S(1)}, bf16[161,8,128]{2,1,0:T(8,128)(2,1)S(1)}, u32[]{:S(2)}, u32[]{:S(2)}) %collective-permute-start.8) | collective-permute-done | bytes 329760 | tf_op jit(solution)/shard_map/ppermute | solution.py:410
  227.8 12.8 %all_to_all.42.norms = f32[64,1,128]{2,1,0:T(1,128)S(1)} all-to-all(f32[64,1,128]{2,1,0:T(1,128)S(1)} %get-tuple-element.67), channel_id=1, replica_groups=mesh['rows'=64,'cols'=2] {'rows'}, dimensions={0} | all-to-all | bytes 65536 | tf_op jit(solution)/shard_map/all_to_all | solution.py:446
  (27 shorter events, 21.6 us)
Async XLA Ops:
  9.5 3.9 %collective-permute-start = (bf16[32,17,8,128]{3,2,1,0:T(8,128)(2,1)S(1)}, bf16[32,17,8,128]{3,2,1,0:T(8,128)(2,1)S(1)}, u32[]{:S(2)}, u32[]{:S(2)}) collective-permute-start(bf16[32,17,8,128]{3,2,1,0:T(8,128)(2,1)S(1)} %get-tuple-element.39), channel_id=1, source_target_pairs={{0,2},{2,0},{4,6},{6,4},{8,10},{10,8},{12,14},{14,12},{16,18},{18,... | collective-permute-start | bytes 3342344 | tf_op jit(solution)/shard_map/ppermute | solution.py:349
  13.6 26.7 %copy-start.1 = (f32[16,128,128]{2,1,0:T(8,128)S(1)}, f32[16,128,128]{2,1,0:T(8,128)}, u32[]{:S(2)}) copy-start(f32[16,128,128]{2,1,0:T(8,128)} %refs_0_.1) | copy-start | bytes 3145732
  41.3 24.0 %copy-start.3 = (s32[640]{0:T(1024)S(1)}, s32[640]{0:T(1024)}, u32[]{:S(2)}) copy-start(s32[640]{0:T(1024)} %column_in.1) | copy-start | bytes 7684
  41.3 26.4 %copy-start.2 = (s32[640]{0:T(1024)S(1)}, s32[640]{0:T(1024)}, u32[]{:S(2)}) copy-start(s32[640]{0:T(1024)} %row.9) | copy-start | bytes 7684
  62.8 4.9 %collective-permute-start.1 = (bf16[32,17,8,128]{3,2,1,0:T(8,128)(2,1)S(1)}, bf16[32,17,8,128]{3,2,1,0:T(8,128)(2,1)S(1)}, u32[]{:S(2)}, u32[]{:S(2)}) collective-permute-start(bf16[32,17,8,128]{3,2,1,0:T(8,128)(2,1)S(1)} %all_to_all.37), channel_id=1, source_target_pairs={{0,2},{2,0},{4,6},{6,4},{8,10},{10,8},{12,14},{14,12},{16,18},{18,... | collective-permute-start | bytes 3342344 | tf_op jit(solution)/shard_map/ppermute | solution.py:349
  72.1 10.8 %copy-start = (f32[160,8,128]{2,1,0:T(8,128)S(1)}, f32[160,8,128]{2,1,0:T(8,128)}, u32[]{:S(2)}) copy-start(f32[160,8,128]{2,1,0:T(8,128)} %before.1) | copy-start | bytes 1966084
  72.1 10.7 %collective-permute-start.2 = (bf16[161,8,128]{2,1,0:T(8,128)(2,1)S(1)}, bf16[161,8,128]{2,1,0:T(8,128)(2,1)S(1)}, u32[]{:S(2)}, u32[]{:S(2)}) collective-permute-start(bf16[161,8,128]{2,1,0:T(8,128)(2,1)S(1)} %forward_0.1.after.mine), channel_id=1, source_target_pairs={{0,1},{1,0},{2,3},{3,2},{4,5},{5,4},{6,7},{7,6},{8,9},{9,8},{10,11... | collective-permute-start | bytes 989192 | tf_op jit(solution)/shard_map/ppermute | solution.py:410
  87.7 3.6 %collective-permute-start.3 = (bf16[32,17,8,128]{3,2,1,0:T(8,128)(2,1)S(1)}, bf16[32,17,8,128]{3,2,1,0:T(8,128)(2,1)S(1)}, u32[]{:S(2)}, u32[]{:S(2)}) collective-permute-start(bf16[32,17,8,128]{3,2,1,0:T(8,128)(2,1)S(1)} %get-tuple-element.44), channel_id=1, source_target_pairs={{0,2},{2,0},{4,6},{6,4},{8,10},{10,8},{12,14},{14,12},{16,18},{18,... | collective-permute-start | bytes 3342344 | tf_op jit(solution)/shard_map/ppermute | solution.py:349
  135.1 4.9 %collective-permute-start.4 = (bf16[32,17,8,128]{3,2,1,0:T(8,128)(2,1)S(1)}, bf16[32,17,8,128]{3,2,1,0:T(8,128)(2,1)S(1)}, u32[]{:S(2)}, u32[]{:S(2)}) collective-permute-start(bf16[32,17,8,128]{3,2,1,0:T(8,128)(2,1)S(1)} %all_to_all.39), channel_id=1, source_target_pairs={{0,2},{2,0},{4,6},{6,4},{8,10},{10,8},{12,14},{14,12},{16,18},{18,... | collective-permute-start | bytes 3342344 | tf_op jit(solution)/shard_map/ppermute | solution.py:349
  144.4 10.8 %collective-permute-start.5 = (bf16[161,8,128]{2,1,0:T(8,128)(2,1)S(1)}, bf16[161,8,128]{2,1,0:T(8,128)(2,1)S(1)}, u32[]{:S(2)}, u32[]{:S(2)}) collective-permute-start(bf16[161,8,128]{2,1,0:T(8,128)(2,1)S(1)} %forward_1.1.after.mine), channel_id=1, source_target_pairs={{0,1},{1,0},{2,3},{3,2},{4,5},{5,4},{6,7},{7,6},{8,9},{9,8},{10,11... | collective-permute-start | bytes 989192 | tf_op jit(solution)/shard_map/ppermute | solution.py:410
  160.0 3.6 %collective-permute-start.6 = (bf16[32,17,8,128]{3,2,1,0:T(8,128)(2,1)S(1)}, bf16[32,17,8,128]{3,2,1,0:T(8,128)(2,1)S(1)}, u32[]{:S(2)}, u32[]{:S(2)}) collective-permute-start(bf16[32,17,8,128]{3,2,1,0:T(8,128)(2,1)S(1)} %get-tuple-element.53), channel_id=1, source_target_pairs={{0,2},{2,0},{4,6},{6,4},{8,10},{10,8},{12,14},{14,12},{16,18},{18,... | collective-permute-start | bytes 3342344 | tf_op jit(solution)/shard_map/ppermute | solution.py:349
  207.4 4.9 %collective-permute-start.7 = (bf16[32,17,8,128]{3,2,1,0:T(8,128)(2,1)S(1)}, bf16[32,17,8,128]{3,2,1,0:T(8,128)(2,1)S(1)}, u32[]{:S(2)}, u32[]{:S(2)}) collective-permute-start(bf16[32,17,8,128]{3,2,1,0:T(8,128)(2,1)S(1)} %all_to_all.41), channel_id=1, source_target_pairs={{0,2},{2,0},{4,6},{6,4},{8,10},{10,8},{12,14},{14,12},{16,18},{18,... | collective-permute-start | bytes 3342344 | tf_op jit(solution)/shard_map/ppermute | solution.py:349
  216.7 10.6 %collective-permute-start.8 = (bf16[161,8,128]{2,1,0:T(8,128)(2,1)S(1)}, bf16[161,8,128]{2,1,0:T(8,128)(2,1)S(1)}, u32[]{:S(2)}, u32[]{:S(2)}) collective-permute-start(bf16[161,8,128]{2,1,0:T(8,128)(2,1)S(1)} %forward_2.1.after.mine), channel_id=1, source_target_pairs={{0,1},{1,0},{2,3},{3,2},{4,5},{5,4},{6,7},{7,6},{8,9},{9,8},{10,11... | collective-permute-start | bytes 989192 | tf_op jit(solution)/shard_map/ppermute | solution.py:410

commit v6 on v5

--- a/solution.py
+++ b/solution.py
@@ -16,7 +16,7 @@
 VM = pl.BlockSpec(memory_space=pltpu.VMEM)
 SM = pl.BlockSpec(memory_space=pltpu.SMEM)
 LATE = 16
-AHEAD = 3
+AHEAD = 5
 PLAIN = (0, 1)
 
 

time: 242 us -> 242 us (level)
  no operation moved by 1% of the time
where the time goes in v6:
time: 242 us
  blocking collectives  146 us (60%)
  Pallas kernels  52 us (21%)
  waiting for transfers between devices  23.2 us (10%)
  starting transfers between devices  19.6 us (8%)
    all_to_all x6, blocking collectives, exchange(): lax.all_to_all(parts, 'rows', 0, 0, axis_index_groups=same_core, tiled=True)  133 us
    pallas_call x18, Pallas kernels, call(): pl.pallas_call(kernel, out_shape=out_shape, in_specs=[SM] * scalars + [pl...  52 us
    ppermute x6, waiting for transfers between devices, core_swap(): return lax.ppermute(array, 'rows', swap)  14.3 us
    all_to_all x1, blocking collectives, shards(): norms = lax.all_to_all(norms, 'rows', 0, 0, tiled=True)  12.8 us
    ppermute x6, starting transfers between devices, core_swap(): return lax.ppermute(array, 'rows', swap)  11.6 us
    ppermute x3, waiting for transfers between devices, shards(): crossed = lax.ppermute(product, 'cols', [(0, 1), (1, 0)])  8.91 us
    ppermute x3, starting transfers between devices, shards(): crossed = lax.ppermute(product, 'cols', [(0, 1), (1, 0)])  7.99 us
  transfers between devices with their start and end apart: 9, of which 9 were waited for; matrix products, arithmetic and copies ran while one was open for 0% of the time, Pallas kernels for 6%

profile of v6, /device:TPU:1, one launch (start us, length us, event | category | flops | bytes accessed | tf_op | source)
XLA Modules:
  0.0 241.6 jit_solution(14250675348659355158)
XLA Ops:
  0.6 8.8 %first_backward.1 = (f32[1088,8,128]{2,1,0:T(8,128)S(1)}, bf16[32,17,8,128]{3,2,1,0:T(8,128)(2,1)S(1)}, bf16[640,128,128]{2,1,0:T(8,128)(2,1)S(1)}) custom-call(s32[1]{0:T(128)} %bitcast.here, s32[640]{0:T(1024)} %row.9, s32[640]{0:T(1024)} %column_in.1, f32[160,8,128]{2,1,0:T(8,128)} %before.1, bf16[640,128,128]{2,1,0:T(8,128)(2,1)} %blocks.5), custom_call_target="tpu_custom_call" | custom-call | tf_op jit(solution)/shard_map/first_backward/pallas_call | solution.py:319
  10.9 2.4 collective-permute-done.arrived
  13.5 26.7 %all_to_all.36.chunks = bf16[32,17,8,128]{3,2,1,0:T(8,128)(2,1)S(1)} all-to-all(bf16[32,17,8,128]{3,2,1,0:T(8,128)(2,1)S(1)} %add_cores.3), channel_id=1, replica_groups={{0,4,8,12,16,20,24,28,32,36,40,44,48,52,56,60,64,68,72,76,80,84,88,92,9..., dimensions={0} | all-to-all | bytes 2228224 | tf_op jit(solution)/shard_map/all_to_all | solution.py:346
  41.3 21.5 %all_to_all.37 = bf16[32,17,8,128]{3,2,1,0:T(8,128)(2,1)S(1)} all-to-all(bf16[32,17,8,128]{3,2,1,0:T(8,128)(2,1)S(1)} %get-tuple-element.40), channel_id=1, replica_groups={{0,4,8,12,16,20,24,28,32,36,40,44,48,52,56,60,64,68,72,76,80,84,88,92,9..., dimensions={0} | all-to-all | bytes 2228224 | tf_op jit(solution)/shard_map/all_to_all | solution.py:346
  62.7 2.5 %collective-permute-start.1 = (bf16[32,17,8,128]{3,2,1,0:T(8,128)(2,1)S(1)}, bf16[32,17,8,128]{3,2,1,0:T(8,128)(2,1)S(1)}, u32[]{:S(2)}, u32[]{:S(2)}) collective-permute-start(bf16[32,17,8,128]{3,2,1,0:T(8,128)(2,1)S(1)} %all_to_all.37), channel_id=1, source_target_pairs={{0,2},{2,0},{4,6},{6,4},{8,10},{10,8},{12,14},{14,12},{16,18},{18,... | collective-permute-start | bytes 3342344 | tf_op jit(solution)/shard_map/ppermute | solution.py:349
  67.6 4.4 %forward_0.1.after.mine = bf16[161,8,128]{2,1,0:T(8,128)(2,1)S(1)} custom-call(s32[640]{0:T(1024)S(1)} %copy-done.2, s32[640]{0:T(1024)S(1)} %place.1.spot, bf16[544,8,128]{2,1,0:T(8,128)(2,1)S(1)} %bitcast.7, bf16[544,8,128]{2,1,0:T(8,128)(2,1)S(1)} %bitcast.10, bf16[640,128,128]{2,1,0:T(8,128)(2,1)S(1)} %get-tuple-element.41.stored), custom_call_target="tpu_custom_call" | custom-call | tf_op jit(solution)/shard_map/forward_0/pallas_call | solution.py:319
  72.0 2.7 %collective-permute-start.2 = (bf16[161,8,128]{2,1,0:T(8,128)(2,1)S(1)}, bf16[161,8,128]{2,1,0:T(8,128)(2,1)S(1)}, u32[]{:S(2)}, u32[]{:S(2)}) collective-permute-start(bf16[161,8,128]{2,1,0:T(8,128)(2,1)S(1)} %forward_0.1.after.mine), channel_id=1, source_target_pairs={{0,1},{1,0},{2,3},{3,2},{4,5},{5,4},{6,7},{7,6},{8,9},{9,8},{10,11... | collective-permute-start | bytes 989192 | tf_op jit(solution)/shard_map/ppermute | solution.py:410
  74.7 7.1 %load_0.1.blocks = bf16[640,128,128]{2,1,0:T(8,128)(2,1)S(1)} custom-call(bf16[640,128,128]{2,1,0:T(8,128)(2,1)} %blocks.5, bf16[161,8,128]{2,1,0:T(8,128)(2,1)S(1)} %forward_0.1.after.mine), custom_call_target="tpu_custom_call" | custom-call | bytes 41943040 | tf_op jit(solution)/shard_map/load_0/pallas_call | solution.py:319
  82.8 4.8 %backward_0.1 = (f32[160,8,128]{2,1,0:T(8,128)S(1)}, f32[8,128]{1,0:T(8,128)S(1)}, f32[1088,8,128]{2,1,0:T(8,128)S(1)}, bf16[32,17,8,128]{3,2,1,0:T(8,128)(2,1)S(1)}) custom-call(s32[1]{0:T(128)} %bitcast.here, s32[640]{0:T(1024)S(1)} %copy-done.2, s32[640]{0:T(1024)S(1)} %place.1.spot, bf16[161,8,128]{2,1,0:T(8,128)(2,1)S(1)} %forward_0.1.after.mine, ...), custom_call_target="tpu_custom_call" | custom-call | tf_op jit(solution)/shard_map/backward_0/pallas_call | solution.py:319
  91.4 21.1 %all_to_all.38.chunks = bf16[32,17,8,128]{3,2,1,0:T(8,128)(2,1)S(1)} all-to-all(bf16[32,17,8,128]{3,2,1,0:T(8,128)(2,1)S(1)} %add_cores.4), channel_id=1, replica_groups={{0,4,8,12,16,20,24,28,32,36,40,44,48,52,56,60,64,68,72,76,80,84,88,92,9..., dimensions={0} | all-to-all | bytes 2228224 | tf_op jit(solution)/shard_map/all_to_all | solution.py:346
  113.5 21.5 %all_to_all.39 = bf16[32,17,8,128]{3,2,1,0:T(8,128)(2,1)S(1)} all-to-all(bf16[32,17,8,128]{3,2,1,0:T(8,128)(2,1)S(1)} %get-tuple-element.49), channel_id=1, replica_groups={{0,4,8,12,16,20,24,28,32,36,40,44,48,52,56,60,64,68,72,76,80,84,88,92,9..., dimensions={0} | all-to-all | bytes 2228224 | tf_op jit(solution)/shard_map/all_to_all | solution.py:346
  135.0 2.5 %collective-permute-start.4 = (bf16[32,17,8,128]{3,2,1,0:T(8,128)(2,1)S(1)}, bf16[32,17,8,128]{3,2,1,0:T(8,128)(2,1)S(1)}, u32[]{:S(2)}, u32[]{:S(2)}) collective-permute-start(bf16[32,17,8,128]{3,2,1,0:T(8,128)(2,1)S(1)} %all_to_all.39), channel_id=1, source_target_pairs={{0,2},{2,0},{4,6},{6,4},{8,10},{10,8},{12,14},{14,12},{16,18},{18,... | collective-permute-start | bytes 3342344 | tf_op jit(solution)/shard_map/ppermute | solution.py:349
  139.9 4.4 %forward_1.1.after.mine = bf16[161,8,128]{2,1,0:T(8,128)(2,1)S(1)} custom-call(s32[640]{0:T(1024)S(1)} %copy-done.2, s32[640]{0:T(1024)S(1)} %place.1.spot, bf16[544,8,128]{2,1,0:T(8,128)(2,1)S(1)} %bitcast.9, bf16[544,8,128]{2,1,0:T(8,128)(2,1)S(1)} %bitcast.12, bf16[640,128,128]{2,1,0:T(8,128)(2,1)S(1)} %get-tuple-element.41.stored), custom_call_target="tpu_custom_call" | custom-call | tf_op jit(solution)/shard_map/forward_1/pallas_call | solution.py:319
  144.3 2.7 %collective-permute-start.5 = (bf16[161,8,128]{2,1,0:T(8,128)(2,1)S(1)}, bf16[161,8,128]{2,1,0:T(8,128)(2,1)S(1)}, u32[]{:S(2)}, u32[]{:S(2)}) collective-permute-start(bf16[161,8,128]{2,1,0:T(8,128)(2,1)S(1)} %forward_1.1.after.mine), channel_id=1, source_target_pairs={{0,1},{1,0},{2,3},{3,2},{4,5},{5,4},{6,7},{7,6},{8,9},{9,8},{10,11... | collective-permute-start | bytes 989192 | tf_op jit(solution)/shard_map/ppermute | solution.py:410
  147.0 7.1 %load_1.1.blocks = bf16[640,128,128]{2,1,0:T(8,128)(2,1)S(1)} custom-call(bf16[640,128,128]{2,1,0:T(8,128)(2,1)} %blocks.5, bf16[161,8,128]{2,1,0:T(8,128)(2,1)S(1)} %forward_1.1.after.mine), custom_call_target="tpu_custom_call" | custom-call | bytes 41943040 | tf_op jit(solution)/shard_map/load_1/pallas_call | solution.py:319
  155.1 4.8 %backward_1.1 = (f32[160,8,128]{2,1,0:T(8,128)S(1)}, f32[8,128]{1,0:T(8,128)S(1)}, f32[1088,8,128]{2,1,0:T(8,128)S(1)}, bf16[32,17,8,128]{3,2,1,0:T(8,128)(2,1)S(1)}) custom-call(s32[1]{0:T(128)} %bitcast.here, s32[640]{0:T(1024)S(1)} %copy-done.2, s32[640]{0:T(1024)S(1)} %place.1.spot, bf16[161,8,128]{2,1,0:T(8,128)(2,1)S(1)} %forward_1.1.after.mine, ...), custom_call_target="tpu_custom_call" | custom-call | tf_op jit(solution)/shard_map/backward_1/pallas_call | solution.py:319
  163.7 21.1 %all_to_all.40.chunks = bf16[32,17,8,128]{3,2,1,0:T(8,128)(2,1)S(1)} all-to-all(bf16[32,17,8,128]{3,2,1,0:T(8,128)(2,1)S(1)} %add_cores.5), channel_id=1, replica_groups={{0,4,8,12,16,20,24,28,32,36,40,44,48,52,56,60,64,68,72,76,80,84,88,92,9..., dimensions={0} | all-to-all | bytes 2228224 | tf_op jit(solution)/shard_map/all_to_all | solution.py:346
  185.8 21.5 %all_to_all.41 = bf16[32,17,8,128]{3,2,1,0:T(8,128)(2,1)S(1)} all-to-all(bf16[32,17,8,128]{3,2,1,0:T(8,128)(2,1)S(1)} %get-tuple-element.60), channel_id=1, replica_groups={{0,4,8,12,16,20,24,28,32,36,40,44,48,52,56,60,64,68,72,76,80,84,88,92,9..., dimensions={0} | all-to-all | bytes 2228224 | tf_op jit(solution)/shard_map/all_to_all | solution.py:346
  207.3 2.5 %collective-permute-start.7 = (bf16[32,17,8,128]{3,2,1,0:T(8,128)(2,1)S(1)}, bf16[32,17,8,128]{3,2,1,0:T(8,128)(2,1)S(1)}, u32[]{:S(2)}, u32[]{:S(2)}) collective-permute-start(bf16[32,17,8,128]{3,2,1,0:T(8,128)(2,1)S(1)} %all_to_all.41), channel_id=1, source_target_pairs={{0,2},{2,0},{4,6},{6,4},{8,10},{10,8},{12,14},{14,12},{16,18},{18,... | collective-permute-start | bytes 3342344 | tf_op jit(solution)/shard_map/ppermute | solution.py:349
  209.8 2.4 collective-permute-done.7
  212.2 4.4 %forward_2.1.after.mine = bf16[161,8,128]{2,1,0:T(8,128)(2,1)S(1)} custom-call(s32[640]{0:T(1024)S(1)} %copy-done.2, s32[640]{0:T(1024)S(1)} %place.1.spot, bf16[544,8,128]{2,1,0:T(8,128)(2,1)S(1)} %bitcast.8, bf16[544,8,128]{2,1,0:T(8,128)(2,1)S(1)} %bitcast.11, bf16[640,128,128]{2,1,0:T(8,128)(2,1)S(1)} %get-tuple-element.41.stored), custom_call_target="tpu_custom_call" | custom-call | tf_op jit(solution)/shard_map/forward_2/pallas_call | solution.py:319
  216.6 2.5 %collective-permute-start.8 = (bf16[161,8,128]{2,1,0:T(8,128)(2,1)S(1)}, bf16[161,8,128]{2,1,0:T(8,128)(2,1)S(1)}, u32[]{:S(2)}, u32[]{:S(2)}) collective-permute-start(bf16[161,8,128]{2,1,0:T(8,128)(2,1)S(1)} %forward_2.1.after.mine), channel_id=1, source_target_pairs={{0,1},{1,0},{2,3},{3,2},{4,5},{5,4},{6,7},{7,6},{8,9},{9,8},{10,11... | collective-permute-start | bytes 989192 | tf_op jit(solution)/shard_map/ppermute | solution.py:410
  220.1 7.1 %collective-permute-done.8.other = bf16[161,8,128]{2,1,0:T(8,128)(2,1)S(1)} collective-permute-done((bf16[161,8,128]{2,1,0:T(8,128)(2,1)S(1)}, bf16[161,8,128]{2,1,0:T(8,128)(2,1)S(1)}, u32[]{:S(2)}, u32[]{:S(2)}) %collective-permute-start.8) | collective-permute-done | bytes 329760 | tf_op jit(solution)/shard_map/ppermute | solution.py:410
  227.7 12.8 %all_to_all.42.norms = f32[64,1,128]{2,1,0:T(1,128)S(1)} all-to-all(f32[64,1,128]{2,1,0:T(1,128)S(1)} %get-tuple-element.67), channel_id=1, replica_groups=mesh['rows'=64,'cols'=2] {'rows'}, dimensions={0} | all-to-all | bytes 65536 | tf_op jit(solution)/shard_map/all_to_all | solution.py:446
  (27 shorter events, 21.6 us)
Async XLA Ops:
  9.4 3.9 %collective-permute-start = (bf16[32,17,8,128]{3,2,1,0:T(8,128)(2,1)S(1)}, bf16[32,17,8,128]{3,2,1,0:T(8,128)(2,1)S(1)}, u32[]{:S(2)}, u32[]{:S(2)}) collective-permute-start(bf16[32,17,8,128]{3,2,1,0:T(8,128)(2,1)S(1)} %get-tuple-element.39), channel_id=1, source_target_pairs={{0,2},{2,0},{4,6},{6,4},{8,10},{10,8},{12,14},{14,12},{16,18},{18,... | collective-permute-start | bytes 3342344 | tf_op jit(solution)/shard_map/ppermute | solution.py:349
  13.5 26.7 %copy-start.1 = (f32[16,128,128]{2,1,0:T(8,128)S(1)}, f32[16,128,128]{2,1,0:T(8,128)}, u32[]{:S(2)}) copy-start(f32[16,128,128]{2,1,0:T(8,128)} %refs_0_.1) | copy-start | bytes 3145732
  41.2 24.0 %copy-start.3 = (s32[640]{0:T(1024)S(1)}, s32[640]{0:T(1024)}, u32[]{:S(2)}) copy-start(s32[640]{0:T(1024)} %column_in.1) | copy-start | bytes 7684
  41.2 26.4 %copy-start.2 = (s32[640]{0:T(1024)S(1)}, s32[640]{0:T(1024)}, u32[]{:S(2)}) copy-start(s32[640]{0:T(1024)} %row.9) | copy-start | bytes 7684
  62.7 4.9 %collective-permute-start.1 = (bf16[32,17,8,128]{3,2,1,0:T(8,128)(2,1)S(1)}, bf16[32,17,8,128]{3,2,1,0:T(8,128)(2,1)S(1)}, u32[]{:S(2)}, u32[]{:S(2)}) collective-permute-start(bf16[32,17,8,128]{3,2,1,0:T(8,128)(2,1)S(1)} %all_to_all.37), channel_id=1, source_target_pairs={{0,2},{2,0},{4,6},{6,4},{8,10},{10,8},{12,14},{14,12},{16,18},{18,... | collective-permute-start | bytes 3342344 | tf_op jit(solution)/shard_map/ppermute | solution.py:349
  72.0 10.7 %copy-start = (f32[160,8,128]{2,1,0:T(8,128)S(1)}, f32[160,8,128]{2,1,0:T(8,128)}, u32[]{:S(2)}) copy-start(f32[160,8,128]{2,1,0:T(8,128)} %before.1) | copy-start | bytes 1966084
  72.0 10.7 %collective-permute-start.2 = (bf16[161,8,128]{2,1,0:T(8,128)(2,1)S(1)}, bf16[161,8,128]{2,1,0:T(8,128)(2,1)S(1)}, u32[]{:S(2)}, u32[]{:S(2)}) collective-permute-start(bf16[161,8,128]{2,1,0:T(8,128)(2,1)S(1)} %forward_0.1.after.mine), channel_id=1, source_target_pairs={{0,1},{1,0},{2,3},{3,2},{4,5},{5,4},{6,7},{7,6},{8,9},{9,8},{10,11... | collective-permute-start | bytes 989192 | tf_op jit(solution)/shard_map/ppermute | solution.py:410
  87.6 3.7 %collective-permute-start.3 = (bf16[32,17,8,128]{3,2,1,0:T(8,128)(2,1)S(1)}, bf16[32,17,8,128]{3,2,1,0:T(8,128)(2,1)S(1)}, u32[]{:S(2)}, u32[]{:S(2)}) collective-permute-start(bf16[32,17,8,128]{3,2,1,0:T(8,128)(2,1)S(1)} %get-tuple-element.44), channel_id=1, source_target_pairs={{0,2},{2,0},{4,6},{6,4},{8,10},{10,8},{12,14},{14,12},{16,18},{18,... | collective-permute-start | bytes 3342344 | tf_op jit(solution)/shard_map/ppermute | solution.py:349
  135.0 4.9 %collective-permute-start.4 = (bf16[32,17,8,128]{3,2,1,0:T(8,128)(2,1)S(1)}, bf16[32,17,8,128]{3,2,1,0:T(8,128)(2,1)S(1)}, u32[]{:S(2)}, u32[]{:S(2)}) collective-permute-start(bf16[32,17,8,128]{3,2,1,0:T(8,128)(2,1)S(1)} %all_to_all.39), channel_id=1, source_target_pairs={{0,2},{2,0},{4,6},{6,4},{8,10},{10,8},{12,14},{14,12},{16,18},{18,... | collective-permute-start | bytes 3342344 | tf_op jit(solution)/shard_map/ppermute | solution.py:349
  144.3 10.8 %collective-permute-start.5 = (bf16[161,8,128]{2,1,0:T(8,128)(2,1)S(1)}, bf16[161,8,128]{2,1,0:T(8,128)(2,1)S(1)}, u32[]{:S(2)}, u32[]{:S(2)}) collective-permute-start(bf16[161,8,128]{2,1,0:T(8,128)(2,1)S(1)} %forward_1.1.after.mine), channel_id=1, source_target_pairs={{0,1},{1,0},{2,3},{3,2},{4,5},{5,4},{6,7},{7,6},{8,9},{9,8},{10,11... | collective-permute-start | bytes 989192 | tf_op jit(solution)/shard_map/ppermute | solution.py:410
  159.9 3.7 %collective-permute-start.6 = (bf16[32,17,8,128]{3,2,1,0:T(8,128)(2,1)S(1)}, bf16[32,17,8,128]{3,2,1,0:T(8,128)(2,1)S(1)}, u32[]{:S(2)}, u32[]{:S(2)}) collective-permute-start(bf16[32,17,8,128]{3,2,1,0:T(8,128)(2,1)S(1)} %get-tuple-element.53), channel_id=1, source_target_pairs={{0,2},{2,0},{4,6},{6,4},{8,10},{10,8},{12,14},{14,12},{16,18},{18,... | collective-permute-start | bytes 3342344 | tf_op jit(solution)/shard_map/ppermute | solution.py:349
  207.3 4.9 %collective-permute-start.7 = (bf16[32,17,8,128]{3,2,1,0:T(8,128)(2,1)S(1)}, bf16[32,17,8,128]{3,2,1,0:T(8,128)(2,1)S(1)}, u32[]{:S(2)}, u32[]{:S(2)}) collective-permute-start(bf16[32,17,8,128]{3,2,1,0:T(8,128)(2,1)S(1)} %all_to_all.41), channel_id=1, source_target_pairs={{0,2},{2,0},{4,6},{6,4},{8,10},{10,8},{12,14},{14,12},{16,18},{18,... | collective-permute-start | bytes 3342344 | tf_op jit(solution)/shard_map/ppermute | solution.py:349
  216.6 10.6 %collective-permute-start.8 = (bf16[161,8,128]{2,1,0:T(8,128)(2,1)S(1)}, bf16[161,8,128]{2,1,0:T(8,128)(2,1)S(1)}, u32[]{:S(2)}, u32[]{:S(2)}) collective-permute-start(bf16[161,8,128]{2,1,0:T(8,128)(2,1)S(1)} %forward_2.1.after.mine), channel_id=1, source_target_pairs={{0,1},{1,0},{2,3},{3,2},{4,5},{5,4},{6,7},{7,6},{8,9},{9,8},{10,11... | collective-permute-start | bytes 989192 | tf_op jit(solution)/shard_map/ppermute | solution.py:410
